TPU v7x, 128 devices: a whole 4x4x4 slice. The times are simulated.
128 devices in a mesh: page: 32 (over y, x, core), tp: 4 (over z).
Axes of the slice: x: 4, y: 4, z: 4, core: 2. Of those that a mesh axis runs over, the one named last changes fastest.
Arguments:
- x3: bfloat16 [800, 32, 4, 512], P('page', None, None, 'tp'), may hold values from -150 to 150
- res_group: int32 [32], P('page'), may hold values from 0 to 3, as said below
- merge_gain: float32 [4, 512], P(None, 'tp'), may hold values from 0.5 to 1.5
- merge_bias: float32 [4, 512], P(None, 'tp'), may hold values from -1.5 to 1.5
- merge_w: bfloat16 [4, 512, 1024], P(None, 'tp'), may hold values from -0.125 to 0.125
- ln1_gain: float32 [2, 1024], replicated, may hold values from 0.5 to 1.5
- ln1_bias: float32 [2, 1024], replicated, may hold values from -1.5 to 1.5
- qkv_w: bfloat16 [2, 1024, 3, 1024], P(None, None, None, 'tp'), may hold values from -0.1875 to 0.1875
- qv_bias: float32 [2, 2, 1024], P(None, None, 'tp'), may hold values from -2.5 to 2.5
- rel_table: float32 [2, 32, 361], P(None, 'tp'), may hold values from -4 to 4
- proj_w: bfloat16 [2, 1024, 1024], P(None, 'tp'), may hold values from -1 to 1
- proj_bias: float32 [2, 1024], replicated, may hold values from -1.5 to 1.5
- ln2_gain: float32 [2, 1024], replicated, may hold values from 0.5 to 1.5
- ln2_bias: float32 [2, 1024], replicated, may hold values from -1.5 to 1.5
- fc1_w: bfloat16 [2, 1024, 4096], P(None, None, 'tp'), may hold values from -0.1875 to 0.1875
- fc1_bias: float32 [2, 4096], P(None, 'tp'), may hold values from -1.5 to 1.5
- fc2_w: bfloat16 [2, 4096, 1024], P(None, 'tp'), may hold values from -0.125 to 0.125
- fc2_bias: float32 [2, 1024], replicated, may hold values from -1.5 to 1.5
- out_grad: bfloat16 [32, 20, 40, 1024], P('page'), may hold values from -6 to 6
Outputs:
- output: float32 [32, 20, 40, 1024], P('page')
- grad_x3: float32 [800, 32, 4, 512], P('page', None, None, 'tp')
- g_merge_gain: float32 [4, 512], P(None, 'tp')
- g_merge_bias: float32 [4, 512], P(None, 'tp')
- g_merge_w: float32 [4, 512, 1024], P(None, 'tp', 'page')
- g_ln1_gain: float32 [2, 1024], P(None, 'page')
- g_ln1_bias: float32 [2, 1024], P(None, 'page')
- g_qkv_w: float32 [2, 1024, 3, 1024], P(None, 'page', None, 'tp')
- g_qv_bias: float32 [2, 2, 1024], P(None, None, 'tp')
- g_rel_table: float32 [2, 32, 361], P(None, 'tp')
- g_proj_w: float32 [2, 1024, 1024], P(None, 'tp', 'page')
- g_proj_bias: float32 [2, 1024], P(None, 'page')
- g_ln2_gain: float32 [2, 1024], P(None, 'page')
- g_ln2_bias: float32 [2, 1024], P(None, 'page')
- g_fc1_w: float32 [2, 1024, 4096], P(None, 'page', 'tp')
- g_fc1_bias: float32 [2, 4096], P(None, 'tp')
- g_fc2_w: float32 [2, 4096, 1024], P(None, 'tp', 'page')
- g_fc2_bias: float32 [2, 1024], P(None, 'page')
Inputs may be any that keep to these rules, and one draw needn't show every extreme that they name: Page p has 10 * (res_group[p] + 1) columns of real tokens, the rest of its 40 columns is padding; in every draw some page has all 4 window columns.
All inputs are finite; a program needn't handle non-finite values.
Results may differ from a plain program's by a relative error of at most 0.03.
Values may be sent and summed in bfloat16 or wider, within the bound.
No kernel may reach another device: no remote copies, remote signals or barrier semaphores. Data moves between devices by JAX's collectives and lax.ppermute only.
A program may use at most 256 MiB of HBM per device.

v0:
```python
from functools import partial

import jax
import jax.numpy as jnp
import numpy as np
from jax import lax
from jax.experimental import pallas as pl
from jax.experimental.pallas import tpu as pltpu
from jax.sharding import Mesh
from jax.sharding import PartitionSpec as P

D = 1024
FF = 4096
MERGED = 2048
WIN = 10
SHIFT = 5
GH = 20
GW = 40
RELS = 361
TOK = 100
ROWS = 112
T = 2 * ROWS
SEND = 112
EPS = 1e-05
SCALE = 32 ** (-0.5)
YX = 16
TP = 4
UNITS = 18
HIGH = lax.Precision.HIGHEST
BF = jnp.bfloat16
F32 = jnp.float32
PAGE_AXES = ("y", "x", "core")
CHIP_AXES = ("y", "x")
GATHER_AXES = ("tp", "y", "x", "core")
VMEM = 58 << 20


def row_at(row, col):
    return (row // WIN) * ROWS + (row % WIN) * WIN + col


def place_matrices():
    own = np.zeros((T, T), np.float32)
    recv = np.zeros((T, SEND), np.float32)
    send = np.zeros((SEND, T), np.float32)
    pack = np.zeros((2 * TOK, T), np.float32)
    out = np.zeros((2 * TOK, T), np.float32)
    for row in range(GH):
        for col in range(WIN):
            source = (row + SHIFT) % GH
            if col < SHIFT:
                own[row_at(row, col), row_at(source, col + SHIFT)] = 1
                send[row * SHIFT + col, row_at(row, col)] = 1
            else:
                recv[row_at(row, col), source * SHIFT + col - SHIFT] = 1
            pack[row * WIN + col, row_at(row, col)] = 1
            out[source * WIN + col, row_at(row, col)] = 1
    return own, recv, send, pack, out


OWN, RECV, SENT, PACK, OUT = place_matrices()


def const(matrix):
    return jnp.asarray(matrix, BF)


def dot(left, right):
    return lax.dot_general(left, right, (((1,), (0,)), ((), ())), preferred_element_type=F32)


def dot_nt(left, right):
    return lax.dot_general(left, right, (((1,), (1,)), ((), ())), preferred_element_type=F32)


def dot_tn(left, right):
    return lax.dot_general(left, right, (((0,), (0,)), ((), ())), preferred_element_type=F32)


def select_rows(matrix, value):
    high = value.astype(BF)
    rest = value - high.astype(F32)
    mid = rest.astype(BF)
    low = (rest - mid.astype(F32)).astype(BF)
    return dot(matrix, high) + dot(matrix, mid) + dot(matrix, low)


def norm_stats(value):
    mean = jnp.mean(value, axis=-1, keepdims=True)
    center = value - mean
    return center, lax.rsqrt(jnp.mean(center * center, axis=-1, keepdims=True) + EPS)


def norm_back(upstream, normed, spread, gain):
    scaled = upstream * gain
    inner = (
        scaled
        - jnp.mean(scaled, axis=-1, keepdims=True)
        - normed * jnp.mean(scaled * normed, axis=-1, keepdims=True)
    )
    return spread * inner


def col_sum(value):
    return jnp.sum(value, axis=0, keepdims=True)


def whole(shape):
    return pl.BlockSpec(shape, lambda step, core: (0,) * len(shape))


def shape_of(shape, dtype):
    return jax.ShapeDtypeStruct(shape, dtype)


def run(kernel, steps, core, args, in_specs, outs, out_specs, scratch, flops, moved):
    return pl.pallas_call(
        kernel,
        grid_spec=pltpu.PrefetchScalarGridSpec(
            num_scalar_prefetch=1,
            grid=(steps,),
            in_specs=in_specs,
            out_specs=out_specs,
            scratch_shapes=scratch,
        ),
        out_shape=outs,
        compiler_params=pltpu.CompilerParams(
            vmem_limit_bytes=VMEM, dimension_semantics=("arbitrary",)
        ),
        cost_estimate=pl.CostEstimate(flops=0, bytes_accessed=1024, transcendentals=0),
    )(core, *args)


def put_halves(core_ref, mine, other, low, high):
    @pl.when(core_ref[0] == 0)
    def _():
        mine(low)
        other(high)

    @pl.when(core_ref[0] != 0)
    def _():
        mine(high)
        other(low)


def pack_kernel(
    place_ref, up_ref, down_ref, mix_ref, proj_ref, merge_ref, out_ref, late_ref, all_ref
):
    low = place_ref[1] == 0
    late_ref[...] = jnp.where(low, up_ref[1], down_ref[1]).reshape(4, 16, D)
    all_ref[0:4] = up_ref[0].reshape(4, 16, D)
    all_ref[4:8] = down_ref[0].reshape(4, 16, D)
    for level in range(2):
        for part in range(3):
            for group in range(4):
                all_ref[8 + 4 * level + part, :, 256 * group : 256 * group + 256] = mix_ref[
                    level, part, 16 * group : 16 * group + 16
                ]
        all_ref[11 + 4 * level] = proj_ref[level]
    all_ref[16:18] = merge_ref[...].reshape(2, 16, D)
    out_ref[...] = all_ref[pl.ds(place_ref[1] * 9, 9)]


def pack_weights(place, up, down, mix, proj, merge):
    return pl.pallas_call(
        pack_kernel,
        grid_spec=pltpu.PrefetchScalarGridSpec(
            num_scalar_prefetch=1,
            grid=(1,),
            in_specs=[
                pl.BlockSpec((2, 64, D), lambda step, place: (0, place[0], 0)),
                pl.BlockSpec((2, 64, D), lambda step, place: (0, place[0], 0)),
                pl.BlockSpec((2, 3, 64, 256), lambda step, place: (0, 0, place[0], 0)),
                pl.BlockSpec((2, 16, D), lambda step, place: (0, place[0], 0)),
                pl.BlockSpec((32, D), lambda step, place: (place[0], 0)),
            ],
            out_specs=[whole((9, 16, D)), whole((4, 16, D))],
            scratch_shapes=[pltpu.VMEM((UNITS, 16, D), BF)],
        ),
        out_shape=[shape_of((9, 16, D), BF), shape_of((4, 16, D), BF)],
        compiler_params=pltpu.CompilerParams(vmem_limit_bytes=VMEM),
        cost_estimate=pl.CostEstimate(flops=0, bytes_accessed=1 << 20, transcendentals=0),
    )(place, up, down, mix, proj, merge)


def merge_stats(x_ref, pack_ref, full):
    total = jnp.zeros((T, 1), F32)
    for part in range(TP):
        rows = dot_tn(pack_ref[...], x_ref[part])
        full[part] = rows
        total = total + jnp.sum(rows, axis=-1, keepdims=True)
    mean = total / MERGED
    square = jnp.zeros((T, 1), F32)
    for part in range(TP):
        center = full[part] - mean
        square = square + jnp.sum(center * center, axis=-1, keepdims=True)
    return mean, lax.rsqrt(square / MERGED + EPS)


def merge_kernel(
    core_ref, x_ref, pack_ref, gain_ref, bias_ref, w_ref, out_ref, mine_ref, other_ref, full, stats
):
    step = pl.program_id(0)

    @pl.when(step == 0)
    def _():
        mean, spread = merge_stats(x_ref, pack_ref, full)
        stats[0] = mean
        stats[1] = spread

    normed = (full[step] - stats[0]) * stats[1]
    value = (normed * gain_ref[0] + bias_ref[0]).astype(BF)

    def set_mine(part):
        mine_ref[...] = part

    def set_other(part):
        other_ref[...] = part

    put_halves(core_ref, set_mine, set_other, value[:, :256], value[:, 256:])
    term = dot(value, w_ref[...].reshape(512, D))

    @pl.when(step == 0)
    def _():
        out_ref[...] = term

    @pl.when(step != 0)
    def _():
        out_ref[...] += term


def merge_forward(core, parts, gain, bias, weights):
    return run(
        merge_kernel,
        TP,
        core,
        (parts, const(PACK), gain.reshape(TP, 1, 512), bias.reshape(TP, 1, 512), weights),
        [
            whole((TP, 2 * TOK, 512)),
            whole((2 * TOK, T)),
            pl.BlockSpec((1, 1, 512), lambda step, core: (step, 0, 0)),
            pl.BlockSpec((1, 1, 512), lambda step, core: (step, 0, 0)),
            pl.BlockSpec((YX, 2, 16, D), lambda step, core: (step, 8, 0, 0)),
        ],
        [shape_of((T, D), F32), shape_of((T, D), BF), shape_of((T, D), BF)],
        [
            whole((T, D)),
            pl.BlockSpec((T, 256), lambda step, core: (0, step)),
            pl.BlockSpec((T, 256), lambda step, core: (0, step)),
        ],
        [pltpu.VMEM((TP, T, 512), F32), pltpu.VMEM((2, T, 1), F32)],
        2 * T * MERGED * D,
        8 << 20,
    )


def merge_back_kernel(
    core_ref, x_ref, pack_ref, gain_ref, w_ref, dx_ref,
    start_ref, dm_ref, gains_ref, biases_ref,
    full, stats, upstream,
):
    step = pl.program_id(0)

    @pl.when(step == 0)
    def _():
        mean, spread = merge_stats(x_ref, pack_ref, full)
        stats[0] = mean
        stats[1] = spread
        stats[2] = jnp.zeros((T, 1), F32)
        stats[3] = jnp.zeros((T, 1), F32)
        start_ref[...] = dx_ref[...].astype(BF)

    grad = dot_nt(start_ref[...], w_ref[...].reshape(512, D))
    normed = (full[step] - stats[0]) * stats[1]
    full[step] = normed
    gains_ref[0] = col_sum(grad * normed)
    biases_ref[0] = col_sum(grad)
    scaled = grad * gain_ref[0]
    upstream[step] = scaled
    stats[2] += jnp.sum(scaled, axis=-1, keepdims=True)
    stats[3] += jnp.sum(scaled * normed, axis=-1, keepdims=True)

    @pl.when(step == TP - 1)
    def _():
        for part in range(TP):
            value = stats[1] * (
                upstream[part] - stats[2] / MERGED - full[part] * (stats[3] / MERGED)
            )
            dm_ref[part] = dot(pack_ref[...], value.astype(BF)).astype(BF)


def merge_backward(core, parts, gain, weights, grad):
    return run(
        merge_back_kernel,
        TP,
        core,
        (parts, const(PACK), gain.reshape(TP, 1, 512), weights, grad),
        [
            whole((TP, 2 * TOK, 512)),
            whole((2 * TOK, T)),
            pl.BlockSpec((1, 1, 512), lambda step, core: (step, 0, 0)),
            pl.BlockSpec((YX, 2, 16, D), lambda step, core: (step, 8, 0, 0)),
            whole((T, D)),
        ],
        [
            shape_of((T, D), BF),
            shape_of((TP, 2 * TOK, 512), BF),
            shape_of((TP, 1, 512), F32),
            shape_of((TP, 1, 512), F32),
        ],
        [
            whole((T, D)),
            whole((TP, 2 * TOK, 512)),
            pl.BlockSpec((1, 1, 512), lambda step, core: (step, 0, 0)),
            pl.BlockSpec((1, 1, 512), lambda step, core: (step, 0, 0)),
        ],
        [pltpu.VMEM((TP, T, 512), F32), pltpu.VMEM((4, T, 1), F32), pltpu.VMEM((TP, T, 512), F32)],
        2 * T * MERGED * D,
        8 << 20,
    )


def head_masks(rows):
    lane = lax.broadcasted_iota(jnp.int32, (rows, 128), 1)
    return [(lane >= 32 * place) & (lane < 32 * place + 32) for place in range(4)]


def spread_heads(value, masks):
    zero = jnp.zeros_like(value)
    return jnp.concatenate([jnp.where(mask, value, zero) for mask in masks], axis=0)


def fold_heads(value, masks):
    total = jnp.zeros((ROWS, 128), F32)
    for place, mask in enumerate(masks):
        total = jnp.where(mask, value[place * ROWS : (place + 1) * ROWS], total)
    return total


def unfold(ref):
    value = ref[...].reshape(YX, 16, D)
    parts = [value[:, :, 256 * group : 256 * group + 256] for group in range(4)]
    return jnp.stack(parts, axis=1).reshape(D, 256)


def attn_kernel(level, *refs):
    (core_ref, x_ref), refs = refs[:2], refs[2:]
    if level:
        (halo_ref, own_ref, recv_ref), refs = refs[:3], refs[3:]
    (
        gain_ref, bias_ref, wq_ref, wk_ref, wv_ref, wp_ref, qb_ref, vb_ref, table_ref, mask_ref,
        shift_ref,
    ), refs = refs[:11], refs[11:]
    (
        mid_ref, a_ref, q_ref, k_ref, v_ref, probs_ref, mine_ref, other_ref,
    ), refs = refs[:8], refs[8:]
    step = pl.program_id(0)

    @pl.when(step == 0)
    def _():
        value = x_ref[...]
        if level:
            value = select_rows(own_ref[...], value) + dot(recv_ref[...], halo_ref[...])
            refs[0][...] = value
        center, spread = norm_stats(value)
        a_ref[...] = (center * spread * gain_ref[...] + bias_ref[...]).astype(BF)
        mid_ref[...] = value + shift_ref[...]

    a = a_ref[...]
    q = (dot(a, unfold(wq_ref)) + qb_ref[...]).astype(BF)
    k = dot(a, unfold(wk_ref)).astype(BF)
    v = (dot(a, unfold(wv_ref)) + vb_ref[...]).astype(BF)
    q_ref[...] = q
    k_ref[...] = k
    v_ref[...] = v
    masks = head_masks(ROWS)
    halves = []
    for half in range(2):
        lanes = slice(half * 128, half * 128 + 128)
        table = table_ref[4 * half : 4 * half + 4]
        parts = []
        for w in range(2):
            rows = slice(w * ROWS, (w + 1) * ROWS)
            raw = dot_nt(spread_heads(q[rows, lanes], masks), k[rows, lanes]) * SCALE
            scores = raw.reshape(4, ROWS, ROWS) + table + mask_ref[w][None]
            top = jnp.max(scores, axis=-1, keepdims=True)
            terms = jnp.exp(scores - top)
            probs = (terms / jnp.sum(terms, axis=-1, keepdims=True)).astype(BF)
            probs_ref[0, w, 4 * half : 4 * half + 4] = probs
            mixed = dot(probs.reshape(4 * ROWS, ROWS), v[rows, lanes])
            parts.append(fold_heads(mixed, masks))
        halves.append(jnp.concatenate(parts, axis=0).astype(BF))

    def set_mine(part):
        mine_ref[...] = part

    def set_other(part):
        other_ref[...] = part

    put_halves(core_ref, set_mine, set_other, *halves)
    heads = jnp.concatenate(halves, axis=1)
    mid_ref[...] += dot(heads, wp_ref[...].reshape(256, D))


def unit_spec(unit):
    return pl.BlockSpec((YX, 1, 16, D), lambda step, core: (step, unit, 0, 0))


def attn_forward(core, level, state, halo, weights, small, table, mask):
    gain, bias, qbias, vbias, shift = small
    unit = 8 + 4 * level
    args = [state]
    specs = [whole((T, D))]
    if level:
        args += [halo, const(OWN), const(RECV)]
        specs += [whole((SEND, D)), whole((T, T)), whole((T, SEND))]
    args += [gain, bias, weights, weights, weights, weights, qbias, vbias, table, mask, shift]
    cols = pl.BlockSpec((1, 256), lambda step, core: (0, step))
    specs += [whole((1, D)), whole((1, D))] + [unit_spec(unit + place) for place in range(4)]
    specs += [
        cols,
        cols,
        pl.BlockSpec((8, ROWS, ROWS), lambda step, core: (step, 0, 0)),
        whole((2, ROWS, ROWS)),
        whole((1, D)),
    ]
    block = pl.BlockSpec((T, 256), lambda step, core: (0, step))
    half = pl.BlockSpec((T, 128), lambda step, core: (0, step))
    outs = [
        shape_of((T, D), F32),
        shape_of((T, D), BF),
        shape_of((T, D), BF),
        shape_of((T, D), BF),
        shape_of((T, D), BF),
        shape_of((TP, 2, 8, ROWS, ROWS), BF),
        shape_of((T, D // 2), BF),
        shape_of((T, D // 2), BF),
    ]
    out_specs = [
        whole((T, D)),
        whole((T, D)),
        block,
        block,
        block,
        pl.BlockSpec((1, 2, 8, ROWS, ROWS), lambda step, core: (step, 0, 0, 0, 0)),
        half,
        half,
    ]
    if level:
        outs.append(shape_of((T, D), F32))
        out_specs.append(whole((T, D)))
    return run(
        partial(attn_kernel, level), TP, core, args, specs, outs, out_specs, [], 8 * T * D * D, 24 << 20
    )


def quad_spec(unit):
    return pl.BlockSpec(
        (YX, 4, 16, D), lambda step, core: (lax.rem(core[1] + step, TP), unit, 0, 0)
    )


def wide_spec(rows):
    return pl.BlockSpec((rows, D), lambda step, core: (0, lax.rem(core[1] + step, TP)))


def half_spec():
    return pl.BlockSpec((T, 512), lambda step, core: (0, lax.rem(core[1] + step, TP)))


def gelu_parts(pre):
    phi = 0.5 + 0.5 * lax.erf(pre * (0.5**0.5))
    slope = phi + pre * ((2.0 * np.pi) ** -0.5 * jnp.exp(-0.5 * pre * pre))
    return (pre * phi).astype(BF), slope


def start_norm(mid_ref, gain_ref, bias_ref, shift_ref, c2_ref, total):
    value = mid_ref[...]
    center, spread = norm_stats(value)
    c2_ref[...] = (center * spread * gain_ref[...] + bias_ref[...]).astype(BF)
    total[...] = value + shift_ref[...]


def end_norm(mid_ref, gain_ref, grad, dmlp, upstream, dmid_ref, dattn_ref, rows_ref):
    center, spread = norm_stats(mid_ref[...])
    normed = center * spread
    dmid = grad + norm_back(upstream, normed, spread, gain_ref[...])
    dmid_ref[...] = dmid
    dattn = dmid.astype(BF)
    dattn_ref[...] = dattn
    rows_ref[0:1] = col_sum(upstream * normed)
    rows_ref[1:2] = col_sum(upstream)
    rows_ref[2:3] = col_sum(dmlp.astype(F32))
    rows_ref[3:4] = col_sum(dattn.astype(F32))


def put_parts(core_ref, mine_ref, other_ref, value):
    def set_mine(part):
        mine_ref[...] = part

    def set_other(part):
        other_ref[...] = part

    put_halves(core_ref, set_mine, set_other, value[:, :512], value[:, 512:])


def put_quarter(refs, value):
    for ahead, ref in enumerate(refs):

        @pl.when(pl.program_id(0) == ahead)
        def _(ref=ref):
            ref[...] = value


def mlp_kernel(
    core_ref, mid_ref, gain_ref, bias_ref, w1_ref, w2_ref, b1_ref, b2_ref, place_ref,
    c2_ref, slope_ref, halo_ref, mine_ref, other_ref, next_ref, total,
):
    step = pl.program_id(0)

    @pl.when(step == 0)
    def _():
        start_norm(mid_ref, gain_ref, bias_ref, b2_ref, c2_ref, total)

    act, slope = gelu_parts(dot(c2_ref[...], w1_ref[...].reshape(D, D)) + b1_ref[...])
    slope_ref[...] = slope.astype(BF)
    put_parts(core_ref, mine_ref, other_ref, act)
    total[...] += dot(act, w2_ref[...].reshape(D, D))

    @pl.when(step == TP - 1)
    def _():
        value = total[...]
        halo_ref[...] = dot(place_ref[...], value.astype(BF)).astype(BF)
        next_ref[...] = value


def mlp_forward(core, mid, weights, small):
    gain, bias, b1, b2 = small
    return run(
        mlp_kernel,
        TP,
        core,
        (mid, gain, bias, weights, weights, b1, b2, const(SENT)),
        [
            whole((T, D)),
            whole((1, D)),
            whole((1, D)),
            quad_spec(0),
            quad_spec(1),
            wide_spec(1),
            whole((1, D)),
            whole((SEND, T)),
        ],
        [
            shape_of((T, D), BF),
            shape_of((T, FF), BF),
            shape_of((SEND, D), BF),
            shape_of((T, FF // 2), BF),
            shape_of((T, FF // 2), BF),
            shape_of((T, D), F32),
        ],
        [whole((T, D)), wide_spec(T), whole((SEND, D)), half_spec(), half_spec(), whole((T, D))],
        [pltpu.VMEM((T, D), F32)],
        4 * T * D * FF,
        24 << 20,
    )


def mlp_both_kernel(
    core_ref, mid_ref, gain_ref, bias_ref, w1_ref, w2_ref, b1_ref, b2_ref, place_ref, keep_ref,
    dx_ref, c2_ref, out_ref, one, two, three, four, dmid_ref, dattn_ref, db1_ref, rows_ref,
    mine_ref, other_ref, total, back,
):
    step = pl.program_id(0)

    @pl.when(step == 0)
    def _():
        start_norm(mid_ref, gain_ref, bias_ref, b2_ref, c2_ref, total)
        back[...] = jnp.zeros((T, D), F32)

    up = w1_ref[...].reshape(D, D)
    down = w2_ref[...].reshape(D, D)
    act, slope = gelu_parts(dot(c2_ref[...], up) + b1_ref[...])
    put_quarter((one, two, three, four), act)
    total[...] += dot(act, down)
    dpre = (dot_nt(dx_ref[...], down) * slope).astype(BF)
    db1_ref[...] = col_sum(dpre.astype(F32))
    put_parts(core_ref, mine_ref, other_ref, dpre)
    back[...] += dot_nt(dpre, up)

    @pl.when(step == TP - 1)
    def _():
        out_ref[...] = dot(place_ref[...], (total[...] * keep_ref[...]).astype(BF)).astype(BF)
        dmlp = dx_ref[...]
        end_norm(
            mid_ref, gain_ref, dmlp.astype(F32), dmlp, back[...], dmid_ref, dattn_ref, rows_ref
        )


def mlp_both(core, mid, weights, small, keep, dx):
    gain, bias, b1, b2 = small
    return run(
        mlp_both_kernel,
        TP,
        core,
        (mid, gain, bias, weights, weights, b1, b2, const(OUT), keep, dx),
        [
            whole((T, D)),
            whole((1, D)),
            whole((1, D)),
            quad_spec(0),
            quad_spec(1),
            wide_spec(1),
            whole((1, D)),
            whole((2 * TOK, T)),
            whole((T, 1)),
            whole((T, D)),
        ],
        [shape_of((T, D), BF), shape_of((2 * TOK, D), BF)]
        + [shape_of((T, D), BF)] * TP
        + [
            shape_of((T, D), F32),
            shape_of((T, D), BF),
            shape_of((1, FF), F32),
            shape_of((4, D), F32),
            shape_of((T, FF // 2), BF),
            shape_of((T, FF // 2), BF),
        ],
        [whole((T, D)), whole((2 * TOK, D))]
        + [whole((T, D))] * TP
        + [whole((T, D)), whole((T, D)), wide_spec(1), whole((4, D)), half_spec(), half_spec()],
        [pltpu.VMEM((T, D), F32), pltpu.VMEM((T, D), F32)],
        8 * T * D * FF,
        24 << 20,
    )


def mlp_back_kernel(
    core_ref, dx_ref, halo_ref, own_ref, sent_ref, mid_ref, gain_ref, w1_ref, w2_ref, slope_ref,
    dmid_ref, dmlp_ref, dattn_ref, db1_ref, rows_ref, one, two, three, four, total, grad,
):
    step = pl.program_id(0)

    @pl.when(step == 0)
    def _():
        value = select_rows_t(own_ref[...], dx_ref[...]) + dot_tn(sent_ref[...], halo_ref[...])
        grad[...] = value
        dmlp_ref[...] = value.astype(BF)
        total[...] = jnp.zeros((T, D), F32)

    dact = dot_nt(dmlp_ref[...], w2_ref[...].reshape(D, D))
    dpre = (dact * slope_ref[...].astype(F32)).astype(BF)
    db1_ref[...] = col_sum(dpre.astype(F32))
    put_quarter((one, two, three, four), dpre)
    total[...] += dot_nt(dpre, w1_ref[...].reshape(D, D))

    @pl.when(step == TP - 1)
    def _():
        end_norm(
            mid_ref, gain_ref, grad[...], dmlp_ref[...], total[...], dmid_ref, dattn_ref, rows_ref
        )


def select_rows_t(matrix, value):
    high = value.astype(BF)
    rest = value - high.astype(F32)
    mid = rest.astype(BF)
    low = (rest - mid.astype(F32)).astype(BF)
    return dot_tn(matrix, high) + dot_tn(matrix, mid) + dot_tn(matrix, low)


def mlp_backward(core, grad, halo, mid, gain, weights, slope):
    return run(
        mlp_back_kernel,
        TP,
        core,
        (grad, halo, const(OWN), const(SENT), mid, gain, weights, weights, slope),
        [
            whole((T, D)),
            whole((SEND, D)),
            whole((T, T)),
            whole((SEND, T)),
            whole((T, D)),
            whole((1, D)),
            quad_spec(0),
            quad_spec(1),
            wide_spec(T),
        ],
        [
            shape_of((T, D), F32),
            shape_of((T, D), BF),
            shape_of((T, D), BF),
            shape_of((1, FF), F32),
            shape_of((4, D), F32),
        ]
        + [shape_of((T, D), BF)] * TP,
        [whole((T, D)), whole((T, D)), whole((T, D)), wide_spec(1), whole((4, D))]
        + [whole((T, D))] * TP,
        [pltpu.VMEM((T, D), F32), pltpu.VMEM((T, D), F32)],
        4 * T * D * FF,
        24 << 20,
    )


def attn_back_kernel(level, *refs):
    (
        core_ref, dmid_ref, dattn_ref, x_ref, gain_ref, wq_ref, wk_ref, wv_ref, wp_ref,
        q_ref, k_ref, v_ref, probs_ref,
    ), refs = refs[:13], refs[13:]
    if level:
        (place_ref,), refs = refs[:1], refs[1:]
    (dx_ref, mine_ref, other_ref, pair_ref, sums_ref, rows_ref), refs = refs[:6], refs[6:]
    if level:
        (sent_ref,), refs = refs[:1], refs[1:]
    (total,) = refs
    step = pl.program_id(0)

    @pl.when(step == 0)
    def _():
        total[...] = jnp.zeros((T, D), F32)

    dheads = dot_nt(dattn_ref[...], wp_ref[...].reshape(256, D)).astype(BF)
    masks = head_masks(ROWS)
    dqs, dks, dvs = [], [], []
    for half in range(2):
        lanes = slice(half * 128, half * 128 + 128)
        dq_parts, dk_parts, dv_parts = [], [], []
        pairs = None
        for w in range(2):
            rows = slice(w * ROWS, (w + 1) * ROWS)
            rounded = probs_ref[0, w, 4 * half : 4 * half + 4].reshape(4 * ROWS, ROWS)
            probs = rounded.astype(F32)
            spread_out = spread_heads(dheads[rows, lanes], masks)
            dprobs = dot_nt(spread_out, v_ref[rows, lanes])
            dv_parts.append(dot_tn(rounded, spread_out))
            inner = jnp.sum(probs * dprobs, axis=-1, keepdims=True)
            dscores = (probs * (dprobs - inner)).astype(BF)
            wide = dscores.astype(F32)
            pairs = wide if pairs is None else pairs + wide
            dq_parts.append(fold_heads(dot(dscores, k_ref[rows, lanes]), masks))
            dk_parts.append(dot_tn(dscores, spread_heads(q_ref[rows, lanes], masks)))
        pair_ref[4 * half : 4 * half + 4] = pairs.reshape(4, ROWS, ROWS)
        dqs.append((jnp.concatenate(dq_parts, axis=0) * SCALE).astype(BF))
        dks.append((jnp.concatenate(dk_parts, axis=0) * SCALE).astype(BF))
        dvs.append(jnp.concatenate(dv_parts, axis=0).astype(BF))

    def set_mine(part):
        mine_ref[...] = part

    def set_other(part):
        other_ref[...] = part

    put_halves(
        core_ref,
        set_mine,
        set_other,
        jnp.concatenate([dqs[0], dks[0], dvs[0]], axis=1),
        jnp.concatenate([dqs[1], dks[1], dvs[1]], axis=1),
    )
    dq = jnp.concatenate(dqs, axis=1)
    dk = jnp.concatenate(dks, axis=1)
    dv = jnp.concatenate(dvs, axis=1)
    sums_ref[0:1] = col_sum(dq.astype(F32))
    sums_ref[1:2] = col_sum(dv.astype(F32))
    total[...] += (
        dot_nt(dq, unfold(wq_ref))
        + dot_nt(dk, unfold(wk_ref))
        + dot_nt(dv, unfold(wv_ref))
    )

    @pl.when(step == TP - 1)
    def _():
        center, spread = norm_stats(x_ref[...])
        normed = center * spread
        upstream = total[...]
        value = dmid_ref[...] + norm_back(upstream, normed, spread, gain_ref[...])
        dx_ref[...] = value
        rows_ref[0:1] = col_sum(upstream * normed)
        rows_ref[1:2] = col_sum(upstream)
        if level:
            sent_ref[...] = dot_tn(place_ref[...], value.astype(BF)).astype(BF)


def attn_backward(core, level, dmid, dattn, state, gain, weights, q, k, v, probs):
    unit = 8 + 4 * level
    block = pl.BlockSpec((T, 256), lambda step, core: (0, step))
    part = pl.BlockSpec((T, 384), lambda step, core: (0, step))
    args = [dmid, dattn, state, gain, weights, weights, weights, weights, q, k, v, probs]
    specs = [whole((T, D)), whole((T, D)), whole((T, D)), whole((1, D))]
    specs += [unit_spec(unit + place) for place in range(4)]
    specs += [
        block,
        block,
        block,
        pl.BlockSpec((1, 2, 8, ROWS, ROWS), lambda step, core: (step, 0, 0, 0, 0)),
    ]
    outs = [
        shape_of((T, D), F32),
        shape_of((T, 1536), BF),
        shape_of((T, 1536), BF),
        shape_of((32, ROWS, ROWS), F32),
        shape_of((2, D), F32),
        shape_of((2, D), F32),
    ]
    out_specs = [
        whole((T, D)),
        part,
        part,
        pl.BlockSpec((8, ROWS, ROWS), lambda step, core: (step, 0, 0)),
        pl.BlockSpec((2, 256), lambda step, core: (0, step)),
        whole((2, D)),
    ]
    if level:
        args.append(const(RECV))
        specs.append(whole((T, SEND)))
        outs.append(shape_of((SEND, D), BF))
        out_specs.append(whole((SEND, D)))
    return run(
        partial(attn_back_kernel, level),
        TP,
        core,
        args,
        specs,
        outs,
        out_specs,
        [pltpu.VMEM((T, D), F32)],
        8 * T * D * D,
        24 << 20,
    )


def weight_kernel(plan, *refs):
    refs, out_ref = refs[1:-1], refs[-1]
    place = 0
    column = 0
    for kind, size, count in plan:
        parts = [ref[...] for ref in refs[place : place + count]]
        if kind == "matrix":
            value = dot_tn(
                jnp.concatenate(parts[:2], axis=0), jnp.concatenate(parts[2:], axis=0)
            )
        else:
            value = sum(part.astype(F32) for part in parts)
        out_ref[:, 0, :, column : column + size] = value.astype(BF).reshape(YX, 64, size)
        column += size
        place += count


def weight_grads(core, items, sums):
    plan, args, specs = [], [], []
    for left, right in items:
        size = right[0].shape[1] // TP
        plan.append(("matrix", size, 4))
        args += [left[0], left[1], right[0], right[1]]
        block = pl.BlockSpec((T, size), lambda step, core: (0, step))
        specs += [whole((T, D)), whole((T, D)), block, block]
    for pieces in sums:
        plan.append(("sum", 128, len(pieces)))
        args += pieces
        specs += [pl.BlockSpec((D, 128), lambda step, core: (0, step))] * len(pieces)
    width = sum(size for unused, size, count in plan)
    return run(
        partial(weight_kernel, plan),
        TP,
        core,
        args,
        specs,
        shape_of((YX, TP, 64, width), BF),
        pl.BlockSpec((YX, 1, 64, width), lambda step, core: (0, step, 0, 0)),
        [],
        4 * T * D * width * TP,
        (2 * D * width * TP) + (8 << 20),
    )


def column_kernel(core_ref, *refs):
    lefts, rights, (other_ref, mine_ref) = refs[:TP], refs[TP : 2 * TP], refs[2 * TP :]
    left = jnp.concatenate([ref[...] for ref in lefts], axis=0)
    right = jnp.concatenate([ref[...] for ref in rights], axis=0)
    value = dot_tn(left, right).astype(BF)

    @pl.when(pl.program_id(0) == 0)
    def _():
        other_ref[...] = value

    @pl.when(pl.program_id(0) == 1)
    def _():
        mine_ref[...] = value


def column_grads(core, lefts, rights):
    half = pl.BlockSpec((T, 512), lambda step, core: (0, (core[0] + 1 + step) % 2))
    return run(
        column_kernel,
        2,
        core,
        list(lefts) + list(rights),
        [whole((T, D))] * TP + [half] * TP,
        [shape_of((D, 512), BF)] * 2,
        [whole((D, 512))] * 2,
        [],
        4 * T * D * 2048,
        8 << 20,
    )


def send_ahead(pieces):
    return [pieces[0]] + [
        lax.ppermute(pieces[step], "tp", [(i, (i + step) % TP) for i in range(TP)])
        for step in range(1, TP)
    ]


def send_all(value):
    return send_ahead([value] * TP)


def sum_quarters(value, column):
    pieces = [
        lax.dynamic_index_in_dim(value, (column + step) % TP, 0, keepdims=False)
        for step in range(TP)
    ]
    got = [piece.astype(F32) for piece in send_ahead(pieces)]
    return (got[0] + got[1]) + (got[2] + got[3])


def table_index():
    place = np.zeros((RELS, WIN * 190), np.float32)
    for row in range(WIN):
        for step in range(19):
            for col in range(WIN):
                place[(18 - step) * 19 + row - col + 9, row * 190 + step * WIN + col] = 1
    return place


PAIRS = table_index()


def spread_tables(tables):
    compact = jnp.dot(tables.reshape(64, RELS), jnp.asarray(PAIRS), precision=HIGH)
    compact = compact.reshape(2, 32, WIN, 190)
    rows = [compact[..., (9 - row) * WIN : (9 - row) * WIN + TOK] for row in range(WIN)]
    full = jnp.stack(rows, axis=2).reshape(2, 32, TOK, TOK)
    return jnp.pad(full, ((0, 0), (0, 0), (0, ROWS - TOK), (0, ROWS - TOK)))


def fold_tables(pairs):
    total = jnp.zeros((32, WIN, 190), F32)
    for row in range(WIN):
        low = (9 - row) * WIN
        total = total + jnp.pad(
            pairs[:, row * WIN : (row + 1) * WIN, :TOK], ((0, 0), (0, 0), (low, 90 - low))
        )
    return jnp.dot(total.reshape(32, -1), jnp.asarray(PAIRS.T), precision=HIGH)


def window_masks(level, valid, column):
    place = np.arange(ROWS)
    row = np.minimum(place // WIN, WIN - 1)
    col = jnp.asarray(place % WIN, jnp.int32)
    real = jnp.asarray(place < TOK)
    offset = SHIFT if level else 0
    rolled = column * WIN + col
    usable = (rolled + offset) % GW < valid
    masks = []
    for w in range(2):
        rolled_row = w * WIN + row
        row_region = (rolled_row >= GH - WIN).astype(np.int32) + (rolled_row >= GH - SHIFT)
        col_region = (rolled >= GW - WIN).astype(jnp.int32) + (rolled >= GW - SHIFT)
        region = jnp.asarray(row_region * 3, jnp.int32) + col_region
        allowed = usable[None, :]
        if level:
            allowed = allowed & (region[:, None] == region[None, :])
        mask = jnp.where(allowed, F32(0.0), F32(-100.0))
        mask = jnp.where(real[None, :], mask, F32(-1e30))
        masks.append(jnp.broadcast_to(mask, (ROWS, ROWS)))
    return jnp.stack(masks)


def gather_tp(value, place):
    parts = [value]
    for step in range(1, TP):
        parts.append(lax.ppermute(value, "tp", [(i, (i + step) % TP) for i in range(TP)]))
    stacked = jnp.stack(parts)
    order = (place - jnp.arange(TP)) % TP
    return [lax.dynamic_index_in_dim(stacked, order[i], 0, keepdims=False) for i in range(TP)]


def after(value, others):
    return lax.optimization_barrier((value, others))


def swap_core(value):
    return lax.ppermute(value, "core", [(0, 1), (1, 0)])


def sum_all(value):
    sent = value.astype(BF)
    value = sent.astype(F32) + swap_core(sent).astype(F32)
    for axis in ("x", "y", "tp"):
        sent = value.astype(BF)
        got = [
            lax.ppermute(sent, axis, [(i, (i + gap) % 4) for i in range(4)]).astype(F32)
            for gap in (1, 2, 3)
        ]
        value = (sent.astype(F32) + got[1]) + (got[0] + got[2])
    return value


def body(
    x3,
    res_group,
    merge_gain,
    merge_bias,
    merge_w,
    ln1_gain,
    ln1_bias,
    qkv_w,
    qv_bias,
    rel_table,
    proj_w,
    proj_bias,
    ln2_gain,
    ln2_bias,
    fc1_w,
    fc1_bias,
    fc2_w,
    fc2_bias,
    out_grad,
):
    core_at = lax.axis_index("core")
    chip_at = lax.axis_index("y") * 4 + lax.axis_index("x")
    column = lax.axis_index("tp")
    core = jnp.stack([core_at, column]).astype(jnp.int32)

    piece, late_piece = pack_weights(
        jnp.stack([chip_at, core_at]).astype(jnp.int32),
        fc1_w,
        fc2_w,
        jnp.swapaxes(qkv_w, 1, 2),
        proj_w,
        merge_w.reshape(512, D),
    )
    weights = lax.all_gather(piece.reshape(-1, D), GATHER_AXES, axis=0, tiled=True)
    weights = weights.reshape(64, UNITS, 16, D)
    late_weights = lax.all_gather(late_piece.reshape(-1, D), GATHER_AXES, axis=0, tiled=True)
    late_weights = late_weights.reshape(64, 8, 16, D)

    pages = lax.all_to_all(x3, PAGE_AXES, split_axis=1, concat_axis=0, tiled=True)
    tiles = pages.reshape(GH, TP, WIN, 512).transpose(1, 0, 2, 3).reshape(TP * 2 * TOK, 512)
    parts = lax.all_to_all(tiles, "tp", split_axis=0, concat_axis=0, tiled=True)
    parts = parts.reshape(TP, 2 * TOK, 512)

    packed = jnp.concatenate(
        [
            merge_gain.reshape(-1),
            merge_bias.reshape(-1),
            qv_bias.reshape(-1),
            fc1_bias.reshape(-1),
            rel_table.reshape(-1),
            jnp.zeros((10240 - 9872,), F32),
        ]
    ).reshape(80, 128)
    quarters = [part.reshape(-1) for part in gather_tp(packed, column)]

    def joined(low, shape, axis):
        size = int(np.prod(shape))
        return jnp.concatenate([part[low : low + size].reshape(shape) for part in quarters], axis)

    merge_gain_all = joined(0, (1, 512), 0)
    merge_bias_all = joined(512, (1, 512), 0)
    qv_bias_all = joined(1024, (2, 2, 256), 2)
    fc1_bias_all = joined(2048, (2, 1024), 1)
    tables = spread_tables(joined(4096, (2, 8, RELS), 1))
    tables = [tables[0], tables[1]]

    valid = (res_group[0] + 1) * WIN
    masks = [window_masks(level, valid, column) for level in range(2)]
    spot = np.arange(T) % ROWS
    keep = ((column * WIN + SHIFT + jnp.asarray(spot % WIN, jnp.int32)) % GW < valid) & jnp.asarray(
        spot < TOK
    )
    keep = keep.astype(F32)[:, None]
    page_keep = (jnp.asarray(np.arange(GW), jnp.int32) < valid).astype(BF)[None, :, None]
    tiles = jnp.roll(out_grad[0] * page_keep, (-SHIFT, -SHIFT), (0, 1))
    tiles = tiles.reshape(2, WIN, TP, WIN, D).transpose(2, 0, 1, 3, 4).reshape(TP, 2, TOK, D)
    tiles = jnp.pad(tiles, ((0, 0), (0, 0), (0, ROWS - TOK), (0, 0))).reshape(TP, T, D)
    tiles = [
        lax.dynamic_index_in_dim(tiles, (column + TP - back) % TP, 0, keepdims=False)
        for back in range(TP)
    ]

    weights, (tables, masks, tiles, keep, parts) = after(
        weights, (tables, masks, tiles, keep, parts)
    )
    state, merged_mine, merged_other = merge_forward(
        core, parts, merge_gain_all, merge_bias_all, weights
    )
    halo = None
    pending = [swap_core(merged_other)]
    for level in range(2):
        small = (
            ln1_gain[level : level + 1],
            ln1_bias[level : level + 1],
            qv_bias_all[level, 0:1],
            qv_bias_all[level, 1:2],
            proj_bias[level : level + 1],
        )
        got = attn_forward(
            core, level, state, halo, weights, small, tables[level], masks[level]
        )
        mid, a, q, k, v, probs, heads_mine, heads_other = got[:8]
        start = got[8] if level else state
        mid, pending = after(mid, pending)
        small = (
            ln2_gain[level : level + 1],
            ln2_bias[level : level + 1],
            fc1_bias_all[level : level + 1],
            fc2_bias[level : level + 1],
        )
        if level:
            got = mlp_both(core, mid, late_weights, small, keep, tiles[0])
            c2, extra, *acts = got[:6]
            dmid, dattn, db1, rows_two, dpre_mine, dpre_other = got[6:]
            dattn, (a_zero, heads_zero, c2_all, a_sent, heads_sent) = after(
                dattn, (*pending, c2_all, a, heads_other)
            )
        else:
            swapped = [swap_core(a), swap_core(heads_other)]
            c2, slope, halo, act_mine, act_other, state = mlp_forward(core, mid, weights, small)
            (merged_got,) = pending
            pending = swapped
            kept = (start, mid, a, q, k, v, probs, slope, c2, heads_mine)
            halo = lax.ppermute(halo, "tp", [((i + 1) % TP, i) for i in range(TP)])
            halo, c2 = lax.optimization_barrier((halo, c2))
            c2_all = send_all(c2)
    acts = send_ahead(acts)
    a_got, heads_got, dpre_got, dattn_got, c2_got = [
        swap_core(value) for value in (a_sent, heads_sent, dpre_other, dattn, c2)
    ]

    sums = [None, None]
    got = attn_backward(core, 1, dmid, dattn, start, ln1_gain[1:2], weights, q, k, v, probs)
    grad, mixed_mine, mixed_other, pairs, dqv, rows_one, sent = got
    sent, (a_got, heads_got, dpre_got, dattn_got, c2_got) = after(
        sent, (a_got, heads_got, dpre_got, dattn_got, c2_got)
    )
    halo = lax.ppermute(sent, "tp", [(i, (i + 1) % TP) for i in range(TP)])
    mixed_got = swap_core(mixed_other)
    sums[1] = (db1, rows_two, dqv, rows_one, pairs)
    items = [
        ((c2, c2_got), (dpre_mine, dpre_got)),
        ((a, a_got), (mixed_mine, mixed_got)),
        ((dattn, dattn_got), (heads_mine, heads_got)),
    ]
    late = weight_grads(core, items, [])
    late, halo = lax.optimization_barrier((late, halo))
    late = lax.psum_scatter(late, CHIP_AXES, scatter_dimension=0, tiled=True)
    late = lax.optimization_barrier(late)[0]

    start, mid, a, q, k, v, probs, slope, c2, heads_mine = kept
    halo, act_other = lax.optimization_barrier((halo, act_other))
    act_got = swap_core(act_other)
    got = mlp_backward(core, grad, halo, mid, ln2_gain[0:1], weights, slope)
    dmid, dmlp, dattn, db1, rows_two = got[:5]
    dattn, (dpre, act_got, acts, tiles) = after(dattn, (list(got[5:]), act_got, acts, tiles))
    dpre = send_ahead(dpre)
    got = attn_backward(core, 0, dmid, dattn, start, ln1_gain[0:1], weights, q, k, v, probs)
    grad, mixed_mine, mixed_other, pairs, dqv, rows_one = got
    sums[0] = (db1, rows_two, dqv, rows_one, pairs)
    grad, dattn_sent = lax.optimization_barrier((grad, dattn))
    mixed_got, dattn_got = [swap_core(value) for value in (mixed_other, dattn_sent)]
    first, dm, dgain, dbias = merge_backward(core, parts, merge_gain_all, weights, grad)
    last_other, last_mine = column_grads(core, tiles, acts)
    first, (dpre, dmlp_sent, last_other) = after(first, (dpre, dmlp, last_other))
    first_got, dmlp_got = swap_core(first), swap_core(dmlp_sent)
    up_other, up_mine = column_grads(core, c2_all, dpre)
    items = [
        ((a, a_zero), (mixed_mine, mixed_got)),
        ((dattn, dattn_got), (heads_mine, heads_zero)),
        ((first, first_got), (merged_mine, merged_got)),
        ((dmlp, dmlp_got), (act_mine, act_got)),
    ]
    early = weight_grads(
        core, items, [[up_mine, swap_core(up_other)], [last_mine, swap_core(last_other)]]
    )
    early, (extra, sums, dgain, dbias) = after(early, (extra, sums, dgain, dbias))
    early = lax.psum_scatter(early, CHIP_AXES, scatter_dimension=0, tiled=True)
    early = lax.optimization_barrier(early)[0]

    tiles_out = jnp.stack(gather_tp(extra, column)).reshape(TP, GH, WIN, D)
    output = jnp.roll(tiles_out.transpose(1, 0, 2, 3).reshape(GH, GW, D), SHIFT, 1)
    output = output.astype(F32)[None]
    back = lax.all_to_all(
        dm.reshape(TP * 2 * TOK, 512), "tp", split_axis=0, concat_axis=0, tiled=True
    )
    back = back.reshape(TP, GH, WIN, 512).transpose(1, 0, 2, 3).reshape(800, 1, 4, 128)
    grad_x3 = lax.all_to_all(back, PAGE_AXES, split_axis=0, concat_axis=1, tiled=True).astype(F32)

    def both_cores(value):
        rows = value.reshape(2, 32, -1)
        kept_rows = lax.dynamic_index_in_dim(rows, core_at, 0, keepdims=False).astype(F32)
        sent_rows = lax.dynamic_index_in_dim(rows, 1 - core_at, 0, keepdims=False)
        got_rows = swap_core(sent_rows.astype(BF)).astype(F32)
        return (
            jnp.where(core_at == 0, kept_rows, got_rows),
            jnp.where(core_at == 0, got_rows, kept_rows),
        )

    def wide(halves, low, size):
        return jnp.concatenate([half[:, low : low + size] for half in halves], axis=1)

    def finish(value, split):
        complete = value[..., split:].reshape(TP, 64, -1, 128).transpose(1, 2, 0, 3)
        partial_sums = sum_quarters(value[..., :split], column)
        return both_cores(
            jnp.concatenate([partial_sums, complete.reshape(64, -1).astype(F32)], axis=1)
        )

    late = both_cores(sum_quarters(late, column))
    early = finish(early, 1280)
    g_fc1 = jnp.stack([wide(early, 1280, 512), wide(late, 0, 512)])
    g_fc2 = jnp.stack([wide(early, 768, 512).T, wide(early, 1792, 512).T])
    pair = ((early, 0), (late, 512))
    g_qkv = jnp.stack(
        [jnp.stack([wide(half, low + 128 * s, 128) for s in range(3)], axis=1) for half, low in pair]
    )
    g_proj = jnp.stack([wide(half, low + 384, 128).T for half, low in pair])
    g_merge_w = wide(early, 512, 256).T.reshape(4, 128, 32)

    flat = []
    for level in range(2):
        db1, rows_two, dqv, rows_one, pairs = sums[level]
        flat += [rows_one, rows_two, dqv, db1, fold_tables(pairs)]
    flat += [dgain, dbias]
    flat = jnp.concatenate([item.reshape(-1) for item in flat])
    count = flat.shape[0]
    flat = jnp.pad(flat, (0, -count % 16384)).reshape(-1, 1024)
    flat = sum_all(flat).reshape(-1)
    page_at = chip_at * 2 + core_at

    def take(low, shape):
        return flat[low : low + int(np.prod(shape))].reshape(shape)

    def page_part(value):
        return lax.dynamic_slice_in_dim(value, page_at * 32, 32, value.ndim - 1)

    def tp_part(value, axis):
        size = value.shape[axis] // TP
        return lax.dynamic_slice_in_dim(value, column * size, size, axis)

    span = 2 * D + 4 * D + 2 * D + FF + 32 * RELS
    rows = [take(level * span, (6, D)) for level in range(2)]
    rows = page_part(jnp.stack(rows))
    dqv = tp_part(jnp.stack([take(level * span + 6 * D, (2, D)) for level in range(2)]), 2)
    db1 = tp_part(jnp.stack([take(level * span + 8 * D, (FF,)) for level in range(2)]), 1)
    table = tp_part(
        jnp.stack([take(level * span + 8 * D + FF, (32, RELS)) for level in range(2)]), 1
    )
    dgain = tp_part(take(2 * span, (TP, 512)), 0).reshape(4, 128)
    dbias = tp_part(take(2 * span + MERGED, (TP, 512)), 0).reshape(4, 128)
    return (
        output,
        grad_x3,
        dgain,
        dbias,
        g_merge_w,
        rows[:, 0],
        rows[:, 1],
        g_qkv,
        dqv,
        table,
        g_proj,
        rows[:, 5],
        rows[:, 2],
        rows[:, 3],
        g_fc1,
        db1,
        g_fc2,
        rows[:, 4],
    )


def solution(mesh):
    grid = Mesh(mesh.devices.reshape(4, 4, 2, TP), ("y", "x", "core", "tp"))
    page = PAGE_AXES
    return jax.shard_map(
        body,
        mesh=grid,
        in_specs=(
            P(page, None, None, "tp"),
            P(page),
            P(None, "tp"),
            P(None, "tp"),
            P(None, "tp", None),
            P(),
            P(),
            P(None, None, None, "tp"),
            P(None, None, "tp"),
            P(None, "tp", None),
            P(None, "tp", None),
            P(),
            P(),
            P(),
            P(None, None, "tp"),
            P(None, "tp"),
            P(None, "tp", None),
            P(),
            P(page, None, None, None),
        ),
        out_specs=(
            P(page, None, None, None),
            P(page, None, None, "tp"),
            P(None, "tp"),
            P(None, "tp"),
            P(None, "tp", page),
            P(None, page),
            P(None, page),
            P(None, page, None, "tp"),
            P(None, None, "tp"),
            P(None, "tp", None),
            P(None, "tp", page),
            P(None, page),
            P(None, page),
            P(None, page),
            P(None, page, "tp"),
            P(None, "tp"),
            P(None, "tp", page),
            P(None, page),
        ),
        check_vma=False,
    )
```

profile of v0, /device:TPU:1, one launch (start us, length us, event | category | flops | bytes accessed | tf_op | source)
XLA Modules:
  0.0 519.1 jit_solution(10361792113011299986)
XLA Ops:
  7.9 2.7 shard_map.511
  12.2 2.5 collective-permute-start
  14.7 3.3 collective-permute-start.1
  19.9 9.0 %all-to-all-start = ((bf16[25,32,4,128]{3,2,0,1:T(4,128)(2,1)}), bf16[25,32,4,128]{3,2,0,1:T(4,128)(2,1)}, u32[]{:S(2)}, u32[]{:S(2)}) async-start(bf16[25,32,4,128]{3,2,0,1:T(4,128)(2,1)} %copy.96), calls=%async_computation | async-start | bytes 1638400 | tf_op jit(solution)/shard_map/all_to_all | solution.py:1049
  31.8 2.5 reshape.582
  34.3 1.7 copy.94
  52.0 5.7 %fusion.16 = f32[2,32,10,190]{3,1,2,0:T(8,128)S(1)} fusion(f32[10,190,361,1]{2,1,0,3:T(8,128)} %constant.309, f32[2,8,361]{2,1,0:T(8,128)S(1)} %reshape.580, f32[2,8,361]{2,1,0:T(8,128)S(1)} %reshape.578, f32[2,8,361]{2,1,0:T(8,128)S(1)} %reshape.576, f32[2,8,361]{2,1,0:T(8,128)S(1)} %reshape.574), kind=kOutput, calls=%fused_computation.80 | convolution fusion | flops 526840512 | bytes 3322416 | tf_op jit(solution)/shard_map/dot_general | solution.py:940
  59.7 1.9 copy.93
  63.7 2.2 reshape.585
  66.0 2.0 copy.97
  69.1 4.4 all-to-all-start.1
  73.6 2.6 fusion.1
  76.8 17.8 %all-to-all-done.1.x_ref = bf16[4,200,512]{2,1,0:T(8,128)(2,1)} async-done(((bf16[4,200,512]{2,1,0:T(8,128)(2,1)}), bf16[4,200,512]{2,1,0:T(8,128)(2,1)}, u32[]{:S(2)}, u32[]{:S(2)}) %all-to-all-start.1) | async-done | bytes 819232 | tf_op jit(solution)/shard_map/all_to_all | solution.py:1051
  94.6 45.6 %all-gather.3.cloned.1.call-done = bf16[18432,1024]{1,0:T(8,128)(2,1)} async-done(((bf16[144,1024]{1,0:T(8,128)(2,1)}), bf16[18432,1024]{1,0:T(8,128)(2,1)}) %all-gather.3.cloned.1.call-update) | async-done | bytes 37748752 | tf_op jit(solution)/shard_map/all_gather | solution.py:1044
  140.2 7.4 %shard_map.512 = (f32[224,1024]{1,0:T(8,128)}, bf16[224,1024]{1,0:T(8,128)(2,1)}, bf16[224,1024]{1,0:T(8,128)(2,1)}) custom-call(s32[2]{0:T(128)} %pad_add_fusion.2.core_ref.refs_0_, bf16[4,200,512]{2,1,0:T(8,128)(2,1)} %all-to-all-done.1.x_ref, bf16[200,224]{1,0:T(8,128)(2,1)} %constant.244.clone.pack_ref, f32[4,1,512]{2,1,0:T(1,128)} %reshape.590.gain_ref, ...), custom_call_target="tpu_custom_call" | custom-call | bytes 1024 | tf_op jit(solution)/shard_map/pallas_call | solution.py:117
  147.9 11.3 %shard_map.513 = (f32[224,1024]{1,0:T(8,128)}, bf16[224,1024]{1,0:T(8,128)(2,1)}, bf16[224,1024]{1,0:T(8,128)(2,1)}, bf16[224,1024]{1,0:T(8,128)(2,1)}, bf16[224...) custom-call(s32[2]{0:T(128)} %pad_add_fusion.2.core_ref.refs_0_, ...), custom_call_target="tpu_custom_call" | custom-call | bytes 1024 | tf_op jit(solution)/shard_map/pallas_call | solution.py:117
  160.2 13.3 %shard_map.514 = (bf16[224,1024]{1,0:T(8,128)(2,1)}, bf16[224,4096]{1,0:T(8,128)(2,1)}, bf16[112,1024]{1,0:T(8,128)(2,1)}, bf16[224,2048]{1,0:T(8,128)(2,1)}, bf...) custom-call(s32[2]{0:T(128)} %pad_add_fusion.2.core_ref.refs_0_, f32[224,1024]{1,0:T(8,128)} %get-tuple-element.171.mid_ref, ...), custom_call_target="tpu_custom_call" | custom-call | bytes 1024 | tf_op jit(solution)/shard_map/pallas_call | solution.py:117
  175.4 8.9 %collective-permute-done.4.refs_2_ = bf16[112,1024]{1,0:T(8,128)(2,1)S(1)} collective-permute-done((bf16[112,1024]{1,0:T(8,128)(2,1)}, bf16[112,1024]{1,0:T(8,128)(2,1)S(1)}, u32[]{:S(2)}, u32[]{:S(2)}) %collective-permute-start.4) | collective-permute-done | bytes 229408 | tf_op jit(solution)/shard_map/ppermute | solution.py:1134
  184.3 1.6 collective-permute-start.8
  187.4 12.2 %shard_map.515 = (f32[224,1024]{1,0:T(8,128)}, bf16[224,1024]{1,0:T(8,128)(2,1)}, bf16[224,1024]{1,0:T(8,128)(2,1)}, bf16[224,1024]{1,0:T(8,128)(2,1)}, bf16[224...) custom-call(s32[2]{0:T(128)} %pad_add_fusion.2.core_ref.refs_0_, ...), custom_call_target="tpu_custom_call" | custom-call | bytes 1024 | tf_op jit(solution)/shard_map/pallas_call | solution.py:117
  199.7 34.0 %all-gather.5.cloned.1.call-done = bf16[8192,1024]{1,0:T(8,128)(2,1)} async-done(((bf16[64,1024]{1,0:T(8,128)(2,1)}), bf16[8192,1024]{1,0:T(8,128)(2,1)}) %all-gather.5.cloned.1.call-update) | async-done | bytes 16777232 | tf_op jit(solution)/shard_map/all_gather | solution.py:1046
  233.6 20.4 %shard_map.516 = (bf16[224,1024]{1,0:T(8,128)(2,1)}, bf16[200,1024]{1,0:T(8,128)(2,1)}, bf16[224,1024]{1,0:T(8,128)(2,1)}, bf16[224,1024]{1,0:T(8,128)(2,1)}, bf...) custom-call(s32[2]{0:T(128)} %pad_add_fusion.2.core_ref.refs_0_, ...), custom_call_target="tpu_custom_call" | custom-call | bytes 1024 | tf_op jit(solution)/shard_map/pallas_call | solution.py:117
  254.7 15.9 %shard_map.517 = (f32[224,1024]{1,0:T(8,128)}, bf16[224,1536]{1,0:T(8,128)(2,1)}, bf16[224,1536]{1,0:T(8,128)(2,1)}, f32[32,112,112]{2,1,0:T(8,128)}, f32[2,1024...) custom-call(s32[2]{0:T(128)} %pad_add_fusion.2.core_ref.refs_0_, f32[224,1024]{1,0:T(8,128)} %get-tuple-element.191.refs_1_, ...), custom_call_target="tpu_custom_call" | custom-call | bytes 1024 | tf_op jit(solution)/shard_map/pallas_call | solution.py:117
  271.8 2.7 collective-permute-done.11.refs_12_
  276.0 11.1 %shard_map.518 = bf16[16,4,64,1024]{3,2,1,0:T(8,128)(2,1)} custom-call(s32[2]{0:T(128)} %pad_add_fusion.2.core_ref.refs_0_, bf16[224,1024]{1,0:T(8,128)(2,1)} %get-tuple-element.199.refs_1_, bf16[224,1024]{1,0:T(8,128)(2,1)} %copy-done.24, bf16[224,2048]{1,0:T(8,128)(2,1)} %get-tuple-element.205.refs_3_, bf16[224,2048]{1,0:T(8,128)(2,1)} %copy-done.9, ...), custom_call_target="tpu_custom_call" | custom-call | bytes 1024 | tf_op jit(solution)/shard_map/pallas_call | solution.py:117
  288.8 3.5 collective-permute-start.19
  292.4 1.7 collective-permute-start.20
  294.1 14.9 %shard_map.519 = (f32[224,1024]{1,0:T(8,128)}, bf16[224,1024]{1,0:T(8,128)(2,1)}, bf16[224,1024]{1,0:T(8,128)(2,1)}, f32[1,4096]{1,0:T(1,128)}, f32[4,1024]{1,0:...) custom-call(s32[2]{0:T(128)} %pad_add_fusion.2.core_ref.refs_0_, ...), custom_call_target="tpu_custom_call" | custom-call | bytes 1024 | tf_op jit(solution)/shard_map/pallas_call | solution.py:117
  309.0 4.0 collective-permute-done.19.refs_6_
  313.1 3.3 collective-permute-start.24
  316.4 1.6 collective-permute-start.25
  318.0 15.4 %shard_map.520 = (f32[224,1024]{1,0:T(8,128)}, bf16[224,1536]{1,0:T(8,128)(2,1)}, bf16[224,1536]{1,0:T(8,128)(2,1)}, f32[32,112,112]{2,1,0:T(8,128)}, f32[2,1024]{1,0:T(2,128)}, /*index=5*/f32[2,1024]{1,0:T(2,128)}) custom-call(s32[2]{0:T(128)} %pad_add_fusion.2.core_ref.refs_0_, f32[224,1024]{1,0:T(8,128)} %get-tuple-element.218.refs_1_, ...), custom_call_target="tpu_custom_call" | custom-call | bytes 1024 | tf_op jit(solution)/shard_map/pallas_call | solution.py:117
  333.4 8.3 %shard_map.521 = (bf16[224,1024]{1,0:T(8,128)(2,1)}, bf16[4,200,512]{2,1,0:T(8,128)(2,1)}, f32[4,1,512]{2,1,0:T(1,128)}, f32[4,1,512]{2,1,0:T(1,128)}) custom-call(s32[2]{0:T(128)} %pad_add_fusion.2.core_ref.refs_0_, bf16[4,200,512]{2,1,0:T(8,128)(2,1)} %all-to-all-done.1.x_ref, bf16[200,224]{1,0:T(8,128)(2,1)} %constant.244.clone.pack_ref, ...), custom_call_target="tpu_custom_call" | custom-call | bytes 1024 | tf_op jit(solution)/shard_map/pallas_call | solution.py:117
  341.7 6.9 %shard_map.522 = (bf16[1024,512]{1,0:T(8,128)(2,1)}, bf16[1024,512]{1,0:T(8,128)(2,1)}) custom-call(s32[2]{0:T(128)} %pad_add_fusion.2.core_ref.refs_0_, bf16[224,1024]{1,0:T(8,128)(2,1)} %get-tuple-element.250.dx_ref.refs_0_, bf16[224,1024]{1,0:T(8,128)(2,1)} %get-tuple-element.251.refs_1_, bf16[224,1024]{1,0:T(8,128)(2,1)} %get-tuple-element.252.refs_2_, ...), custom_call_target="tpu_custom_call" | custom-call | bytes 1024 | tf_op jit(solution)/shard_map/pallas_call | solution.py:117
  349.7 6.9 %shard_map.523 = (bf16[1024,512]{1,0:T(8,128)(2,1)}, bf16[1024,512]{1,0:T(8,128)(2,1)}) custom-call(s32[2]{0:T(128)} %pad_add_fusion.2.core_ref.refs_0_, bf16[224,1024]{1,0:T(8,128)(2,1)} %get-tuple-element.265.refs_0_, bf16[224,1024]{1,0:T(8,128)(2,1)} %copy-done.15, bf16[224,1024]{1,0:T(8,128)(2,1)} %copy-done.16, bf16[224,1024]{1,0:T(8,128)(2,1)} %copy-done.17, ...), custom_call_target="tpu_custom_call" | custom-call | bytes 1024 | tf_op jit(solution)/shard_map/pallas_call | solution.py:117
  356.6 2.0 collective-permute-start.28
  359.7 4.4 collective-permute-done.22.refs_6_
  367.3 14.8 %shard_map.524 = bf16[16,4,64,1536]{3,2,1,0:T(8,128)(2,1)} custom-call(s32[2]{0:T(128)} %pad_add_fusion.2.core_ref.refs_0_, bf16[224,1024]{1,0:T(8,128)(2,1)} %get-tuple-element.168.refs_1_, bf16[224,1024]{1,0:T(8,128)(2,1)} %copy-done.14, bf16[224,1536]{1,0:T(8,128)(2,1)} %get-tuple-element.237.refs_3_, bf16[224,1536]{1,0:T(8,128)(2,1)} %copy-done.11, ...), custom_call_target="tpu_custom_call" | custom-call | bytes 1024 | tf_op jit(solution)/shard_map/pallas_call | solution.py:117
  382.2 4.8 all-to-all-start.2
  389.4 2.6 convolution_convert_fusion
  392.1 2.3 fusion.31
  396.7 2.6 convolution_convert_fusion.1
  401.9 1.6 copy.102
  405.0 7.4 %all-to-all-start.3 = ((bf16[800,1,4,128]{3,2,1,0:T(4,128)(2,1)}), bf16[800,1,4,128]{3,2,1,0:T(4,128)(2,1)S(1)}, u32[]{:S(2)}, u32[]{:S(2)}) async-start(bf16[800,1,4,128]{3,2,1,0:T(4,128)(2,1)} %bitcast.77), calls=%async_computation.3 | async-start | bytes 1638400 | tf_op jit(solution)/shard_map/all_to_all | solution.py:1198
  412.4 3.0 collective-permute-start.34
  415.7 2.4 collective-permute-start.36
  418.1 19.8 %collective-permute-done.34 = bf16[64,1024]{1,0:T(8,128)(2,1)S(1)} collective-permute-done((bf16[64,1024]{1,0:T(8,128)(2,1)S(1)}, bf16[64,1024]{1,0:T(8,128)(2,1)S(1)}, u32[]{:S(2)}, u32[]{:S(2)}) %collective-permute-start.34) | collective-permute-done | bytes 131104 | tf_op jit(solution)/shard_map/ppermute | solution.py:1003
  440.7 3.1 collective-permute-start.37
  443.8 1.8 collective-permute-start.30
  445.6 2.7 collective-permute-start.31
  450.1 2.3 collective-permute-start.39
  452.5 1.6 copy.107
  454.1 4.4 collective-permute-done.38
  458.5 3.1 collective-permute-start.40
  461.9 2.4 collective-permute-start.42
  469.4 3.6 copy.106
  476.8 1.6 collective-permute-start.47
  478.3 3.5 collective-permute-start.48
  483.5 4.2 collective-permute-done.48
  488.6 1.6 collective-permute-start.50
  491.3 2.4 reduce-scatter.7.cloned.1.call-done
  496.3 2.5 collective-permute-start.44
  501.4 4.3 collective-permute-done.44
  505.8 2.0 collective-permute-start.46
  (411 shorter events, 71.1 us)
Async XLA Ops:
  7.2 133.1 %all-gather.3.cloned.1.call-start = ((), (), s32[]{:S(2)}) async-start(), calls=%async_computation.6 | async-start | bytes 38043648 | tf_op jit(solution)/shard_map/all_gather | solution.py:1044
  10.6 223.1 %all-gather.5.cloned.1.call-start = ((), (), s32[]{:S(2)}) async-start(), calls=%async_computation.7 | async-start | bytes 16908288 | tf_op jit(solution)/shard_map/all_gather | solution.py:1046
  12.2 38.3 %collective-permute-start = (f32[80,128]{1,0:T(8,128)}, f32[80,128]{1,0:T(8,128)}, u32[]{:S(2)}, u32[]{:S(2)}) collective-permute-start(f32[80,128]{1,0:T(8,128)} %bitcast.10), channel_id=1, source_target_pairs={{0,1},{1,2},{2,3},{3,0},{4,5},{5,6},{6,7},{7,4},{8,9},{9,10},{10,1... | collective-permute-start | bytes 122888 | tf_op jit(solution)/shard_map/ppermute | solution.py:983
  14.7 35.9 %collective-permute-start.1 = (f32[80,128]{1,0:T(8,128)}, f32[80,128]{1,0:T(8,128)}, u32[]{:S(2)}, u32[]{:S(2)}) collective-permute-start(f32[80,128]{1,0:T(8,128)} %bitcast.10), channel_id=1, source_target_pairs={{0,2},{1,3},{2,0},{3,1},{4,6},{5,7},{6,4},{7,5},{8,10},{9,11},{10,... | collective-permute-start | bytes 122888 | tf_op jit(solution)/shard_map/ppermute | solution.py:983
  18.0 32.6 %collective-permute-start.2 = (f32[80,128]{1,0:T(8,128)}, f32[80,128]{1,0:T(8,128)}, u32[]{:S(2)}, u32[]{:S(2)}) collective-permute-start(f32[80,128]{1,0:T(8,128)} %bitcast.10), channel_id=1, source_target_pairs={{0,3},{1,0},{2,1},{3,2},{4,7},{5,4},{6,5},{7,6},{8,11},{9,8},{10,9... | collective-permute-start | bytes 122888 | tf_op jit(solution)/shard_map/ppermute | solution.py:983
  19.9 43.8 %all-to-all-start = ((bf16[25,32,4,128]{3,2,0,1:T(4,128)(2,1)}), bf16[25,32,4,128]{3,2,0,1:T(4,128)(2,1)}, u32[]{:S(2)}, u32[]{:S(2)}) async-start(bf16[25,32,4,128]{3,2,0,1:T(4,128)(2,1)} %copy.96), calls=%async_computation | async-start | bytes 1638400 | tf_op jit(solution)/shard_map/all_to_all | solution.py:1049
  69.1 25.5 %all-to-all-start.1 = ((bf16[4,200,512]{2,1,0:T(8,128)(2,1)}), bf16[4,200,512]{2,1,0:T(8,128)(2,1)}, u32[]{:S(2)}, u32[]{:S(2)}) async-start(bf16[4,200,512]{2,1,0:T(8,128)(2,1)} %copy.98), calls=%async_computation.1 | async-start | bytes 1638400 | tf_op jit(solution)/shard_map/all_to_all | solution.py:1051
  73.5 402.0 %reduce-scatter.9.cloned.1.call-start = ((), (), s32[]{:S(2)}) async-start(), calls=%async_computation.9 | async-start | bytes 8912896
  147.6 12.5 %collective-permute-start.3 = (bf16[224,1024]{1,0:T(8,128)(2,1)}, bf16[224,1024]{1,0:T(8,128)(2,1)S(1)}, u32[]{:S(2)}, u32[]{:S(2)}) collective-permute-start(bf16[224,1024]{1,0:T(8,128)(2,1)} %get-tuple-element.170), channel_id=1, source_target_pairs={{0,4},{4,0},{1,5},{5,1},{2,6},{6,2},{3,7},{7,3},{8,12},{12,8},{9,1... | collective-permute-start | bytes 1376264 | tf_op jit(solution)/shard_map/ppermute | solution.py:994
  159.2 40.5 %collective-permute-start.5 = (bf16[224,1024]{1,0:T(8,128)(2,1)}, bf16[224,1024]{1,0:T(8,128)(2,1)S(1)}, u32[]{:S(2)}, u32[]{:S(2)}) collective-permute-start(bf16[224,1024]{1,0:T(8,128)(2,1)} %get-tuple-element.168.refs_1_), channel_id=1, source_target_pairs={{0,4},{4,0},{1,5},{5,1},{2,6},{6,2},{3,7},{7,3},{8,12},{12,8},{9,1... | collective-permute-start | bytes 1376264 | tf_op jit(solution)/shard_map/ppermute | solution.py:994
  173.4 10.9 %collective-permute-start.4 = (bf16[112,1024]{1,0:T(8,128)(2,1)}, bf16[112,1024]{1,0:T(8,128)(2,1)S(1)}, u32[]{:S(2)}, u32[]{:S(2)}) collective-permute-start(bf16[112,1024]{1,0:T(8,128)(2,1)} %get-tuple-element.173), channel_id=1, source_target_pairs={{1,0},{2,1},{3,2},{0,3},{5,4},{6,5},{7,6},{4,7},{9,8},{10,9},{11,1... | collective-permute-start | bytes 688136 | tf_op jit(solution)/shard_map/ppermute | solution.py:1134
  174.1 25.5 %collective-permute-start.6 = (bf16[224,512]{1,0:T(8,128)(2,1)S(1)}, bf16[224,512]{1,0:T(8,128)(2,1)S(1)}, u32[]{:S(2)}, u32[]{:S(2)}) collective-permute-start(bf16[224,512]{1,0:T(8,128)(2,1)S(1)} %copy-done.69), channel_id=1, source_target_pairs={{0,4},{4,0},{1,5},{5,1},{2,6},{6,2},{3,7},{7,3},{8,12},{12,8},{9,1... | collective-permute-start | bytes 688136 | tf_op jit(solution)/shard_map/ppermute | solution.py:994
  184.3 70.3 %collective-permute-start.7 = (bf16[224,1024]{1,0:T(8,128)(2,1)}, bf16[224,1024]{1,0:T(8,128)(2,1)S(1)}, u32[]{:S(2)}, u32[]{:S(2)}) collective-permute-start(bf16[224,1024]{1,0:T(8,128)(2,1)} %get-tuple-element.265.refs_0_), channel_id=1, source_target_pairs={{0,1},{1,2},{2,3},{3,0},{4,5},{5,6},{6,7},{7,4},{8,9},{9,10},{10,1... | collective-permute-start | bytes 1376264 | tf_op jit(solution)/shard_map/ppermute | solution.py:909
  184.3 70.3 %collective-permute-start.8 = (bf16[224,1024]{1,0:T(8,128)(2,1)}, bf16[224,1024]{1,0:T(8,128)(2,1)S(1)}, u32[]{:S(2)}, u32[]{:S(2)}) collective-permute-start(bf16[224,1024]{1,0:T(8,128)(2,1)} %get-tuple-element.265.refs_0_), channel_id=1, source_target_pairs={{0,2},{1,3},{2,0},{3,1},{4,6},{5,7},{6,4},{7,5},{8,10},{9,11},{10,... | collective-permute-start | bytes 1376264 | tf_op jit(solution)/shard_map/ppermute | solution.py:909
  185.9 68.8 %collective-permute-start.9 = (bf16[224,1024]{1,0:T(8,128)(2,1)}, bf16[224,1024]{1,0:T(8,128)(2,1)S(1)}, u32[]{:S(2)}, u32[]{:S(2)}) collective-permute-start(bf16[224,1024]{1,0:T(8,128)(2,1)} %get-tuple-element.265.refs_0_), channel_id=1, source_target_pairs={{0,3},{1,0},{2,1},{3,2},{4,7},{5,4},{6,5},{7,6},{8,11},{9,8},{10,9... | collective-permute-start | bytes 1376264 | tf_op jit(solution)/shard_map/ppermute | solution.py:909
  199.6 54.4 %copy-start.35 = (bf16[224,512]{1,0:T(8,128)(2,1)}, bf16[224,512]{1,0:T(8,128)(2,1)S(1)}, u32[]{:S(2)}) copy-start(bf16[224,512]{1,0:T(8,128)(2,1)S(1)} %collective-permute-done.6.refs_8_) | copy-start | bytes 688132
  199.7 54.4 %copy-start.14 = (bf16[224,1024]{1,0:T(8,128)(2,1)}, bf16[224,1024]{1,0:T(8,128)(2,1)S(1)}, u32[]{:S(2)}) copy-start(bf16[224,1024]{1,0:T(8,128)(2,1)S(1)} %collective-permute-done.5.refs_2_) | copy-start | bytes 1376260
  254.1 20.5 %collective-permute-start.12 = (bf16[224,2048]{1,0:T(8,128)(2,1)}, bf16[224,2048]{1,0:T(8,128)(2,1)S(1)}, u32[]{:S(2)}, u32[]{:S(2)}) collective-permute-start(bf16[224,2048]{1,0:T(8,128)(2,1)} %get-tuple-element.203), channel_id=1, source_target_pairs={{0,4},{4,0},{1,5},{5,1},{2,6},{6,2},{3,7},{7,3},{8,12},{12,8},{9,1... | collective-permute-start | bytes 2752520 | tf_op jit(solution)/shard_map/ppermute | solution.py:994
  254.4 17.1 %collective-permute-start.14 = (bf16[224,1024]{1,0:T(8,128)(2,1)}, bf16[224,1024]{1,0:T(8,128)(2,1)S(1)}, u32[]{:S(2)}, u32[]{:S(2)}) collective-permute-start(bf16[224,1024]{1,0:T(8,128)(2,1)} %get-tuple-element.199.refs_1_), channel_id=1, source_target_pairs={{0,4},{4,0},{1,5},{5,1},{2,6},{6,2},{3,7},{7,3},{8,12},{12,8},{9,1... | collective-permute-start | bytes 1376264 | tf_op jit(solution)/shard_map/ppermute | solution.py:994
  270.6 4.2 collective-permute-start.15
  270.9 3.6 collective-permute-start.10
  271.2 3.3 collective-permute-start.13
  271.5 3.0 collective-permute-start.11
  274.5 12.6 %collective-permute-start.16 = (bf16[112,1024]{1,0:T(8,128)(2,1)}, bf16[112,1024]{1,0:T(8,128)(2,1)S(1)}, u32[]{:S(2)}, u32[]{:S(2)}) collective-permute-start(bf16[112,1024]{1,0:T(8,128)(2,1)} %get-tuple-element.213), channel_id=1, source_target_pairs={{0,1},{1,2},{2,3},{3,0},{4,5},{5,6},{6,7},{7,4},{8,9},{9,10},{10,1... | collective-permute-start | bytes 688136 | tf_op jit(solution)/shard_map/ppermute | solution.py:1148
  287.8 205.9 %reduce-scatter.7.cloned.1.call-start = ((), (), s32[]{:S(2)}) async-start(), calls=%async_computation.8 | async-start | bytes 13369344
  288.4 24.7 %collective-permute-start.17 = (bf16[224,2048]{1,0:T(8,128)(2,1)S(1)}, bf16[224,2048]{1,0:T(8,128)(2,1)S(1)}, u32[]{:S(2)}, u32[]{:S(2)}) collective-permute-start(bf16[224,2048]{1,0:T(8,128)(2,1)S(1)} %copy-done.65), channel_id=1, source_target_pairs={{0,4},{4,0},{1,5},{5,1},{2,6},{6,2},{3,7},{7,3},{8,12},{12,8},{9,1... | collective-permute-start | bytes 2752520 | tf_op jit(solution)/shard_map/ppermute | solution.py:994
  288.6 20.4 %collective-permute-start.18 = (bf16[224,1024]{1,0:T(8,128)(2,1)}, bf16[224,1024]{1,0:T(8,128)(2,1)S(1)}, u32[]{:S(2)}, u32[]{:S(2)}) collective-permute-start(bf16[224,1024]{1,0:T(8,128)(2,1)} %get-tuple-element.226), channel_id=1, source_target_pairs={{0,1},{1,2},{2,3},{3,0},{4,5},{5,6},{6,7},{7,4},{8,9},{9,10},{10,1... | collective-permute-start | bytes 1376264 | tf_op jit(solution)/shard_map/ppermute | solution.py:909
  288.8 24.2 %collective-permute-start.19 = (bf16[224,1024]{1,0:T(8,128)(2,1)S(1)}, bf16[224,1024]{1,0:T(8,128)(2,1)S(1)}, u32[]{:S(2)}, u32[]{:S(2)}) collective-permute-start(bf16[224,1024]{1,0:T(8,128)(2,1)S(1)} %copy-done.67), channel_id=1, source_target_pairs={{0,2},{1,3},{2,0},{3,1},{4,6},{5,7},{6,4},{7,5},{8,10},{9,11},{10,... | collective-permute-start | bytes 1376264 | tf_op jit(solution)/shard_map/ppermute | solution.py:909
  292.4 20.7 %collective-permute-start.20 = (bf16[224,1024]{1,0:T(8,128)(2,1)S(1)}, bf16[224,1024]{1,0:T(8,128)(2,1)S(1)}, u32[]{:S(2)}, u32[]{:S(2)}) collective-permute-start(bf16[224,1024]{1,0:T(8,128)(2,1)S(1)} %copy-done.66), channel_id=1, source_target_pairs={{0,3},{1,0},{2,1},{3,2},{4,7},{5,4},{6,5},{7,6},{8,11},{9,8},{10,9... | collective-permute-start | bytes 1376264 | tf_op jit(solution)/shard_map/ppermute | solution.py:909
  309.0 24.3 %copy-start.21 = (bf16[224,1024]{1,0:T(8,128)(2,1)}, bf16[224,1024]{1,0:T(8,128)(2,1)S(1)}, u32[]{:S(2)}) copy-start(bf16[224,1024]{1,0:T(8,128)(2,1)S(1)} %collective-permute-done.18.refs_5_) | copy-start | bytes 1376260
  313.0 20.3 %copy-start.8 = (bf16[224,2048]{1,0:T(8,128)(2,1)}, bf16[224,2048]{1,0:T(8,128)(2,1)S(1)}, u32[]{:S(2)}) copy-start(bf16[224,2048]{1,0:T(8,128)(2,1)S(1)} %collective-permute-done.17.refs_16_) | copy-start | bytes 2752516
  313.1 35.5 %collective-permute-start.23 = (bf16[224,1024]{1,0:T(8,128)(2,1)}, bf16[224,1024]{1,0:T(8,128)(2,1)S(1)}, u32[]{:S(2)}, u32[]{:S(2)}) collective-permute-start(bf16[224,1024]{1,0:T(8,128)(2,1)} %get-tuple-element.246), channel_id=1, source_target_pairs={{0,1},{1,2},{2,3},{3,0},{4,5},{5,6},{6,7},{7,4},{8,9},{9,10},{10,1... | collective-permute-start | bytes 1376264 | tf_op jit(solution)/shard_map/ppermute | solution.py:909
  313.1 35.5 %collective-permute-start.24 = (bf16[224,1024]{1,0:T(8,128)(2,1)}, bf16[224,1024]{1,0:T(8,128)(2,1)S(1)}, u32[]{:S(2)}, u32[]{:S(2)}) collective-permute-start(bf16[224,1024]{1,0:T(8,128)(2,1)} %get-tuple-element.247), channel_id=1, source_target_pairs={{0,2},{1,3},{2,0},{3,1},{4,6},{5,7},{6,4},{7,5},{8,10},{9,11},{10,... | collective-permute-start | bytes 1376264 | tf_op jit(solution)/shard_map/ppermute | solution.py:909
  316.4 32.2 %collective-permute-start.25 = (bf16[224,1024]{1,0:T(8,128)(2,1)}, bf16[224,1024]{1,0:T(8,128)(2,1)S(1)}, u32[]{:S(2)}, u32[]{:S(2)}) collective-permute-start(bf16[224,1024]{1,0:T(8,128)(2,1)} %get-tuple-element.248), channel_id=1, source_target_pairs={{0,3},{1,0},{2,1},{3,2},{4,7},{5,4},{6,5},{7,6},{8,11},{9,8},{10,9... | collective-permute-start | bytes 1376264 | tf_op jit(solution)/shard_map/ppermute | solution.py:909
  356.6 9.3 %collective-permute-start.28 = (bf16[1024,512]{1,0:T(8,128)(2,1)}, bf16[1024,512]{1,0:T(8,128)(2,1)S(1)}, u32[]{:S(2)}, u32[]{:S(2)}) collective-permute-start(bf16[1024,512]{1,0:T(8,128)(2,1)} %get-tuple-element.274), channel_id=1, source_target_pairs={{0,4},{4,0},{1,5},{5,1},{2,6},{6,2},{3,7},{7,3},{8,12},{12,8},{9,1... | collective-permute-start | bytes 3145736 | tf_op jit(solution)/shard_map/ppermute | solution.py:994
  358.6 7.3 %collective-permute-start.29 = (bf16[1024,512]{1,0:T(8,128)(2,1)S(1)}, bf16[1024,512]{1,0:T(8,128)(2,1)S(1)}, u32[]{:S(2)}, u32[]{:S(2)}) collective-permute-start(bf16[1024,512]{1,0:T(8,128)(2,1)S(1)} %copy-done.64), channel_id=1, source_target_pairs={{0,4},{4,0},{1,5},{5,1},{2,6},{6,2},{3,7},{7,3},{8,12},{12,8},{9,1... | collective-permute-start | bytes 3145736 | tf_op jit(solution)/shard_map/ppermute | solution.py:994
  358.7 5.3 %collective-permute-start.22 = (bf16[224,1024]{1,0:T(8,128)(2,1)S(1)}, bf16[224,1024]{1,0:T(8,128)(2,1)S(1)}, u32[]{:S(2)}, u32[]{:S(2)}) collective-permute-start(bf16[224,1024]{1,0:T(8,128)(2,1)S(1)} %copy-done.3), channel_id=1, source_target_pairs={{0,4},{4,0},{1,5},{5,1},{2,6},{6,2},{3,7},{7,3},{8,12},{12,8},{9,1... | collective-permute-start | bytes 1376264 | tf_op jit(solution)/shard_map/ppermute | solution.py:994
  359.1 5.3 %collective-permute-start.21 = (bf16[224,1536]{1,0:T(8,128)(2,1)}, bf16[224,1536]{1,0:T(8,128)(2,1)S(1)}, u32[]{:S(2)}, u32[]{:S(2)}) collective-permute-start(bf16[224,1536]{1,0:T(8,128)(2,1)} %get-tuple-element.238), channel_id=1, source_target_pairs={{0,4},{4,0},{1,5},{5,1},{2,6},{6,2},{3,7},{7,3},{8,12},{12,8},{9,1... | collective-permute-start | bytes 2064392 | tf_op jit(solution)/shard_map/ppermute | solution.py:994
  359.2 5.5 %collective-permute-start.26 = (bf16[224,1024]{1,0:T(8,128)(2,1)S(1)}, bf16[224,1024]{1,0:T(8,128)(2,1)S(1)}, u32[]{:S(2)}, u32[]{:S(2)}) collective-permute-start(bf16[224,1024]{1,0:T(8,128)(2,1)S(1)} %copy-done.20), channel_id=1, source_target_pairs={{0,4},{4,0},{1,5},{5,1},{2,6},{6,2},{3,7},{7,3},{8,12},{12,8},{9,1... | collective-permute-start | bytes 1376264 | tf_op jit(solution)/shard_map/ppermute | solution.py:994
  364.1 1.8 collective-permute-start.27
  382.2 19.8 %all-to-all-start.2 = ((bf16[4,200,512]{2,1,0:T(8,128)(2,1)}), bf16[4,200,512]{2,1,0:T(8,128)(2,1)}, u32[]{:S(2)}, u32[]{:S(2)}) async-start(bf16[4,200,512]{2,1,0:T(8,128)(2,1)} %get-tuple-element.291), calls=%async_computation.2 | async-start | bytes 1638400 | tf_op jit(solution)/shard_map/all_to_all | solution.py:1194
  401.5 10.9 %collective-permute-start.33 = (bf16[64,1024]{1,0:T(8,128)(2,1)S(1)}, bf16[64,1024]{1,0:T(8,128)(2,1)S(1)}, u32[]{:S(2)}, u32[]{:S(2)}) collective-permute-start(bf16[64,1024]{1,0:T(8,128)(2,1)S(1)} %convert_element_type.193), channel_id=1, source_target_pairs={{0,4},{4,0},{1,5},{5,1},{2,6},{6,2},{3,7},{7,3},{8,12},{12,8},{9,1... | collective-permute-start | bytes 393224 | tf_op jit(solution)/shard_map/ppermute | solution.py:994
  403.8 40.0 %copy-start.33 = (bf16[200,1024]{1,0:T(8,128)(2,1)S(1)}, bf16[200,1024]{1,0:T(8,128)(2,1)}, u32[]{:S(2)}) copy-start(bf16[200,1024]{1,0:T(8,128)(2,1)} %get-tuple-element.290) | copy-start | bytes 1228804
  405.0 47.3 %all-to-all-start.3 = ((bf16[800,1,4,128]{3,2,1,0:T(4,128)(2,1)}), bf16[800,1,4,128]{3,2,1,0:T(4,128)(2,1)S(1)}, u32[]{:S(2)}, u32[]{:S(2)}) async-start(bf16[800,1,4,128]{3,2,1,0:T(4,128)(2,1)} %bitcast.77), calls=%async_computation.3 | async-start | bytes 1638400 | tf_op jit(solution)/shard_map/all_to_all | solution.py:1198
  412.4 25.5 %collective-permute-start.34 = (bf16[64,1024]{1,0:T(8,128)(2,1)S(1)}, bf16[64,1024]{1,0:T(8,128)(2,1)S(1)}, u32[]{:S(2)}, u32[]{:S(2)}) collective-permute-start(bf16[64,1024]{1,0:T(8,128)(2,1)S(1)} %add_convert_fusion.2), channel_id=1, source_target_pairs={{0,16},{8,24},{16,0},{24,8},{1,17},{9,25},{17,1},{25,9},{2,18},{10... | collective-permute-start | bytes 393224 | tf_op jit(solution)/shard_map/ppermute | solution.py:1003
  415.4 24.0 %collective-permute-start.35 = (bf16[64,1024]{1,0:T(8,128)(2,1)S(1)}, bf16[64,1024]{1,0:T(8,128)(2,1)S(1)}, u32[]{:S(2)}, u32[]{:S(2)}) collective-permute-start(bf16[64,1024]{1,0:T(8,128)(2,1)S(1)} %add_convert_fusion.2), channel_id=1, source_target_pairs={{0,8},{8,16},{16,24},{24,0},{1,9},{9,17},{17,25},{25,1},{2,10},{10... | collective-permute-start | bytes 393224 | tf_op jit(solution)/shard_map/ppermute | solution.py:1003
  415.7 24.9 %collective-permute-start.36 = (bf16[64,1024]{1,0:T(8,128)(2,1)S(1)}, bf16[64,1024]{1,0:T(8,128)(2,1)S(1)}, u32[]{:S(2)}, u32[]{:S(2)}) collective-permute-start(bf16[64,1024]{1,0:T(8,128)(2,1)S(1)} %add_convert_fusion.2), channel_id=1, source_target_pairs={{0,24},{8,0},{16,8},{24,16},{1,25},{9,1},{17,9},{25,17},{2,26},{10... | collective-permute-start | bytes 393224 | tf_op jit(solution)/shard_map/ppermute | solution.py:1003
  440.7 9.4 %collective-permute-start.37 = (bf16[64,1024]{1,0:T(8,128)(2,1)S(1)}, bf16[64,1024]{1,0:T(8,128)(2,1)S(1)}, u32[]{:S(2)}, u32[]{:S(2)}) collective-permute-start(bf16[64,1024]{1,0:T(8,128)(2,1)S(1)} %add_convert_fusion.1), channel_id=1, source_target_pairs={{0,64},{32,96},{64,0},{96,32},{1,65},{33,97},{65,1},{97,33},{2,66}... | collective-permute-start | bytes 393224 | tf_op jit(solution)/shard_map/ppermute | solution.py:1003
  443.8 18.1 %collective-permute-start.30 = (bf16[200,1024]{1,0:T(8,128)(2,1)S(1)}, bf16[200,1024]{1,0:T(8,128)(2,1)S(1)}, u32[]{:S(2)}, u32[]{:S(2)}) collective-permute-start(bf16[200,1024]{1,0:T(8,128)(2,1)S(1)} %copy-done.33), channel_id=1, source_target_pairs={{0,1},{1,2},{2,3},{3,0},{4,5},{5,6},{6,7},{7,4},{8,9},{9,10},{10,1... | collective-permute-start | bytes 1228808 | tf_op jit(solution)/shard_map/ppermute | solution.py:983
  445.6 20.1 %collective-permute-start.31 = (bf16[200,1024]{1,0:T(8,128)(2,1)S(1)}, bf16[200,1024]{1,0:T(8,128)(2,1)S(1)}, u32[]{:S(2)}, u32[]{:S(2)}) collective-permute-start(bf16[200,1024]{1,0:T(8,128)(2,1)S(1)} %copy-done.33), channel_id=1, source_target_pairs={{0,2},{1,3},{2,0},{3,1},{4,6},{5,7},{6,4},{7,5},{8,10},{9,11},{10,... | collective-permute-start | bytes 1228808 | tf_op jit(solution)/shard_map/ppermute | solution.py:983
  448.3 17.9 %collective-permute-start.32 = (bf16[200,1024]{1,0:T(8,128)(2,1)S(1)}, bf16[200,1024]{1,0:T(8,128)(2,1)S(1)}, u32[]{:S(2)}, u32[]{:S(2)}) collective-permute-start(bf16[200,1024]{1,0:T(8,128)(2,1)S(1)} %copy-done.33), channel_id=1, source_target_pairs={{0,3},{1,0},{2,1},{3,2},{4,7},{5,4},{6,5},{7,6},{8,11},{9,8},{10,9... | collective-permute-start | bytes 1228808 | tf_op jit(solution)/shard_map/ppermute | solution.py:983
  449.7 8.8 %collective-permute-start.38 = (bf16[64,1024]{1,0:T(8,128)(2,1)S(1)}, bf16[64,1024]{1,0:T(8,128)(2,1)S(1)}, u32[]{:S(2)}, u32[]{:S(2)}) collective-permute-start(bf16[64,1024]{1,0:T(8,128)(2,1)S(1)} %add_convert_fusion.1), channel_id=1, source_target_pairs={{0,32},{32,64},{64,96},{96,0},{1,33},{33,65},{65,97},{97,1},{2,34}... | collective-permute-start | bytes 393224 | tf_op jit(solution)/shard_map/ppermute | solution.py:1003
  450.1 8.4 %collective-permute-start.39 = (bf16[64,1024]{1,0:T(8,128)(2,1)S(1)}, bf16[64,1024]{1,0:T(8,128)(2,1)S(1)}, u32[]{:S(2)}, u32[]{:S(2)}) collective-permute-start(bf16[64,1024]{1,0:T(8,128)(2,1)S(1)} %add_convert_fusion.1), channel_id=1, source_target_pairs={{0,96},{32,0},{64,32},{96,64},{1,97},{33,1},{65,33},{97,65},{2,98}... | collective-permute-start | bytes 393224 | tf_op jit(solution)/shard_map/ppermute | solution.py:1003
  458.5 14.5 %collective-permute-start.40 = (bf16[64,1024]{1,0:T(8,128)(2,1)S(1)}, bf16[64,1024]{1,0:T(8,128)(2,1)S(1)}, u32[]{:S(2)}, u32[]{:S(2)}) collective-permute-start(bf16[64,1024]{1,0:T(8,128)(2,1)S(1)} %add_convert_fusion), channel_id=1, source_target_pairs={{0,2},{1,3},{2,0},{3,1},{4,6},{5,7},{6,4},{7,5},{8,10},{9,11},{10,... | collective-permute-start | bytes 393224 | tf_op jit(solution)/shard_map/ppermute | solution.py:1003
  461.6 11.4 %collective-permute-start.41 = (bf16[64,1024]{1,0:T(8,128)(2,1)S(1)}, bf16[64,1024]{1,0:T(8,128)(2,1)S(1)}, u32[]{:S(2)}, u32[]{:S(2)}) collective-permute-start(bf16[64,1024]{1,0:T(8,128)(2,1)S(1)} %add_convert_fusion), channel_id=1, source_target_pairs={{0,1},{1,2},{2,3},{3,0},{4,5},{5,6},{6,7},{7,4},{8,9},{9,10},{10,1... | collective-permute-start | bytes 393224 | tf_op jit(solution)/shard_map/ppermute | solution.py:1003
  461.9 11.1 %collective-permute-start.42 = (bf16[64,1024]{1,0:T(8,128)(2,1)S(1)}, bf16[64,1024]{1,0:T(8,128)(2,1)S(1)}, u32[]{:S(2)}, u32[]{:S(2)}) collective-permute-start(bf16[64,1024]{1,0:T(8,128)(2,1)S(1)} %add_convert_fusion), channel_id=1, source_target_pairs={{0,3},{1,0},{2,1},{3,2},{4,7},{5,4},{6,5},{7,6},{8,11},{9,8},{10,9... | collective-permute-start | bytes 393224 | tf_op jit(solution)/shard_map/ppermute | solution.py:1003
  476.8 6.7 %collective-permute-start.47 = (bf16[64,1024]{1,0:T(8,128)(2,1)S(1)}, bf16[64,1024]{1,0:T(8,128)(2,1)S(1)}, u32[]{:S(2)}, u32[]{:S(2)}) collective-permute-start(bf16[64,1024]{1,0:T(8,128)(2,1)S(1)} %get-tuple-element.397), channel_id=1, source_target_pairs={{0,1},{1,2},{2,3},{3,0},{4,5},{5,6},{6,7},{7,4},{8,9},{9,10},{10,1... | collective-permute-start | bytes 393224 | tf_op jit(solution)/shard_map/ppermute | solution.py:909
  478.3 9.3 %collective-permute-start.48 = (bf16[64,1024]{1,0:T(8,128)(2,1)S(1)}, bf16[64,1024]{1,0:T(8,128)(2,1)S(1)}, u32[]{:S(2)}, u32[]{:S(2)}) collective-permute-start(bf16[64,1024]{1,0:T(8,128)(2,1)S(1)} %get-tuple-element.399), channel_id=1, source_target_pairs={{0,2},{1,3},{2,0},{3,1},{4,6},{5,7},{6,4},{7,5},{8,10},{9,11},{10,... | collective-permute-start | bytes 393224 | tf_op jit(solution)/shard_map/ppermute | solution.py:909
  481.9 5.7 %collective-permute-start.49 = (bf16[64,1024]{1,0:T(8,128)(2,1)S(1)}, bf16[64,1024]{1,0:T(8,128)(2,1)S(1)}, u32[]{:S(2)}, u32[]{:S(2)}) collective-permute-start(bf16[64,1024]{1,0:T(8,128)(2,1)S(1)} %get-tuple-element.398), channel_id=1, source_target_pairs={{0,3},{1,0},{2,1},{3,2},{4,7},{5,4},{6,5},{7,6},{8,11},{9,8},{10,9... | collective-permute-start | bytes 393224 | tf_op jit(solution)/shard_map/ppermute | solution.py:909
  488.6 2.5 collective-permute-start.50
  494.9 6.5 %collective-permute-start.43 = (bf16[64,1280]{1,0:T(8,128)(2,1)S(1)}, bf16[64,1280]{1,0:T(8,128)(2,1)S(1)}, u32[]{:S(2)}, u32[]{:S(2)}) collective-permute-start(bf16[64,1280]{1,0:T(8,128)(2,1)S(1)} %get-tuple-element.394), channel_id=1, source_target_pairs={{0,1},{1,2},{2,3},{3,0},{4,5},{5,6},{6,7},{7,4},{8,9},{9,10},{10,1... | collective-permute-start | bytes 491528 | tf_op jit(solution)/shard_map/ppermute | solution.py:909
  496.3 9.3 %collective-permute-start.44 = (bf16[64,1280]{1,0:T(8,128)(2,1)S(1)}, bf16[64,1280]{1,0:T(8,128)(2,1)S(1)}, u32[]{:S(2)}, u32[]{:S(2)}) collective-permute-start(bf16[64,1280]{1,0:T(8,128)(2,1)S(1)} %get-tuple-element.396), channel_id=1, source_target_pairs={{0,2},{1,3},{2,0},{3,1},{4,6},{5,7},{6,4},{7,5},{8,10},{9,11},{10,... | collective-permute-start | bytes 491528 | tf_op jit(solution)/shard_map/ppermute | solution.py:909
  498.8 6.8 %collective-permute-start.45 = (bf16[64,1280]{1,0:T(8,128)(2,1)S(1)}, bf16[64,1280]{1,0:T(8,128)(2,1)S(1)}, u32[]{:S(2)}, u32[]{:S(2)}) collective-permute-start(bf16[64,1280]{1,0:T(8,128)(2,1)S(1)} %get-tuple-element.395), channel_id=1, source_target_pairs={{0,3},{1,0},{2,1},{3,2},{4,7},{5,4},{6,5},{7,6},{8,11},{9,8},{10,9... | collective-permute-start | bytes 491528 | tf_op jit(solution)/shard_map/ppermute | solution.py:909
  505.8 3.0 collective-permute-start.46
  (65 other events, 363.9 us)
Sparse Core Ops, SparseCore 0:
  11.0 129.1 all-gather.2
  143.4 90.2 all-gather.4
  287.3 85.0 reduce-scatter.8
  382.3 111.3 reduce-scatter.6
where the time goes:
time: 523 us; the launch traced here: 519 us
  Pallas kernels  161 us (31%)
  waiting for transfers between devices  161 us (31%)
  starting transfers between devices  90 us (17%)
  local copies, waits for them, and re-layouts  55.1 us (11%)
  between operations  24.3 us (5%)
  other arithmetic  16.4 us (3%)
  matrix products  10.9 us (2%)
    pallas_call x13, Pallas kernels, run(): pl.pallas_call(kernel, grid_spec=pltpu.PrefetchScalarGridSpec(num_scalar_...  159 us
    all_gather x1, waiting for transfers between devices, body(): lax.all_gather(piece.reshape(-1, D), GATHER_AXES, axis=0, tiled=True)  45.6 us
    all_gather x1, waiting for transfers between devices, body(): lax.all_gather(late_piece.reshape(-1, D), GATHER_AXES, axis=0, tiled=True)  34 us
    ppermute x9, waiting for transfers between devices, sum_all(): lax.ppermute(sent, axis, [(i, (i + gap) % 4) for i in range(4)]).astype(F32)  27.3 us
    ppermute x15, starting transfers between devices, send_ahead(): lax.ppermute(pieces[step], 'tp', [(i, (i + step) % TP) for i in range(TP)])  23.7 us
    all_to_all x1, waiting for transfers between devices, body(): parts = lax.all_to_all(tiles, 'tp', split_axis=0, concat_axis=0, tiled=True)  17.8 us
    ppermute x9, starting transfers between devices, sum_all(): lax.ppermute(sent, axis, [(i, (i + gap) % 4) for i in range(4)]).astype(F32)  16.8 us
    unnamed x172, local copies, waits for them, and re-layouts  13.5 us
  transfers between devices with their start and end apart: 59, of which 22 were waited for; matrix products, arithmetic and copies ran while one was open for 14% of the time, Pallas kernels for 31%

commit v1 on v0

--- a/solution.py
+++ b/solution.py
@@ -25,7 +25,7 @@
 SCALE = 32 ** (-0.5)
 YX = 16
 TP = 4
-UNITS = 18
+UNITS = 26
 HIGH = lax.Precision.HIGHEST
 BF = jnp.bfloat16
 F32 = jnp.float32
@@ -143,22 +143,18 @@
         other(low)
 
 
-def pack_kernel(
-    place_ref, up_ref, down_ref, mix_ref, proj_ref, merge_ref, out_ref, late_ref, all_ref
-):
-    low = place_ref[1] == 0
-    late_ref[...] = jnp.where(low, up_ref[1], down_ref[1]).reshape(4, 16, D)
-    all_ref[0:4] = up_ref[0].reshape(4, 16, D)
-    all_ref[4:8] = down_ref[0].reshape(4, 16, D)
+def pack_kernel(place_ref, up_ref, down_ref, mix_ref, proj_ref, merge_ref, out_ref, all_ref):
     for level in range(2):
+        all_ref[8 * level : 8 * level + 4] = up_ref[level].reshape(4, 16, D)
+        all_ref[8 * level + 4 : 8 * level + 8] = down_ref[level].reshape(4, 16, D)
         for part in range(3):
             for group in range(4):
-                all_ref[8 + 4 * level + part, :, 256 * group : 256 * group + 256] = mix_ref[
+                all_ref[16 + 4 * level + part, :, 256 * group : 256 * group + 256] = mix_ref[
                     level, part, 16 * group : 16 * group + 16
                 ]
-        all_ref[11 + 4 * level] = proj_ref[level]
-    all_ref[16:18] = merge_ref[...].reshape(2, 16, D)
-    out_ref[...] = all_ref[pl.ds(place_ref[1] * 9, 9)]
+        all_ref[19 + 4 * level] = proj_ref[level]
+    all_ref[24:26] = merge_ref[...].reshape(2, 16, D)
+    out_ref[...] = all_ref[pl.ds(place_ref[1] * 13, 13)]
 
 
 def pack_weights(place, up, down, mix, proj, merge):
@@ -174,10 +170,10 @@
                 pl.BlockSpec((2, 16, D), lambda step, place: (0, place[0], 0)),
                 pl.BlockSpec((32, D), lambda step, place: (place[0], 0)),
             ],
-            out_specs=[whole((9, 16, D)), whole((4, 16, D))],
+            out_specs=whole((13, 16, D)),
             scratch_shapes=[pltpu.VMEM((UNITS, 16, D), BF)],
         ),
-        out_shape=[shape_of((9, 16, D), BF), shape_of((4, 16, D), BF)],
+        out_shape=shape_of((13, 16, D), BF),
         compiler_params=pltpu.CompilerParams(vmem_limit_bytes=VMEM),
         cost_estimate=pl.CostEstimate(flops=0, bytes_accessed=1 << 20, transcendentals=0),
     )(place, up, down, mix, proj, merge)
@@ -240,7 +236,7 @@
             whole((2 * TOK, T)),
             pl.BlockSpec((1, 1, 512), lambda step, core: (step, 0, 0)),
             pl.BlockSpec((1, 1, 512), lambda step, core: (step, 0, 0)),
-            pl.BlockSpec((YX, 2, 16, D), lambda step, core: (step, 8, 0, 0)),
+            pl.BlockSpec((YX, 2, 16, D), lambda step, core: (step, 12, 0, 0)),
         ],
         [shape_of((T, D), F32), shape_of((T, D), BF), shape_of((T, D), BF)],
         [
@@ -299,7 +295,7 @@
             whole((TP, 2 * TOK, 512)),
             whole((2 * TOK, T)),
             pl.BlockSpec((1, 1, 512), lambda step, core: (step, 0, 0)),
-            pl.BlockSpec((YX, 2, 16, D), lambda step, core: (step, 8, 0, 0)),
+            pl.BlockSpec((YX, 2, 16, D), lambda step, core: (step, 12, 0, 0)),
             whole((T, D)),
         ],
         [
@@ -408,7 +404,7 @@
 
 def attn_forward(core, level, state, halo, weights, small, table, mask):
     gain, bias, qbias, vbias, shift = small
-    unit = 8 + 4 * level
+    unit = 16 + 4 * level
     args = [state]
     specs = [whole((T, D))]
     if level:
@@ -608,8 +604,8 @@
             whole((T, D)),
             whole((1, D)),
             whole((1, D)),
-            quad_spec(0),
-            quad_spec(1),
+            quad_spec(2),
+            quad_spec(3),
             wide_spec(1),
             whole((1, D)),
             whole((2 * TOK, T)),
@@ -782,7 +778,7 @@
 
 
 def attn_backward(core, level, dmid, dattn, state, gain, weights, q, k, v, probs):
-    unit = 8 + 4 * level
+    unit = 16 + 4 * level
     block = pl.BlockSpec((T, 256), lambda step, core: (0, step))
     part = pl.BlockSpec((T, 384), lambda step, core: (0, step))
     args = [dmid, dattn, state, gain, weights, weights, weights, weights, q, k, v, probs]
@@ -1033,7 +1029,7 @@
     column = lax.axis_index("tp")
     core = jnp.stack([core_at, column]).astype(jnp.int32)
 
-    piece, late_piece = pack_weights(
+    piece = pack_weights(
         jnp.stack([chip_at, core_at]).astype(jnp.int32),
         fc1_w,
         fc2_w,
@@ -1043,8 +1039,6 @@
     )
     weights = lax.all_gather(piece.reshape(-1, D), GATHER_AXES, axis=0, tiled=True)
     weights = weights.reshape(64, UNITS, 16, D)
-    late_weights = lax.all_gather(late_piece.reshape(-1, D), GATHER_AXES, axis=0, tiled=True)
-    late_weights = late_weights.reshape(64, 8, 16, D)
 
     pages = lax.all_to_all(x3, PAGE_AXES, split_axis=1, concat_axis=0, tiled=True)
     tiles = pages.reshape(GH, TP, WIN, 512).transpose(1, 0, 2, 3).reshape(TP * 2 * TOK, 512)
@@ -1119,11 +1113,11 @@
             fc2_bias[level : level + 1],
         )
         if level:
-            got = mlp_both(core, mid, late_weights, small, keep, tiles[0])
+            got = mlp_both(core, mid, weights, small, keep, tiles[0])
             c2, extra, *acts = got[:6]
             dmid, dattn, db1, rows_two, dpre_mine, dpre_other = got[6:]
-            dattn, (a_zero, heads_zero, c2_all, a_sent, heads_sent) = after(
-                dattn, (*pending, c2_all, a, heads_other)
+            dattn, (a_zero, heads_zero, c2_all, a_got, heads_got) = after(
+                dattn, (*pending, c2_all, swap_core(a), swap_core(heads_other))
             )
         else:
             swapped = [swap_core(a), swap_core(heads_other)]
@@ -1135,16 +1129,12 @@
             halo, c2 = lax.optimization_barrier((halo, c2))
             c2_all = send_all(c2)
     acts = send_ahead(acts)
-    a_got, heads_got, dpre_got, dattn_got, c2_got = [
-        swap_core(value) for value in (a_sent, heads_sent, dpre_other, dattn, c2)
-    ]
+    dpre_got, dattn_got, c2_got = [swap_core(value) for value in (dpre_other, dattn, c2)]
 
     sums = [None, None]
     got = attn_backward(core, 1, dmid, dattn, start, ln1_gain[1:2], weights, q, k, v, probs)
     grad, mixed_mine, mixed_other, pairs, dqv, rows_one, sent = got
-    sent, (a_got, heads_got, dpre_got, dattn_got, c2_got) = after(
-        sent, (a_got, heads_got, dpre_got, dattn_got, c2_got)
-    )
+    sent, (dpre_got, dattn_got, c2_got) = after(sent, (dpre_got, dattn_got, c2_got))
     halo = lax.ppermute(sent, "tp", [(i, (i + 1) % TP) for i in range(TP)])
     mixed_got = swap_core(mixed_other)
     sums[1] = (db1, rows_two, dqv, rows_one, pairs)

time: 523 us -> 511 us (0.977)
  waiting for transfers between devices: 161 us -> 154 us
    all_gather x1 -> x0, waiting for transfers between devices: 34 us -> none  [body(): lax.all_gather(late_piece.reshape(-1, D), GATHER_AXES, axis=0, tiled=True)]
    all_gather x1, waiting for transfers between devices: 45.6 us -> 79 us  [body(): lax.all_gather(piece.reshape(-1, D), GATHER_AXES, axis=0, tiled=True)]
    all_to_all x1, waiting for transfers between devices: 17.8 us -> 12.1 us  [body(): parts = lax.all_to_all(tiles, 'tp', split_axis=0, concat_axis=0, tiled=True)]
  transfers between devices with their start and end apart: 59 -> 58, of which waited for: 22 -> 24; matrix products, arithmetic and copies ran while one was open for 14% -> 14% of each run, Pallas kernels for 31% -> 30%
where the time goes in v1:
time: 511 us; the launch traced here: 507 us
  Pallas kernels  162 us (32%)
  waiting for transfers between devices  154 us (30%)
  starting transfers between devices  86.9 us (17%)
  local copies, waits for them, and re-layouts  52.4 us (10%)
  between operations  24.2 us (5%)
  other arithmetic  16.4 us (3%)
  matrix products  11.1 us (2%)
    pallas_call x13, Pallas kernels, run(): pl.pallas_call(kernel, grid_spec=pltpu.PrefetchScalarGridSpec(num_scalar_...  160 us
    all_gather x1, waiting for transfers between devices, body(): lax.all_gather(piece.reshape(-1, D), GATHER_AXES, axis=0, tiled=True)  79 us
    ppermute x9, waiting for transfers between devices, sum_all(): lax.ppermute(sent, axis, [(i, (i + gap) % 4) for i in range(4)]).astype(F32)  27.6 us
    ppermute x15, starting transfers between devices, send_ahead(): lax.ppermute(pieces[step], 'tp', [(i, (i + step) % TP) for i in range(TP)])  20.8 us
    ppermute x9, starting transfers between devices, sum_all(): lax.ppermute(sent, axis, [(i, (i + gap) % 4) for i in range(4)]).astype(F32)  16.3 us
    ppermute x15, waiting for transfers between devices, send_ahead(): lax.ppermute(pieces[step], 'tp', [(i, (i + step) % TP) for i in range(TP)])  14.2 us
    unnamed x172, local copies, waits for them, and re-layouts  14.1 us
    all_to_all x1, waiting for transfers between devices, body(): parts = lax.all_to_all(tiles, 'tp', split_axis=0, concat_axis=0, tiled=True)  12.1 us
  transfers between devices with their start and end apart: 58, of which 24 were waited for; matrix products, arithmetic and copies ran while one was open for 14% of the time, Pallas kernels for 30%

profile of v1, /device:TPU:1, one launch (start us, length us, event | category | flops | bytes accessed | tf_op | source)
XLA Modules:
  0.0 507.3 jit_solution(9846160844646661237)
XLA Ops:
  7.9 2.8 shard_map.511
  11.5 2.5 collective-permute-start
  14.0 3.3 collective-permute-start.1
  19.2 9.0 %all-to-all-start = ((bf16[25,32,4,128]{3,2,0,1:T(4,128)(2,1)}), bf16[25,32,4,128]{3,2,0,1:T(4,128)(2,1)}, u32[]{:S(2)}, u32[]{:S(2)}) async-start(bf16[25,32,4,128]{3,2,0,1:T(4,128)(2,1)} %copy.96), calls=%async_computation | async-start | bytes 1638400 | tf_op jit(solution)/shard_map/all_to_all | solution.py:1043
  29.7 1.5 fusion.2
  31.2 2.5 reshape.576
  33.7 1.7 copy.94
  51.6 5.9 %fusion.16 = f32[2,32,10,190]{3,1,2,0:T(8,128)S(1)} fusion(f32[10,190,361,1]{2,1,0,3:T(8,128)} %constant.309, f32[2,8,361]{2,1,0:T(8,128)S(1)} %reshape.574, f32[2,8,361]{2,1,0:T(8,128)S(1)} %reshape.572, f32[2,8,361]{2,1,0:T(8,128)S(1)} %reshape.570, f32[2,8,361]{2,1,0:T(8,128)S(1)} %reshape.568), kind=kOutput, calls=%fused_computation.80 | convolution fusion | flops 526840512 | bytes 3322416 | tf_op jit(solution)/shard_map/dot_general | solution.py:936
  59.5 1.9 copy.93
  62.7 2.2 fusion.1
  64.9 1.6 reshape.579
  68.3 3.5 all-to-all-start.1
  72.5 12.1 %all-to-all-done.1.x_ref = bf16[4,200,512]{2,1,0:T(8,128)(2,1)S(1)} async-done(((bf16[4,200,512]{2,1,0:T(8,128)(2,1)}), bf16[4,200,512]{2,1,0:T(8,128)(2,1)S(1)}, u32[]{:S(2)}, u32[]{:S(2)}) %all-to-all-start.1) | async-done | bytes 819232 | tf_op jit(solution)/shard_map/all_to_all | solution.py:1045
  84.6 79.0 %all-gather.2.cloned.1.call-done = bf16[26624,1024]{1,0:T(8,128)(2,1)} async-done(((bf16[208,1024]{1,0:T(8,128)(2,1)}), bf16[26624,1024]{1,0:T(8,128)(2,1)}) %all-gather.2.cloned.1.call-update) | async-done | bytes 54525968 | tf_op jit(solution)/shard_map/all_gather | solution.py:1040
  163.5 7.4 %shard_map.512 = (f32[224,1024]{1,0:T(8,128)}, bf16[224,1024]{1,0:T(8,128)(2,1)}, bf16[224,1024]{1,0:T(8,128)(2,1)}) custom-call(s32[2]{0:T(128)} %get-tuple-element.471.core_ref.refs_0_, bf16[4,200,512]{2,1,0:T(8,128)(2,1)} %copy-done.1, bf16[200,224]{1,0:T(8,128)(2,1)} %constant.244.clone.pack_ref, f32[4,1,512]{2,1,0:T(1,128)} %reshape.584.gain_ref, ...), custom_call_target="tpu_custom_call" | custom-call | bytes 1024 | tf_op jit(solution)/shard_map/pallas_call | solution.py:117
  171.8 11.2 %shard_map.513 = (f32[224,1024]{1,0:T(8,128)}, bf16[224,1024]{1,0:T(8,128)(2,1)}, bf16[224,1024]{1,0:T(8,128)(2,1)}, bf16[224,1024]{1,0:T(8,128)(2,1)}, bf16[224...) custom-call(s32[2]{0:T(128)} %get-tuple-element.471.core_ref.refs_0_, ...), custom_call_target="tpu_custom_call" | custom-call | bytes 1024 | tf_op jit(solution)/shard_map/pallas_call | solution.py:117
  183.4 13.3 %shard_map.514 = (bf16[224,1024]{1,0:T(8,128)(2,1)}, bf16[224,4096]{1,0:T(8,128)(2,1)}, bf16[112,1024]{1,0:T(8,128)(2,1)}, bf16[224,2048]{1,0:T(8,128)(2,1)}, bf...) custom-call(s32[2]{0:T(128)} %get-tuple-element.471.core_ref.refs_0_, f32[224,1024]{1,0:T(8,128)} %get-tuple-element.166.mid_ref, ...), custom_call_target="tpu_custom_call" | custom-call | bytes 1024 | tf_op jit(solution)/shard_map/pallas_call | solution.py:117
  196.7 1.6 collective-permute-start.4
  198.9 5.0 collective-permute-done.4.refs_2_
  204.6 12.4 %shard_map.515 = (f32[224,1024]{1,0:T(8,128)}, bf16[224,1024]{1,0:T(8,128)(2,1)}, bf16[224,1024]{1,0:T(8,128)(2,1)}, bf16[224,1024]{1,0:T(8,128)(2,1)}, bf16[224...) custom-call(s32[2]{0:T(128)} %get-tuple-element.471.core_ref.refs_0_, ...), custom_call_target="tpu_custom_call" | custom-call | bytes 1024 | tf_op jit(solution)/shard_map/pallas_call | solution.py:117
  218.4 3.8 collective-permute-start.8
  223.0 20.8 %shard_map.516 = (bf16[224,1024]{1,0:T(8,128)(2,1)}, bf16[200,1024]{1,0:T(8,128)(2,1)}, bf16[224,1024]{1,0:T(8,128)(2,1)}, bf16[224,1024]{1,0:T(8,128)(2,1)}, bf...) custom-call(s32[2]{0:T(128)} %get-tuple-element.471.core_ref.refs_0_, ...), custom_call_target="tpu_custom_call" | custom-call | bytes 1024 | tf_op jit(solution)/shard_map/pallas_call | solution.py:117
  245.1 15.8 %shard_map.517 = (f32[224,1024]{1,0:T(8,128)}, bf16[224,1536]{1,0:T(8,128)(2,1)}, bf16[224,1536]{1,0:T(8,128)(2,1)}, f32[32,112,112]{2,1,0:T(8,128)}, f32[2,1024...) custom-call(s32[2]{0:T(128)} %get-tuple-element.471.core_ref.refs_0_, ...), custom_call_target="tpu_custom_call" | custom-call | bytes 1024 | tf_op jit(solution)/shard_map/pallas_call | solution.py:117
  261.6 2.2 collective-permute-done.14.refs_2_
  264.4 1.6 collective-permute-start.16
  266.9 11.1 %shard_map.518 = bf16[16,4,64,1024]{3,2,1,0:T(8,128)(2,1)} custom-call(s32[2]{0:T(128)} %get-tuple-element.471.core_ref.refs_0_, bf16[224,1024]{1,0:T(8,128)(2,1)} %get-tuple-element.193.refs_1_, bf16[224,1024]{1,0:T(8,128)(2,1)} %copy-done.31, bf16[224,2048]{1,0:T(8,128)(2,1)} %get-tuple-element.197.refs_3_, bf16[224,2048]{1,0:T(8,128)(2,1)} %copy-done.9, ...), custom_call_target="tpu_custom_call" | custom-call | bytes 1024 | tf_op jit(solution)/shard_map/pallas_call | solution.py:117
  279.8 2.1 collective-permute-start.19
  282.4 15.4 %shard_map.519 = (f32[224,1024]{1,0:T(8,128)}, bf16[224,1024]{1,0:T(8,128)(2,1)}, bf16[224,1024]{1,0:T(8,128)(2,1)}, f32[1,4096]{1,0:T(1,128)}, f32[4,1024]{1,0:...) custom-call(s32[2]{0:T(128)} %get-tuple-element.471.core_ref.refs_0_, ...), custom_call_target="tpu_custom_call" | custom-call | bytes 1024 | tf_op jit(solution)/shard_map/pallas_call | solution.py:117
  297.8 4.5 collective-permute-done.19.refs_6_
  303.9 3.1 collective-permute-start.24
  307.0 15.6 %shard_map.520 = (f32[224,1024]{1,0:T(8,128)}, bf16[224,1536]{1,0:T(8,128)(2,1)}, bf16[224,1536]{1,0:T(8,128)(2,1)}, f32[32,112,112]{2,1,0:T(8,128)}, f32[2,1024]{1,0:T(2,128)}, /*index=5*/f32[2,1024]{1,0:T(2,128)}) custom-call(s32[2]{0:T(128)} %get-tuple-element.471.core_ref.refs_0_, f32[224,1024]{1,0:T(8,128)} %get-tuple-element.210.refs_1_, ...), custom_call_target="tpu_custom_call" | custom-call | bytes 1024 | tf_op jit(solution)/shard_map/pallas_call | solution.py:117
  322.6 8.4 %shard_map.521 = (bf16[224,1024]{1,0:T(8,128)(2,1)}, bf16[4,200,512]{2,1,0:T(8,128)(2,1)}, f32[4,1,512]{2,1,0:T(1,128)}, f32[4,1,512]{2,1,0:T(1,128)}) custom-call(s32[2]{0:T(128)} %get-tuple-element.471.core_ref.refs_0_, bf16[4,200,512]{2,1,0:T(8,128)(2,1)} %copy-done.1, bf16[200,224]{1,0:T(8,128)(2,1)} %constant.244.clone.pack_ref, ...), custom_call_target="tpu_custom_call" | custom-call | bytes 1024 | tf_op jit(solution)/shard_map/pallas_call | solution.py:117
  331.0 6.8 %shard_map.522 = (bf16[1024,512]{1,0:T(8,128)(2,1)}, bf16[1024,512]{1,0:T(8,128)(2,1)}) custom-call(s32[2]{0:T(128)} %get-tuple-element.471.core_ref.refs_0_, bf16[224,1024]{1,0:T(8,128)(2,1)} %get-tuple-element.242.dx_ref.refs_0_, bf16[224,1024]{1,0:T(8,128)(2,1)} %get-tuple-element.243.refs_1_, bf16[224,1024]{1,0:T(8,128)(2,1)} %get-tuple-element.244.refs_2_, ...), custom_call_target="tpu_custom_call" | custom-call | bytes 1024 | tf_op jit(solution)/shard_map/pallas_call | solution.py:117
  338.9 6.9 %shard_map.523 = (bf16[1024,512]{1,0:T(8,128)(2,1)}, bf16[1024,512]{1,0:T(8,128)(2,1)}) custom-call(s32[2]{0:T(128)} %get-tuple-element.471.core_ref.refs_0_, bf16[224,1024]{1,0:T(8,128)(2,1)} %get-tuple-element.257.refs_0_, bf16[224,1024]{1,0:T(8,128)(2,1)} %copy-done.15, bf16[224,1024]{1,0:T(8,128)(2,1)} %copy-done.16, bf16[224,1024]{1,0:T(8,128)(2,1)} %copy-done.17, ...), custom_call_target="tpu_custom_call" | custom-call | bytes 1024 | tf_op jit(solution)/shard_map/pallas_call | solution.py:117
  348.2 4.2 collective-permute-done.22.refs_6_
  355.7 14.8 %shard_map.524 = bf16[16,4,64,1536]{3,2,1,0:T(8,128)(2,1)} custom-call(s32[2]{0:T(128)} %get-tuple-element.471.core_ref.refs_0_, bf16[224,1024]{1,0:T(8,128)(2,1)} %get-tuple-element.163.refs_1_, bf16[224,1024]{1,0:T(8,128)(2,1)} %collective-permute-done.5.refs_2_, bf16[224,1536]{1,0:T(8,128)(2,1)} %get-tuple-element.229.refs_3_, ...), custom_call_target="tpu_custom_call" | custom-call | bytes 1024 | tf_op jit(solution)/shard_map/pallas_call | solution.py:117
  370.5 4.4 all-to-all-start.2
  377.4 2.6 convolution_convert_fusion
  380.1 2.3 fusion.31
  384.6 2.6 convolution_convert_fusion.1
  387.8 1.5 concatenate.98
  390.2 1.6 copy.102
  393.3 6.3 %all-to-all-start.3 = ((bf16[800,1,4,128]{3,2,1,0:T(4,128)(2,1)}), bf16[800,1,4,128]{3,2,1,0:T(4,128)(2,1)S(1)}, u32[]{:S(2)}, u32[]{:S(2)}) async-start(bf16[800,1,4,128]{3,2,1,0:T(4,128)(2,1)} %bitcast.75), calls=%async_computation.3 | async-start | bytes 1638400 | tf_op jit(solution)/shard_map/all_to_all | solution.py:1188
  399.7 3.0 collective-permute-start.34
  402.9 2.4 collective-permute-start.36
  405.3 20.1 %collective-permute-done.34 = bf16[64,1024]{1,0:T(8,128)(2,1)S(1)} collective-permute-done((bf16[64,1024]{1,0:T(8,128)(2,1)S(1)}, bf16[64,1024]{1,0:T(8,128)(2,1)S(1)}, u32[]{:S(2)}, u32[]{:S(2)}) %collective-permute-start.34) | collective-permute-done | bytes 131104 | tf_op jit(solution)/shard_map/ppermute | solution.py:999
  425.4 1.6 collective-permute-done.35
  428.1 2.7 collective-permute-start.37
  430.9 2.0 collective-permute-start.30
  432.9 1.7 collective-permute-start.31
  434.6 1.4 collective-permute-start.32
  437.6 2.5 collective-permute-start.39
  440.2 1.6 copy.107
  441.8 3.0 collective-permute-done.38
  445.4 2.6 collective-permute-start.40
  448.3 2.4 collective-permute-start.42
  456.3 3.6 copy.106
  463.9 4.7 collective-permute-start.48
  470.2 4.3 collective-permute-done.48
  475.5 1.6 collective-permute-start.50
  478.1 3.8 reduce-scatter.7.cloned.1.call-done
  484.4 2.7 collective-permute-start.44
  489.4 4.6 collective-permute-done.44
  494.2 1.8 collective-permute-start.46
  (407 shorter events, 70.5 us)
Async XLA Ops:
  7.2 156.3 %all-gather.2.cloned.1.call-start = ((), (), s32[]{:S(2)}) async-start(), calls=%async_computation.6 | async-start | bytes 54951936 | tf_op jit(solution)/shard_map/all_gather | solution.py:1040
  11.5 38.6 %collective-permute-start = (f32[80,128]{1,0:T(8,128)}, f32[80,128]{1,0:T(8,128)}, u32[]{:S(2)}, u32[]{:S(2)}) collective-permute-start(f32[80,128]{1,0:T(8,128)} %bitcast.10), channel_id=1, source_target_pairs={{0,1},{1,2},{2,3},{3,0},{4,5},{5,6},{6,7},{7,4},{8,9},{9,10},{10,1... | collective-permute-start | bytes 122888 | tf_op jit(solution)/shard_map/ppermute | solution.py:979
  14.0 36.2 %collective-permute-start.1 = (f32[80,128]{1,0:T(8,128)}, f32[80,128]{1,0:T(8,128)}, u32[]{:S(2)}, u32[]{:S(2)}) collective-permute-start(f32[80,128]{1,0:T(8,128)} %bitcast.10), channel_id=1, source_target_pairs={{0,2},{1,3},{2,0},{3,1},{4,6},{5,7},{6,4},{7,5},{8,10},{9,11},{10,... | collective-permute-start | bytes 122888 | tf_op jit(solution)/shard_map/ppermute | solution.py:979
  17.3 32.9 %collective-permute-start.2 = (f32[80,128]{1,0:T(8,128)}, f32[80,128]{1,0:T(8,128)}, u32[]{:S(2)}, u32[]{:S(2)}) collective-permute-start(f32[80,128]{1,0:T(8,128)} %bitcast.10), channel_id=1, source_target_pairs={{0,3},{1,0},{2,1},{3,2},{4,7},{5,4},{6,5},{7,6},{8,11},{9,8},{10,9... | collective-permute-start | bytes 122888 | tf_op jit(solution)/shard_map/ppermute | solution.py:979
  19.2 45.6 %all-to-all-start = ((bf16[25,32,4,128]{3,2,0,1:T(4,128)(2,1)}), bf16[25,32,4,128]{3,2,0,1:T(4,128)(2,1)}, u32[]{:S(2)}, u32[]{:S(2)}) async-start(bf16[25,32,4,128]{3,2,0,1:T(4,128)(2,1)} %copy.96), calls=%async_computation | async-start | bytes 1638400 | tf_op jit(solution)/shard_map/all_to_all | solution.py:1043
  68.3 16.3 %all-to-all-start.1 = ((bf16[4,200,512]{2,1,0:T(8,128)(2,1)}), bf16[4,200,512]{2,1,0:T(8,128)(2,1)S(1)}, u32[]{:S(2)}, u32[]{:S(2)}) async-start(bf16[4,200,512]{2,1,0:T(8,128)(2,1)} %copy.98), calls=%async_computation.1 | async-start | bytes 1638400 | tf_op jit(solution)/shard_map/all_to_all | solution.py:1045
  71.8 390.6 %reduce-scatter.9.cloned.1.call-start = ((), (), s32[]{:S(2)}) async-start(), calls=%async_computation.8 | async-start | bytes 8912896
  84.6 79.0 %copy-start.1 = (bf16[4,200,512]{2,1,0:T(8,128)(2,1)}, bf16[4,200,512]{2,1,0:T(8,128)(2,1)S(1)}, u32[]{:S(2)}) copy-start(bf16[4,200,512]{2,1,0:T(8,128)(2,1)S(1)} %all-to-all-done.1.x_ref) | copy-start | bytes 2457604
  170.9 12.5 %collective-permute-start.3 = (bf16[224,1024]{1,0:T(8,128)(2,1)}, bf16[224,1024]{1,0:T(8,128)(2,1)S(1)}, u32[]{:S(2)}, u32[]{:S(2)}) collective-permute-start(bf16[224,1024]{1,0:T(8,128)(2,1)} %get-tuple-element.165), channel_id=1, source_target_pairs={{0,4},{4,0},{1,5},{5,1},{2,6},{6,2},{3,7},{7,3},{8,12},{12,8},{9,1... | collective-permute-start | bytes 1376264 | tf_op jit(solution)/shard_map/ppermute | solution.py:990
  183.1 39.1 %collective-permute-start.5 = (bf16[224,1024]{1,0:T(8,128)(2,1)}, bf16[224,1024]{1,0:T(8,128)(2,1)}, u32[]{:S(2)}, u32[]{:S(2)}) collective-permute-start(bf16[224,1024]{1,0:T(8,128)(2,1)} %get-tuple-element.163.refs_1_), channel_id=1, source_target_pairs={{0,4},{4,0},{1,5},{5,1},{2,6},{6,2},{3,7},{7,3},{8,12},{12,8},{9,1... | collective-permute-start | bytes 1376264 | tf_op jit(solution)/shard_map/ppermute | solution.py:990
  196.7 7.2 %collective-permute-start.4 = (bf16[112,1024]{1,0:T(8,128)(2,1)}, bf16[112,1024]{1,0:T(8,128)(2,1)S(1)}, u32[]{:S(2)}, u32[]{:S(2)}) collective-permute-start(bf16[112,1024]{1,0:T(8,128)(2,1)} %get-tuple-element.168), channel_id=1, source_target_pairs={{1,0},{2,1},{3,2},{0,3},{5,4},{6,5},{7,6},{4,7},{9,8},{10,9},{11,1... | collective-permute-start | bytes 688136 | tf_op jit(solution)/shard_map/ppermute | solution.py:1128
  198.3 20.1 %collective-permute-start.6 = (bf16[224,512]{1,0:T(8,128)(2,1)S(1)}, bf16[224,512]{1,0:T(8,128)(2,1)}, u32[]{:S(2)}, u32[]{:S(2)}) collective-permute-start(bf16[224,512]{1,0:T(8,128)(2,1)S(1)} %copy-done.69), channel_id=1, source_target_pairs={{0,4},{4,0},{1,5},{5,1},{2,6},{6,2},{3,7},{7,3},{8,12},{12,8},{9,1... | collective-permute-start | bytes 688136 | tf_op jit(solution)/shard_map/ppermute | solution.py:990
  217.0 26.8 %collective-permute-start.11 = (bf16[224,512]{1,0:T(8,128)(2,1)}, bf16[224,512]{1,0:T(8,128)(2,1)S(1)}, u32[]{:S(2)}, u32[]{:S(2)}) collective-permute-start(bf16[224,512]{1,0:T(8,128)(2,1)} %get-tuple-element.183), channel_id=1, source_target_pairs={{0,4},{4,0},{1,5},{5,1},{2,6},{6,2},{3,7},{7,3},{8,12},{12,8},{9,1... | collective-permute-start | bytes 688136 | tf_op jit(solution)/shard_map/ppermute | solution.py:990
  218.1 26.8 %collective-permute-start.10 = (bf16[224,1024]{1,0:T(8,128)(2,1)}, bf16[224,1024]{1,0:T(8,128)(2,1)S(1)}, u32[]{:S(2)}, u32[]{:S(2)}) collective-permute-start(bf16[224,1024]{1,0:T(8,128)(2,1)} %get-tuple-element.182.refs_5_), channel_id=1, source_target_pairs={{0,4},{4,0},{1,5},{5,1},{2,6},{6,2},{3,7},{7,3},{8,12},{12,8},{9,1... | collective-permute-start | bytes 1376264 | tf_op jit(solution)/shard_map/ppermute | solution.py:990
  218.2 26.7 %collective-permute-start.7 = (bf16[224,1024]{1,0:T(8,128)(2,1)S(1)}, bf16[224,1024]{1,0:T(8,128)(2,1)S(1)}, u32[]{:S(2)}, u32[]{:S(2)}) collective-permute-start(bf16[224,1024]{1,0:T(8,128)(2,1)S(1)} %copy-done.14), channel_id=1, source_target_pairs={{0,1},{1,2},{2,3},{3,0},{4,5},{5,6},{6,7},{7,4},{8,9},{9,10},{10,1... | collective-permute-start | bytes 1376264 | tf_op jit(solution)/shard_map/ppermute | solution.py:905
  218.4 26.6 %collective-permute-start.8 = (bf16[224,1024]{1,0:T(8,128)(2,1)S(1)}, bf16[224,1024]{1,0:T(8,128)(2,1)S(1)}, u32[]{:S(2)}, u32[]{:S(2)}) collective-permute-start(bf16[224,1024]{1,0:T(8,128)(2,1)S(1)} %copy-done.14), channel_id=1, source_target_pairs={{0,2},{1,3},{2,0},{3,1},{4,6},{5,7},{6,4},{7,5},{8,10},{9,11},{10,... | collective-permute-start | bytes 1376264 | tf_op jit(solution)/shard_map/ppermute | solution.py:905
  222.2 22.8 %collective-permute-start.9 = (bf16[224,1024]{1,0:T(8,128)(2,1)S(1)}, bf16[224,1024]{1,0:T(8,128)(2,1)S(1)}, u32[]{:S(2)}, u32[]{:S(2)}) collective-permute-start(bf16[224,1024]{1,0:T(8,128)(2,1)S(1)} %copy-done.14), channel_id=1, source_target_pairs={{0,3},{1,0},{2,1},{3,2},{4,7},{5,4},{6,5},{7,6},{8,11},{9,8},{10,9... | collective-permute-start | bytes 1376264 | tf_op jit(solution)/shard_map/ppermute | solution.py:905
  243.8 20.6 %collective-permute-start.12 = (bf16[224,2048]{1,0:T(8,128)(2,1)}, bf16[224,2048]{1,0:T(8,128)(2,1)S(1)}, u32[]{:S(2)}, u32[]{:S(2)}) collective-permute-start(bf16[224,2048]{1,0:T(8,128)(2,1)} %get-tuple-element.195), channel_id=1, source_target_pairs={{0,4},{4,0},{1,5},{5,1},{2,6},{6,2},{3,7},{7,3},{8,12},{12,8},{9,1... | collective-permute-start | bytes 2752520 | tf_op jit(solution)/shard_map/ppermute | solution.py:990
  260.9 5.2 %collective-permute-start.15 = (bf16[224,1536]{1,0:T(8,128)(2,1)}, bf16[224,1536]{1,0:T(8,128)(2,1)S(1)}, u32[]{:S(2)}, u32[]{:S(2)}) collective-permute-start(bf16[224,1536]{1,0:T(8,128)(2,1)} %get-tuple-element.201), channel_id=1, source_target_pairs={{0,4},{4,0},{1,5},{5,1},{2,6},{6,2},{3,7},{7,3},{8,12},{12,8},{9,1... | collective-permute-start | bytes 2064392 | tf_op jit(solution)/shard_map/ppermute | solution.py:990
  261.0 2.8 collective-permute-start.14
  261.5 2.9 collective-permute-start.13
  264.4 13.6 %collective-permute-start.16 = (bf16[112,1024]{1,0:T(8,128)(2,1)}, bf16[112,1024]{1,0:T(8,128)(2,1)S(1)}, u32[]{:S(2)}, u32[]{:S(2)}) collective-permute-start(bf16[112,1024]{1,0:T(8,128)(2,1)} %get-tuple-element.205), channel_id=1, source_target_pairs={{0,1},{1,2},{2,3},{3,0},{4,5},{5,6},{6,7},{7,4},{8,9},{9,10},{10,1... | collective-permute-start | bytes 688136 | tf_op jit(solution)/shard_map/ppermute | solution.py:1138
  278.8 203.1 %reduce-scatter.7.cloned.1.call-start = ((), (), s32[]{:S(2)}) async-start(), calls=%async_computation.7 | async-start | bytes 13369344
  279.3 23.8 %collective-permute-start.17 = (bf16[224,2048]{1,0:T(8,128)(2,1)S(1)}, bf16[224,2048]{1,0:T(8,128)(2,1)S(1)}, u32[]{:S(2)}, u32[]{:S(2)}) collective-permute-start(bf16[224,2048]{1,0:T(8,128)(2,1)S(1)} %copy-done.65), channel_id=1, source_target_pairs={{0,4},{4,0},{1,5},{5,1},{2,6},{6,2},{3,7},{7,3},{8,12},{12,8},{9,1... | collective-permute-start | bytes 2752520 | tf_op jit(solution)/shard_map/ppermute | solution.py:990
  279.6 18.1 %collective-permute-start.18 = (bf16[224,1024]{1,0:T(8,128)(2,1)S(1)}, bf16[224,1024]{1,0:T(8,128)(2,1)S(1)}, u32[]{:S(2)}, u32[]{:S(2)}) collective-permute-start(bf16[224,1024]{1,0:T(8,128)(2,1)S(1)} %copy-done.68), channel_id=1, source_target_pairs={{0,1},{1,2},{2,3},{3,0},{4,5},{5,6},{6,7},{7,4},{8,9},{9,10},{10,1... | collective-permute-start | bytes 1376264 | tf_op jit(solution)/shard_map/ppermute | solution.py:905
  279.8 22.5 %collective-permute-start.19 = (bf16[224,1024]{1,0:T(8,128)(2,1)S(1)}, bf16[224,1024]{1,0:T(8,128)(2,1)S(1)}, u32[]{:S(2)}, u32[]{:S(2)}) collective-permute-start(bf16[224,1024]{1,0:T(8,128)(2,1)S(1)} %copy-done.67), channel_id=1, source_target_pairs={{0,2},{1,3},{2,0},{3,1},{4,6},{5,7},{6,4},{7,5},{8,10},{9,11},{10,... | collective-permute-start | bytes 1376264 | tf_op jit(solution)/shard_map/ppermute | solution.py:905
  281.9 21.1 %collective-permute-start.20 = (bf16[224,1024]{1,0:T(8,128)(2,1)S(1)}, bf16[224,1024]{1,0:T(8,128)(2,1)S(1)}, u32[]{:S(2)}, u32[]{:S(2)}) collective-permute-start(bf16[224,1024]{1,0:T(8,128)(2,1)S(1)} %copy-done.66), channel_id=1, source_target_pairs={{0,3},{1,0},{2,1},{3,2},{4,7},{5,4},{6,5},{7,6},{8,11},{9,8},{10,9... | collective-permute-start | bytes 1376264 | tf_op jit(solution)/shard_map/ppermute | solution.py:905
  297.8 24.8 %copy-start.22 = (bf16[224,1024]{1,0:T(8,128)(2,1)}, bf16[224,1024]{1,0:T(8,128)(2,1)S(1)}, u32[]{:S(2)}) copy-start(bf16[224,1024]{1,0:T(8,128)(2,1)S(1)} %collective-permute-done.18.refs_5_) | copy-start | bytes 1376260
  302.3 20.3 %copy-start.23 = (bf16[224,1024]{1,0:T(8,128)(2,1)}, bf16[224,1024]{1,0:T(8,128)(2,1)S(1)}, u32[]{:S(2)}) copy-start(bf16[224,1024]{1,0:T(8,128)(2,1)S(1)} %collective-permute-done.19.refs_6_) | copy-start | bytes 1376260
  303.1 19.6 %copy-start.24 = (bf16[224,1024]{1,0:T(8,128)(2,1)}, bf16[224,1024]{1,0:T(8,128)(2,1)S(1)}, u32[]{:S(2)}) copy-start(bf16[224,1024]{1,0:T(8,128)(2,1)S(1)} %collective-permute-done.20.refs_7_) | copy-start | bytes 1376260
  303.1 19.6 %copy-start.8 = (bf16[224,2048]{1,0:T(8,128)(2,1)}, bf16[224,2048]{1,0:T(8,128)(2,1)S(1)}, u32[]{:S(2)}) copy-start(bf16[224,2048]{1,0:T(8,128)(2,1)S(1)} %collective-permute-done.17.refs_16_) | copy-start | bytes 2752516
  303.1 34.8 %collective-permute-start.23 = (bf16[224,1024]{1,0:T(8,128)(2,1)}, bf16[224,1024]{1,0:T(8,128)(2,1)S(1)}, u32[]{:S(2)}, u32[]{:S(2)}) collective-permute-start(bf16[224,1024]{1,0:T(8,128)(2,1)} %get-tuple-element.238), channel_id=1, source_target_pairs={{0,1},{1,2},{2,3},{3,0},{4,5},{5,6},{6,7},{7,4},{8,9},{9,10},{10,1... | collective-permute-start | bytes 1376264 | tf_op jit(solution)/shard_map/ppermute | solution.py:905
  303.9 34.0 %collective-permute-start.24 = (bf16[224,1024]{1,0:T(8,128)(2,1)}, bf16[224,1024]{1,0:T(8,128)(2,1)S(1)}, u32[]{:S(2)}, u32[]{:S(2)}) collective-permute-start(bf16[224,1024]{1,0:T(8,128)(2,1)} %get-tuple-element.239), channel_id=1, source_target_pairs={{0,2},{1,3},{2,0},{3,1},{4,6},{5,7},{6,4},{7,5},{8,10},{9,11},{10,... | collective-permute-start | bytes 1376264 | tf_op jit(solution)/shard_map/ppermute | solution.py:905
  307.0 30.8 %collective-permute-start.25 = (bf16[224,1024]{1,0:T(8,128)(2,1)}, bf16[224,1024]{1,0:T(8,128)(2,1)S(1)}, u32[]{:S(2)}, u32[]{:S(2)}) collective-permute-start(bf16[224,1024]{1,0:T(8,128)(2,1)} %get-tuple-element.240), channel_id=1, source_target_pairs={{0,3},{1,0},{2,1},{3,2},{4,7},{5,4},{6,5},{7,6},{8,11},{9,8},{10,9... | collective-permute-start | bytes 1376264 | tf_op jit(solution)/shard_map/ppermute | solution.py:905
  345.9 8.4 %collective-permute-start.28 = (bf16[1024,512]{1,0:T(8,128)(2,1)}, bf16[1024,512]{1,0:T(8,128)(2,1)S(1)}, u32[]{:S(2)}, u32[]{:S(2)}) collective-permute-start(bf16[1024,512]{1,0:T(8,128)(2,1)} %get-tuple-element.266), channel_id=1, source_target_pairs={{0,4},{4,0},{1,5},{5,1},{2,6},{6,2},{3,7},{7,3},{8,12},{12,8},{9,1... | collective-permute-start | bytes 3145736 | tf_op jit(solution)/shard_map/ppermute | solution.py:990
  347.0 7.3 %collective-permute-start.29 = (bf16[1024,512]{1,0:T(8,128)(2,1)S(1)}, bf16[1024,512]{1,0:T(8,128)(2,1)S(1)}, u32[]{:S(2)}, u32[]{:S(2)}) collective-permute-start(bf16[1024,512]{1,0:T(8,128)(2,1)S(1)} %copy-done.64), channel_id=1, source_target_pairs={{0,4},{4,0},{1,5},{5,1},{2,6},{6,2},{3,7},{7,3},{8,12},{12,8},{9,1... | collective-permute-start | bytes 3145736 | tf_op jit(solution)/shard_map/ppermute | solution.py:990
  347.1 5.3 %collective-permute-start.22 = (bf16[224,1024]{1,0:T(8,128)(2,1)S(1)}, bf16[224,1024]{1,0:T(8,128)(2,1)S(1)}, u32[]{:S(2)}, u32[]{:S(2)}) collective-permute-start(bf16[224,1024]{1,0:T(8,128)(2,1)S(1)} %copy-done.3), channel_id=1, source_target_pairs={{0,4},{4,0},{1,5},{5,1},{2,6},{6,2},{3,7},{7,3},{8,12},{12,8},{9,1... | collective-permute-start | bytes 1376264 | tf_op jit(solution)/shard_map/ppermute | solution.py:990
  347.5 5.3 %collective-permute-start.21 = (bf16[224,1536]{1,0:T(8,128)(2,1)}, bf16[224,1536]{1,0:T(8,128)(2,1)S(1)}, u32[]{:S(2)}, u32[]{:S(2)}) collective-permute-start(bf16[224,1536]{1,0:T(8,128)(2,1)} %get-tuple-element.230), channel_id=1, source_target_pairs={{0,4},{4,0},{1,5},{5,1},{2,6},{6,2},{3,7},{7,3},{8,12},{12,8},{9,1... | collective-permute-start | bytes 2064392 | tf_op jit(solution)/shard_map/ppermute | solution.py:990
  347.6 5.5 %collective-permute-start.26 = (bf16[224,1024]{1,0:T(8,128)(2,1)S(1)}, bf16[224,1024]{1,0:T(8,128)(2,1)S(1)}, u32[]{:S(2)}, u32[]{:S(2)}) collective-permute-start(bf16[224,1024]{1,0:T(8,128)(2,1)S(1)} %copy-done.20), channel_id=1, source_target_pairs={{0,4},{4,0},{1,5},{5,1},{2,6},{6,2},{3,7},{7,3},{8,12},{12,8},{9,1... | collective-permute-start | bytes 1376264 | tf_op jit(solution)/shard_map/ppermute | solution.py:990
  352.4 1.8 collective-permute-start.27
  370.5 19.7 %all-to-all-start.2 = ((bf16[4,200,512]{2,1,0:T(8,128)(2,1)}), bf16[4,200,512]{2,1,0:T(8,128)(2,1)}, u32[]{:S(2)}, u32[]{:S(2)}) async-start(bf16[4,200,512]{2,1,0:T(8,128)(2,1)} %get-tuple-element.283), calls=%async_computation.2 | async-start | bytes 1638400 | tf_op jit(solution)/shard_map/all_to_all | solution.py:1184
  389.4 10.3 %collective-permute-start.33 = (bf16[64,1024]{1,0:T(8,128)(2,1)S(1)}, bf16[64,1024]{1,0:T(8,128)(2,1)S(1)}, u32[]{:S(2)}, u32[]{:S(2)}) collective-permute-start(bf16[64,1024]{1,0:T(8,128)(2,1)S(1)} %convert_element_type.193), channel_id=1, source_target_pairs={{0,4},{4,0},{1,5},{5,1},{2,6},{6,2},{3,7},{7,3},{8,12},{12,8},{9,1... | collective-permute-start | bytes 393224 | tf_op jit(solution)/shard_map/ppermute | solution.py:990
  392.1 38.7 %copy-start.33 = (bf16[200,1024]{1,0:T(8,128)(2,1)S(1)}, bf16[200,1024]{1,0:T(8,128)(2,1)}, u32[]{:S(2)}) copy-start(bf16[200,1024]{1,0:T(8,128)(2,1)} %get-tuple-element.282) | copy-start | bytes 1228804
  393.3 46.7 %all-to-all-start.3 = ((bf16[800,1,4,128]{3,2,1,0:T(4,128)(2,1)}), bf16[800,1,4,128]{3,2,1,0:T(4,128)(2,1)S(1)}, u32[]{:S(2)}, u32[]{:S(2)}) async-start(bf16[800,1,4,128]{3,2,1,0:T(4,128)(2,1)} %bitcast.75), calls=%async_computation.3 | async-start | bytes 1638400 | tf_op jit(solution)/shard_map/all_to_all | solution.py:1188
  399.7 25.7 %collective-permute-start.34 = (bf16[64,1024]{1,0:T(8,128)(2,1)S(1)}, bf16[64,1024]{1,0:T(8,128)(2,1)S(1)}, u32[]{:S(2)}, u32[]{:S(2)}) collective-permute-start(bf16[64,1024]{1,0:T(8,128)(2,1)S(1)} %add_convert_fusion.2), channel_id=1, source_target_pairs={{0,16},{8,24},{16,0},{24,8},{1,17},{9,25},{17,1},{25,9},{2,18},{10... | collective-permute-start | bytes 393224 | tf_op jit(solution)/shard_map/ppermute | solution.py:999
  402.7 24.4 %collective-permute-start.35 = (bf16[64,1024]{1,0:T(8,128)(2,1)S(1)}, bf16[64,1024]{1,0:T(8,128)(2,1)S(1)}, u32[]{:S(2)}, u32[]{:S(2)}) collective-permute-start(bf16[64,1024]{1,0:T(8,128)(2,1)S(1)} %add_convert_fusion.2), channel_id=1, source_target_pairs={{0,8},{8,16},{16,24},{24,0},{1,9},{9,17},{17,25},{25,1},{2,10},{10... | collective-permute-start | bytes 393224 | tf_op jit(solution)/shard_map/ppermute | solution.py:999
  402.9 25.1 %collective-permute-start.36 = (bf16[64,1024]{1,0:T(8,128)(2,1)S(1)}, bf16[64,1024]{1,0:T(8,128)(2,1)S(1)}, u32[]{:S(2)}, u32[]{:S(2)}) collective-permute-start(bf16[64,1024]{1,0:T(8,128)(2,1)S(1)} %add_convert_fusion.2), channel_id=1, source_target_pairs={{0,24},{8,0},{16,8},{24,16},{1,25},{9,1},{17,9},{25,17},{2,26},{10... | collective-permute-start | bytes 393224 | tf_op jit(solution)/shard_map/ppermute | solution.py:999
  428.1 9.4 %collective-permute-start.37 = (bf16[64,1024]{1,0:T(8,128)(2,1)S(1)}, bf16[64,1024]{1,0:T(8,128)(2,1)S(1)}, u32[]{:S(2)}, u32[]{:S(2)}) collective-permute-start(bf16[64,1024]{1,0:T(8,128)(2,1)S(1)} %add_convert_fusion.1), channel_id=1, source_target_pairs={{0,64},{32,96},{64,0},{96,32},{1,65},{33,97},{65,1},{97,33},{2,66}... | collective-permute-start | bytes 393224 | tf_op jit(solution)/shard_map/ppermute | solution.py:999
  430.9 17.4 %collective-permute-start.30 = (bf16[200,1024]{1,0:T(8,128)(2,1)S(1)}, bf16[200,1024]{1,0:T(8,128)(2,1)S(1)}, u32[]{:S(2)}, u32[]{:S(2)}) collective-permute-start(bf16[200,1024]{1,0:T(8,128)(2,1)S(1)} %copy-done.33), channel_id=1, source_target_pairs={{0,1},{1,2},{2,3},{3,0},{4,5},{5,6},{6,7},{7,4},{8,9},{9,10},{10,1... | collective-permute-start | bytes 1228808 | tf_op jit(solution)/shard_map/ppermute | solution.py:979
  432.9 18.8 %collective-permute-start.31 = (bf16[200,1024]{1,0:T(8,128)(2,1)S(1)}, bf16[200,1024]{1,0:T(8,128)(2,1)S(1)}, u32[]{:S(2)}, u32[]{:S(2)}) collective-permute-start(bf16[200,1024]{1,0:T(8,128)(2,1)S(1)} %copy-done.33), channel_id=1, source_target_pairs={{0,2},{1,3},{2,0},{3,1},{4,6},{5,7},{6,4},{7,5},{8,10},{9,11},{10,... | collective-permute-start | bytes 1228808 | tf_op jit(solution)/shard_map/ppermute | solution.py:979
  434.6 18.4 %collective-permute-start.32 = (bf16[200,1024]{1,0:T(8,128)(2,1)S(1)}, bf16[200,1024]{1,0:T(8,128)(2,1)S(1)}, u32[]{:S(2)}, u32[]{:S(2)}) collective-permute-start(bf16[200,1024]{1,0:T(8,128)(2,1)S(1)} %copy-done.33), channel_id=1, source_target_pairs={{0,3},{1,0},{2,1},{3,2},{4,7},{5,4},{6,5},{7,6},{8,11},{9,8},{10,9... | collective-permute-start | bytes 1228808 | tf_op jit(solution)/shard_map/ppermute | solution.py:979
  436.1 8.8 %collective-permute-start.38 = (bf16[64,1024]{1,0:T(8,128)(2,1)S(1)}, bf16[64,1024]{1,0:T(8,128)(2,1)S(1)}, u32[]{:S(2)}, u32[]{:S(2)}) collective-permute-start(bf16[64,1024]{1,0:T(8,128)(2,1)S(1)} %add_convert_fusion.1), channel_id=1, source_target_pairs={{0,32},{32,64},{64,96},{96,0},{1,33},{33,65},{65,97},{97,1},{2,34}... | collective-permute-start | bytes 393224 | tf_op jit(solution)/shard_map/ppermute | solution.py:999
  437.6 7.7 %collective-permute-start.39 = (bf16[64,1024]{1,0:T(8,128)(2,1)S(1)}, bf16[64,1024]{1,0:T(8,128)(2,1)S(1)}, u32[]{:S(2)}, u32[]{:S(2)}) collective-permute-start(bf16[64,1024]{1,0:T(8,128)(2,1)S(1)} %add_convert_fusion.1), channel_id=1, source_target_pairs={{0,96},{32,0},{64,32},{96,64},{1,97},{33,1},{65,33},{97,65},{2,98}... | collective-permute-start | bytes 393224 | tf_op jit(solution)/shard_map/ppermute | solution.py:999
  445.4 14.5 %collective-permute-start.40 = (bf16[64,1024]{1,0:T(8,128)(2,1)S(1)}, bf16[64,1024]{1,0:T(8,128)(2,1)S(1)}, u32[]{:S(2)}, u32[]{:S(2)}) collective-permute-start(bf16[64,1024]{1,0:T(8,128)(2,1)S(1)} %add_convert_fusion), channel_id=1, source_target_pairs={{0,2},{1,3},{2,0},{3,1},{4,6},{5,7},{6,4},{7,5},{8,10},{9,11},{10,... | collective-permute-start | bytes 393224 | tf_op jit(solution)/shard_map/ppermute | solution.py:999
  448.0 11.9 %collective-permute-start.41 = (bf16[64,1024]{1,0:T(8,128)(2,1)S(1)}, bf16[64,1024]{1,0:T(8,128)(2,1)S(1)}, u32[]{:S(2)}, u32[]{:S(2)}) collective-permute-start(bf16[64,1024]{1,0:T(8,128)(2,1)S(1)} %add_convert_fusion), channel_id=1, source_target_pairs={{0,1},{1,2},{2,3},{3,0},{4,5},{5,6},{6,7},{7,4},{8,9},{9,10},{10,1... | collective-permute-start | bytes 393224 | tf_op jit(solution)/shard_map/ppermute | solution.py:999
  448.3 11.6 %collective-permute-start.42 = (bf16[64,1024]{1,0:T(8,128)(2,1)S(1)}, bf16[64,1024]{1,0:T(8,128)(2,1)S(1)}, u32[]{:S(2)}, u32[]{:S(2)}) collective-permute-start(bf16[64,1024]{1,0:T(8,128)(2,1)S(1)} %add_convert_fusion), channel_id=1, source_target_pairs={{0,3},{1,0},{2,1},{3,2},{4,7},{5,4},{6,5},{7,6},{8,11},{9,8},{10,9... | collective-permute-start | bytes 393224 | tf_op jit(solution)/shard_map/ppermute | solution.py:999
  463.5 6.8 %collective-permute-start.47 = (bf16[64,1024]{1,0:T(8,128)(2,1)S(1)}, bf16[64,1024]{1,0:T(8,128)(2,1)S(1)}, u32[]{:S(2)}, u32[]{:S(2)}) collective-permute-start(bf16[64,1024]{1,0:T(8,128)(2,1)S(1)} %get-tuple-element.389), channel_id=1, source_target_pairs={{0,1},{1,2},{2,3},{3,0},{4,5},{5,6},{6,7},{7,4},{8,9},{9,10},{10,1... | collective-permute-start | bytes 393224 | tf_op jit(solution)/shard_map/ppermute | solution.py:905
  463.9 10.6 %collective-permute-start.48 = (bf16[64,1024]{1,0:T(8,128)(2,1)S(1)}, bf16[64,1024]{1,0:T(8,128)(2,1)S(1)}, u32[]{:S(2)}, u32[]{:S(2)}) collective-permute-start(bf16[64,1024]{1,0:T(8,128)(2,1)S(1)} %get-tuple-element.391), channel_id=1, source_target_pairs={{0,2},{1,3},{2,0},{3,1},{4,6},{5,7},{6,4},{7,5},{8,10},{9,11},{10,... | collective-permute-start | bytes 393224 | tf_op jit(solution)/shard_map/ppermute | solution.py:905
  468.7 5.8 %collective-permute-start.49 = (bf16[64,1024]{1,0:T(8,128)(2,1)S(1)}, bf16[64,1024]{1,0:T(8,128)(2,1)S(1)}, u32[]{:S(2)}, u32[]{:S(2)}) collective-permute-start(bf16[64,1024]{1,0:T(8,128)(2,1)S(1)} %get-tuple-element.390), channel_id=1, source_target_pairs={{0,3},{1,0},{2,1},{3,2},{4,7},{5,4},{6,5},{7,6},{8,11},{9,8},{10,9... | collective-permute-start | bytes 393224 | tf_op jit(solution)/shard_map/ppermute | solution.py:905
  475.5 2.5 collective-permute-start.50
  483.1 6.3 %collective-permute-start.43 = (bf16[64,1280]{1,0:T(8,128)(2,1)S(1)}, bf16[64,1280]{1,0:T(8,128)(2,1)S(1)}, u32[]{:S(2)}, u32[]{:S(2)}) collective-permute-start(bf16[64,1280]{1,0:T(8,128)(2,1)S(1)} %get-tuple-element.386), channel_id=1, source_target_pairs={{0,1},{1,2},{2,3},{3,0},{4,5},{5,6},{6,7},{7,4},{8,9},{9,10},{10,1... | collective-permute-start | bytes 491528 | tf_op jit(solution)/shard_map/ppermute | solution.py:905
  484.4 9.6 %collective-permute-start.44 = (bf16[64,1280]{1,0:T(8,128)(2,1)S(1)}, bf16[64,1280]{1,0:T(8,128)(2,1)S(1)}, u32[]{:S(2)}, u32[]{:S(2)}) collective-permute-start(bf16[64,1280]{1,0:T(8,128)(2,1)S(1)} %get-tuple-element.388), channel_id=1, source_target_pairs={{0,2},{1,3},{2,0},{3,1},{4,6},{5,7},{6,4},{7,5},{8,10},{9,11},{10,... | collective-permute-start | bytes 491528 | tf_op jit(solution)/shard_map/ppermute | solution.py:905
  487.1 6.9 %collective-permute-start.45 = (bf16[64,1280]{1,0:T(8,128)(2,1)S(1)}, bf16[64,1280]{1,0:T(8,128)(2,1)S(1)}, u32[]{:S(2)}, u32[]{:S(2)}) collective-permute-start(bf16[64,1280]{1,0:T(8,128)(2,1)S(1)} %get-tuple-element.387), channel_id=1, source_target_pairs={{0,3},{1,0},{2,1},{3,2},{4,7},{5,4},{6,5},{7,6},{8,11},{9,8},{10,9... | collective-permute-start | bytes 491528 | tf_op jit(solution)/shard_map/ppermute | solution.py:905
  494.2 2.8 collective-permute-start.46
  (64 other events, 354.0 us)
Sparse Core Ops, SparseCore 0:
  11.0 152.4 all-gather.1
  278.2 81.5 reduce-scatter.8
  370.6 111.2 reduce-scatter.6

commit v2 on v1

--- a/solution.py
+++ b/solution.py
@@ -1134,7 +1134,7 @@
     sums = [None, None]
     got = attn_backward(core, 1, dmid, dattn, start, ln1_gain[1:2], weights, q, k, v, probs)
     grad, mixed_mine, mixed_other, pairs, dqv, rows_one, sent = got
-    sent, (dpre_got, dattn_got, c2_got) = after(sent, (dpre_got, dattn_got, c2_got))
+    sent, (dpre_got, dattn_got, acts) = after(sent, (dpre_got, dattn_got, acts))
     halo = lax.ppermute(sent, "tp", [(i, (i + 1) % TP) for i in range(TP)])
     mixed_got = swap_core(mixed_other)
     sums[1] = (db1, rows_two, dqv, rows_one, pairs)
@@ -1153,7 +1153,7 @@
     act_got = swap_core(act_other)
     got = mlp_backward(core, grad, halo, mid, ln2_gain[0:1], weights, slope)
     dmid, dmlp, dattn, db1, rows_two = got[:5]
-    dattn, (dpre, act_got, acts, tiles) = after(dattn, (list(got[5:]), act_got, acts, tiles))
+    dattn, (dpre, act_got) = after(dattn, (list(got[5:]), act_got))
     dpre = send_ahead(dpre)
     got = attn_backward(core, 0, dmid, dattn, start, ln1_gain[0:1], weights, q, k, v, probs)
     grad, mixed_mine, mixed_other, pairs, dqv, rows_one = got
@@ -1161,10 +1161,14 @@
     grad, dattn_sent = lax.optimization_barrier((grad, dattn))
     mixed_got, dattn_got = [swap_core(value) for value in (mixed_other, dattn_sent)]
     first, dm, dgain, dbias = merge_backward(core, parts, merge_gain_all, weights, grad)
+    first, (dpre, tiles, acts) = after(first, (dpre, tiles, acts))
+    first_got, dmlp_got = swap_core(first), swap_core(dmlp)
     last_other, last_mine = column_grads(core, tiles, acts)
-    first, (dpre, dmlp_sent, last_other) = after(first, (dpre, dmlp, last_other))
-    first_got, dmlp_got = swap_core(first), swap_core(dmlp_sent)
+    last_got = swap_core(last_other)
     up_other, up_mine = column_grads(core, c2_all, dpre)
+    up_mine, (first_got, dmlp_got, last_got, mixed_got, dattn_got) = after(
+        up_mine, (first_got, dmlp_got, last_got, mixed_got, dattn_got)
+    )
     items = [
         ((a, a_zero), (mixed_mine, mixed_got)),
         ((dattn, dattn_got), (heads_mine, heads_zero)),
@@ -1172,7 +1176,7 @@
         ((dmlp, dmlp_got), (act_mine, act_got)),
     ]
     early = weight_grads(
-        core, items, [[up_mine, swap_core(up_other)], [last_mine, swap_core(last_other)]]
+        core, items, [[up_mine, swap_core(up_other)], [last_mine, last_got]]
     )
     early, (extra, sums, dgain, dbias) = after(early, (extra, sums, dgain, dbias))
     early = lax.psum_scatter(early, CHIP_AXES, scatter_dimension=0, tiled=True)

time: 511 us -> 514 us (level)
    unnamed x5, waiting for transfers between devices: 3.88 us -> 10.3 us
    ppermute x15, waiting for transfers between devices: 14.2 us -> 8.8 us  [send_ahead(): lax.ppermute(pieces[step], 'tp', [(i, (i + step) % TP) for i in range(TP)])]
    unnamed x172 -> x170, local copies, waits for them, and re-layouts: 14.1 us -> 14.1 us
  transfers between devices with their start and end apart: 58 -> 58, of which waited for: 24 -> 21; matrix products, arithmetic and copies ran while one was open for 14% -> 13% of each run, Pallas kernels for 30% -> 27%
where the time goes in v2:
time: 514 us; the launch traced here: 510 us
  Pallas kernels  163 us (32%)
  waiting for transfers between devices  153 us (30%)
  starting transfers between devices  90 us (18%)
  local copies, waits for them, and re-layouts  52.4 us (10%)
  between operations  24.1 us (5%)
  other arithmetic  16.4 us (3%)
  matrix products  11.2 us (2%)
    pallas_call x13, Pallas kernels, run(): pl.pallas_call(kernel, grid_spec=pltpu.PrefetchScalarGridSpec(num_scalar_...  160 us
    all_gather x1, waiting for transfers between devices, body(): lax.all_gather(piece.reshape(-1, D), GATHER_AXES, axis=0, tiled=True)  79 us
    ppermute x9, waiting for transfers between devices, sum_all(): lax.ppermute(sent, axis, [(i, (i + gap) % 4) for i in range(4)]).astype(F32)  28.6 us
    ppermute x15, starting transfers between devices, send_ahead(): lax.ppermute(pieces[step], 'tp', [(i, (i + step) % TP) for i in range(TP)])  23 us
    ppermute x9, starting transfers between devices, sum_all(): lax.ppermute(sent, axis, [(i, (i + gap) % 4) for i in range(4)]).astype(F32)  16.4 us
    unnamed x170, local copies, waits for them, and re-layouts  14.1 us
    ppermute x19, starting transfers between devices, swap_core(): return lax.ppermute(value, 'core', [(0, 1), (1, 0)])  14 us
    all_to_all x1, waiting for transfers between devices, body(): parts = lax.all_to_all(tiles, 'tp', split_axis=0, concat_axis=0, tiled=True)  12.1 us
  transfers between devices with their start and end apart: 58, of which 21 were waited for; matrix products, arithmetic and copies ran while one was open for 13% of the time, Pallas kernels for 27%

profile of v2, /device:TPU:1, one launch (start us, length us, event | category | flops | bytes accessed | tf_op | source)
XLA Modules:
  0.0 509.8 jit_solution(8480255436865637377)
XLA Ops:
  7.9 2.8 shard_map.511
  11.5 2.5 collective-permute-start
  14.0 3.3 collective-permute-start.1
  19.2 9.0 %all-to-all-start = ((bf16[25,32,4,128]{3,2,0,1:T(4,128)(2,1)}), bf16[25,32,4,128]{3,2,0,1:T(4,128)(2,1)}, u32[]{:S(2)}, u32[]{:S(2)}) async-start(bf16[25,32,4,128]{3,2,0,1:T(4,128)(2,1)} %copy.96), calls=%async_computation | async-start | bytes 1638400 | tf_op jit(solution)/shard_map/all_to_all | solution.py:1043
  29.7 1.5 fusion.2
  31.2 2.5 reshape.576
  33.7 1.7 copy.94
  51.7 5.9 %fusion.16 = f32[2,32,10,190]{3,1,2,0:T(8,128)S(1)} fusion(f32[10,190,361,1]{2,1,0,3:T(8,128)} %constant.309, f32[2,8,361]{2,1,0:T(8,128)S(1)} %reshape.574, f32[2,8,361]{2,1,0:T(8,128)S(1)} %reshape.572, f32[2,8,361]{2,1,0:T(8,128)S(1)} %reshape.570, f32[2,8,361]{2,1,0:T(8,128)S(1)} %reshape.568), kind=kOutput, calls=%fused_computation.80 | convolution fusion | flops 526840512 | bytes 3322416 | tf_op jit(solution)/shard_map/dot_general | solution.py:936
  59.5 1.9 copy.93
  62.7 2.2 fusion.1
  64.9 1.6 reshape.579
  68.3 3.5 all-to-all-start.1
  72.5 12.1 %all-to-all-done.1.x_ref = bf16[4,200,512]{2,1,0:T(8,128)(2,1)S(1)} async-done(((bf16[4,200,512]{2,1,0:T(8,128)(2,1)}), bf16[4,200,512]{2,1,0:T(8,128)(2,1)S(1)}, u32[]{:S(2)}, u32[]{:S(2)}) %all-to-all-start.1) | async-done | bytes 819232 | tf_op jit(solution)/shard_map/all_to_all | solution.py:1045
  84.6 79.0 %all-gather.2.cloned.1.call-done = bf16[26624,1024]{1,0:T(8,128)(2,1)} async-done(((bf16[208,1024]{1,0:T(8,128)(2,1)}), bf16[26624,1024]{1,0:T(8,128)(2,1)}) %all-gather.2.cloned.1.call-update) | async-done | bytes 54525968 | tf_op jit(solution)/shard_map/all_gather | solution.py:1040
  163.5 7.4 %shard_map.512 = (f32[224,1024]{1,0:T(8,128)}, bf16[224,1024]{1,0:T(8,128)(2,1)}, bf16[224,1024]{1,0:T(8,128)(2,1)}) custom-call(s32[2]{0:T(128)} %get-tuple-element.485.core_ref.refs_0_, bf16[4,200,512]{2,1,0:T(8,128)(2,1)} %copy-done.1, bf16[200,224]{1,0:T(8,128)(2,1)} %constant.244.clone.pack_ref, f32[4,1,512]{2,1,0:T(1,128)} %reshape.584.gain_ref, ...), custom_call_target="tpu_custom_call" | custom-call | bytes 1024 | tf_op jit(solution)/shard_map/pallas_call | solution.py:117
  171.8 11.2 %shard_map.513 = (f32[224,1024]{1,0:T(8,128)}, bf16[224,1024]{1,0:T(8,128)(2,1)}, bf16[224,1024]{1,0:T(8,128)(2,1)}, bf16[224,1024]{1,0:T(8,128)(2,1)}, bf16[224...) custom-call(s32[2]{0:T(128)} %get-tuple-element.485.core_ref.refs_0_, ...), custom_call_target="tpu_custom_call" | custom-call | bytes 1024 | tf_op jit(solution)/shard_map/pallas_call | solution.py:117
  183.1 13.2 %shard_map.514 = (bf16[224,1024]{1,0:T(8,128)(2,1)}, bf16[224,4096]{1,0:T(8,128)(2,1)}, bf16[112,1024]{1,0:T(8,128)(2,1)}, bf16[224,2048]{1,0:T(8,128)(2,1)}, bf...) custom-call(s32[2]{0:T(128)} %get-tuple-element.485.core_ref.refs_0_, f32[224,1024]{1,0:T(8,128)} %get-tuple-element.173.mid_ref, ...), custom_call_target="tpu_custom_call" | custom-call | bytes 1024 | tf_op jit(solution)/shard_map/pallas_call | solution.py:117
  196.4 1.7 collective-permute-start.4
  198.6 5.0 collective-permute-done.4.refs_2_
  204.3 12.4 %shard_map.515 = (f32[224,1024]{1,0:T(8,128)}, bf16[224,1024]{1,0:T(8,128)(2,1)}, bf16[224,1024]{1,0:T(8,128)(2,1)}, bf16[224,1024]{1,0:T(8,128)(2,1)}, bf16[224...) custom-call(s32[2]{0:T(128)} %get-tuple-element.485.core_ref.refs_0_, ...), custom_call_target="tpu_custom_call" | custom-call | bytes 1024 | tf_op jit(solution)/shard_map/pallas_call | solution.py:117
  219.7 2.9 collective-permute-start.8
  224.5 20.7 %shard_map.516 = (bf16[224,1024]{1,0:T(8,128)(2,1)}, bf16[200,1024]{1,0:T(8,128)(2,1)}, bf16[224,1024]{1,0:T(8,128)(2,1)}, bf16[224,1024]{1,0:T(8,128)(2,1)}, bf...) custom-call(s32[2]{0:T(128)} %get-tuple-element.485.core_ref.refs_0_, ...), custom_call_target="tpu_custom_call" | custom-call | bytes 1024 | tf_op jit(solution)/shard_map/pallas_call | solution.py:117
  247.3 1.4 collective-permute-start.16
  248.8 2.2 collective-permute-start.17
  251.1 15.7 %shard_map.517 = (f32[224,1024]{1,0:T(8,128)}, bf16[224,1536]{1,0:T(8,128)(2,1)}, bf16[224,1536]{1,0:T(8,128)(2,1)}, f32[32,112,112]{2,1,0:T(8,128)}, f32[2,1024...) custom-call(s32[2]{0:T(128)} %get-tuple-element.485.core_ref.refs_0_, ...), custom_call_target="tpu_custom_call" | custom-call | bytes 1024 | tf_op jit(solution)/shard_map/pallas_call | solution.py:117
  272.6 11.1 %shard_map.518 = bf16[16,4,64,1024]{3,2,1,0:T(8,128)(2,1)} custom-call(s32[2]{0:T(128)} %get-tuple-element.485.core_ref.refs_0_, bf16[224,1024]{1,0:T(8,128)(2,1)} %get-tuple-element.200.refs_1_, bf16[224,1024]{1,0:T(8,128)(2,1)} %copy-done.34, bf16[224,2048]{1,0:T(8,128)(2,1)} %get-tuple-element.201.refs_3_, bf16[224,2048]{1,0:T(8,128)(2,1)} %copy-done.9, ...), custom_call_target="tpu_custom_call" | custom-call | bytes 1024 | tf_op jit(solution)/shard_map/pallas_call | solution.py:117
  286.3 15.2 %shard_map.519 = (f32[224,1024]{1,0:T(8,128)}, bf16[224,1024]{1,0:T(8,128)(2,1)}, bf16[224,1024]{1,0:T(8,128)(2,1)}, f32[1,4096]{1,0:T(1,128)}, f32[4,1024]{1,0:...) custom-call(s32[2]{0:T(128)} %get-tuple-element.485.core_ref.refs_0_, ...), custom_call_target="tpu_custom_call" | custom-call | bytes 1024 | tf_op jit(solution)/shard_map/pallas_call | solution.py:117
  302.5 1.7 collective-permute-start.22
  304.2 1.5 collective-permute-start.23
  305.7 15.5 %shard_map.520 = (f32[224,1024]{1,0:T(8,128)}, bf16[224,1536]{1,0:T(8,128)(2,1)}, bf16[224,1536]{1,0:T(8,128)(2,1)}, f32[32,112,112]{2,1,0:T(8,128)}, f32[2,1024]{1,0:T(2,128)}, /*index=5*/f32[2,1024]{1,0:T(2,128)}) custom-call(s32[2]{0:T(128)} %get-tuple-element.485.core_ref.refs_0_, f32[224,1024]{1,0:T(8,128)} %get-tuple-element.220.refs_1_, ...), custom_call_target="tpu_custom_call" | custom-call | bytes 1024 | tf_op jit(solution)/shard_map/pallas_call | solution.py:117
  321.3 8.4 %shard_map.521 = (bf16[224,1024]{1,0:T(8,128)(2,1)}, bf16[4,200,512]{2,1,0:T(8,128)(2,1)}, f32[4,1,512]{2,1,0:T(1,128)}, f32[4,1,512]{2,1,0:T(1,128)}) custom-call(s32[2]{0:T(128)} %get-tuple-element.485.core_ref.refs_0_, bf16[4,200,512]{2,1,0:T(8,128)(2,1)} %copy-done.1, bf16[200,224]{1,0:T(8,128)(2,1)} %constant.244.clone.pack_ref, ...), custom_call_target="tpu_custom_call" | custom-call | bytes 1024 | tf_op jit(solution)/shard_map/pallas_call | solution.py:117
  329.8 6.8 %shard_map.523 = (bf16[1024,512]{1,0:T(8,128)(2,1)}, bf16[1024,512]{1,0:T(8,128)(2,1)}) custom-call(s32[2]{0:T(128)} %get-tuple-element.485.core_ref.refs_0_, bf16[224,1024]{1,0:T(8,128)(2,1)} %get-tuple-element.258.dx_ref.refs_0_, bf16[224,1024]{1,0:T(8,128)(2,1)} %get-tuple-element.259.refs_1_, bf16[224,1024]{1,0:T(8,128)(2,1)} %get-tuple-element.260.refs_2_, ...), custom_call_target="tpu_custom_call" | custom-call | bytes 1024 | tf_op jit(solution)/shard_map/pallas_call | solution.py:117
  337.6 6.9 %shard_map.522 = (bf16[1024,512]{1,0:T(8,128)(2,1)}, bf16[1024,512]{1,0:T(8,128)(2,1)}) custom-call(s32[2]{0:T(128)} %get-tuple-element.485.core_ref.refs_0_, bf16[224,1024]{1,0:T(8,128)(2,1)} %get-tuple-element.233.refs_0_, bf16[224,1024]{1,0:T(8,128)(2,1)} %copy-done.17, bf16[224,1024]{1,0:T(8,128)(2,1)} %copy-done.18, bf16[224,1024]{1,0:T(8,128)(2,1)} %copy-done.19, ...), custom_call_target="tpu_custom_call" | custom-call | bytes 1024 | tf_op jit(solution)/shard_map/pallas_call | solution.py:117
  345.7 2.1 collective-permute-done.25.refs_14_
  348.0 1.5 collective-permute-done.28.refs_6_
  351.6 15.1 %shard_map.524 = bf16[16,4,64,1536]{3,2,1,0:T(8,128)(2,1)} custom-call(s32[2]{0:T(128)} %get-tuple-element.485.core_ref.refs_0_, bf16[224,1024]{1,0:T(8,128)(2,1)} %get-tuple-element.170.refs_1_, bf16[224,1024]{1,0:T(8,128)(2,1)} %copy-done.15, bf16[224,1536]{1,0:T(8,128)(2,1)} %get-tuple-element.232.refs_3_, bf16[224,1536]{1,0:T(8,128)(2,1)} %copy-done.11, ...), custom_call_target="tpu_custom_call" | custom-call | bytes 1024 | tf_op jit(solution)/shard_map/pallas_call | solution.py:117
  366.7 4.4 all-to-all-start.2
  373.6 2.6 convolution_convert_fusion
  376.3 2.3 fusion.31
  380.8 2.8 convolution_convert_fusion.1
  384.2 1.5 concatenate.98
  386.4 1.6 copy.102
  389.5 6.1 %all-to-all-start.3 = ((bf16[800,1,4,128]{3,2,1,0:T(4,128)(2,1)}), bf16[800,1,4,128]{3,2,1,0:T(4,128)(2,1)S(1)}, u32[]{:S(2)}, u32[]{:S(2)}) async-start(bf16[800,1,4,128]{3,2,1,0:T(4,128)(2,1)} %bitcast.75), calls=%async_computation.3 | async-start | bytes 1638400 | tf_op jit(solution)/shard_map/all_to_all | solution.py:1192
  395.7 3.0 collective-permute-start.34
  398.9 2.4 collective-permute-start.36
  401.3 20.3 %collective-permute-done.34 = bf16[64,1024]{1,0:T(8,128)(2,1)S(1)} collective-permute-done((bf16[64,1024]{1,0:T(8,128)(2,1)S(1)}, bf16[64,1024]{1,0:T(8,128)(2,1)S(1)}, u32[]{:S(2)}, u32[]{:S(2)}) %collective-permute-start.34) | collective-permute-done | bytes 131104 | tf_op jit(solution)/shard_map/ppermute | solution.py:999
  421.6 1.6 collective-permute-done.35
  423.3 3.9 collective-permute-start.37
  428.4 2.6 collective-permute-start.31
  431.9 1.7 collective-permute-done.37
  433.7 1.4 collective-permute-start.39
  435.2 1.6 copy.107
  436.8 4.2 collective-permute-done.38
  441.9 2.8 collective-permute-start.40
  445.3 2.1 collective-permute-start.42
  452.3 3.6 copy.106
  460.8 4.1 collective-permute-start.48
  466.4 4.4 collective-permute-done.48
  471.8 1.4 collective-permute-start.50
  474.2 10.2 %reduce-scatter.7.cloned.1.call-done = bf16[1,4,64,1536]{3,2,1,0:T(8,128)(2,1)} async-done(((bf16[16,4,64,1536]{3,2,1,0:T(8,128)(2,1)}), bf16[1,4,64,1536]{3,2,1,0:T(8,128)(2,1)}) %reduce-scatter.7.cloned.1.call-update) | async-done | bytes 786448
  485.6 1.4 collective-permute-start.43
  487.0 2.6 collective-permute-start.44
  492.0 4.3 collective-permute-done.44
  496.5 2.0 collective-permute-start.46
  (405 shorter events, 73.7 us)
Async XLA Ops:
  7.2 156.3 %all-gather.2.cloned.1.call-start = ((), (), s32[]{:S(2)}) async-start(), calls=%async_computation.6 | async-start | bytes 54951936 | tf_op jit(solution)/shard_map/all_gather | solution.py:1040
  11.5 38.6 %collective-permute-start = (f32[80,128]{1,0:T(8,128)}, f32[80,128]{1,0:T(8,128)}, u32[]{:S(2)}, u32[]{:S(2)}) collective-permute-start(f32[80,128]{1,0:T(8,128)} %bitcast.10), channel_id=1, source_target_pairs={{0,1},{1,2},{2,3},{3,0},{4,5},{5,6},{6,7},{7,4},{8,9},{9,10},{10,1... | collective-permute-start | bytes 122888 | tf_op jit(solution)/shard_map/ppermute | solution.py:979
  14.0 36.2 %collective-permute-start.1 = (f32[80,128]{1,0:T(8,128)}, f32[80,128]{1,0:T(8,128)}, u32[]{:S(2)}, u32[]{:S(2)}) collective-permute-start(f32[80,128]{1,0:T(8,128)} %bitcast.10), channel_id=1, source_target_pairs={{0,2},{1,3},{2,0},{3,1},{4,6},{5,7},{6,4},{7,5},{8,10},{9,11},{10,... | collective-permute-start | bytes 122888 | tf_op jit(solution)/shard_map/ppermute | solution.py:979
  17.3 32.9 %collective-permute-start.2 = (f32[80,128]{1,0:T(8,128)}, f32[80,128]{1,0:T(8,128)}, u32[]{:S(2)}, u32[]{:S(2)}) collective-permute-start(f32[80,128]{1,0:T(8,128)} %bitcast.10), channel_id=1, source_target_pairs={{0,3},{1,0},{2,1},{3,2},{4,7},{5,4},{6,5},{7,6},{8,11},{9,8},{10,9... | collective-permute-start | bytes 122888 | tf_op jit(solution)/shard_map/ppermute | solution.py:979
  19.2 45.6 %all-to-all-start = ((bf16[25,32,4,128]{3,2,0,1:T(4,128)(2,1)}), bf16[25,32,4,128]{3,2,0,1:T(4,128)(2,1)}, u32[]{:S(2)}, u32[]{:S(2)}) async-start(bf16[25,32,4,128]{3,2,0,1:T(4,128)(2,1)} %copy.96), calls=%async_computation | async-start | bytes 1638400 | tf_op jit(solution)/shard_map/all_to_all | solution.py:1043
  68.3 16.3 %all-to-all-start.1 = ((bf16[4,200,512]{2,1,0:T(8,128)(2,1)}), bf16[4,200,512]{2,1,0:T(8,128)(2,1)S(1)}, u32[]{:S(2)}, u32[]{:S(2)}) async-start(bf16[4,200,512]{2,1,0:T(8,128)(2,1)} %copy.98), calls=%async_computation.1 | async-start | bytes 1638400 | tf_op jit(solution)/shard_map/all_to_all | solution.py:1045
  71.8 386.6 %reduce-scatter.9.cloned.1.call-start = ((), (), s32[]{:S(2)}) async-start(), calls=%async_computation.8 | async-start | bytes 8912896
  84.6 79.0 %copy-start.1 = (bf16[4,200,512]{2,1,0:T(8,128)(2,1)}, bf16[4,200,512]{2,1,0:T(8,128)(2,1)S(1)}, u32[]{:S(2)}) copy-start(bf16[4,200,512]{2,1,0:T(8,128)(2,1)S(1)} %all-to-all-done.1.x_ref) | copy-start | bytes 2457604
  170.9 12.1 %collective-permute-start.3 = (bf16[224,1024]{1,0:T(8,128)(2,1)}, bf16[224,1024]{1,0:T(8,128)(2,1)S(1)}, u32[]{:S(2)}, u32[]{:S(2)}) collective-permute-start(bf16[224,1024]{1,0:T(8,128)(2,1)} %get-tuple-element.172), channel_id=1, source_target_pairs={{0,4},{4,0},{1,5},{5,1},{2,6},{6,2},{3,7},{7,3},{8,12},{12,8},{9,1... | collective-permute-start | bytes 1376264 | tf_op jit(solution)/shard_map/ppermute | solution.py:990
  196.4 7.2 %collective-permute-start.4 = (bf16[112,1024]{1,0:T(8,128)(2,1)}, bf16[112,1024]{1,0:T(8,128)(2,1)S(1)}, u32[]{:S(2)}, u32[]{:S(2)}) collective-permute-start(bf16[112,1024]{1,0:T(8,128)(2,1)} %get-tuple-element.175), channel_id=1, source_target_pairs={{1,0},{2,1},{3,2},{0,3},{5,4},{6,5},{7,6},{4,7},{9,8},{10,9},{11,1... | collective-permute-start | bytes 688136 | tf_op jit(solution)/shard_map/ppermute | solution.py:1128
  198.1 24.6 %collective-permute-start.5 = (bf16[224,1024]{1,0:T(8,128)(2,1)S(1)}, bf16[224,1024]{1,0:T(8,128)(2,1)S(1)}, u32[]{:S(2)}, u32[]{:S(2)}) collective-permute-start(bf16[224,1024]{1,0:T(8,128)(2,1)S(1)} %copy-done.14), channel_id=1, source_target_pairs={{0,4},{4,0},{1,5},{5,1},{2,6},{6,2},{3,7},{7,3},{8,12},{12,8},{9,1... | collective-permute-start | bytes 1376264 | tf_op jit(solution)/shard_map/ppermute | solution.py:990
  204.3 19.4 %copy-start.58 = (f32[224]{0:T(256)S(1)}, f32[224]{0:T(256)}, u32[]{:S(2)}) copy-start(f32[224]{0:T(256)} %and_convert_fusion) | copy-start | bytes 2692
  216.7 29.8 %collective-permute-start.10 = (bf16[224,1024]{1,0:T(8,128)(2,1)}, bf16[224,1024]{1,0:T(8,128)(2,1)S(1)}, u32[]{:S(2)}, u32[]{:S(2)}) collective-permute-start(bf16[224,1024]{1,0:T(8,128)(2,1)} %get-tuple-element.189.refs_5_), channel_id=1, source_target_pairs={{0,4},{4,0},{1,5},{5,1},{2,6},{6,2},{3,7},{7,3},{8,12},{12,8},{9,1... | collective-permute-start | bytes 1376264 | tf_op jit(solution)/shard_map/ppermute | solution.py:990
  217.8 1.9 collective-permute-start.6
  217.9 29.4 %collective-permute-start.7 = (bf16[224,1024]{1,0:T(8,128)(2,1)S(1)}, bf16[224,1024]{1,0:T(8,128)(2,1)S(1)}, u32[]{:S(2)}, u32[]{:S(2)}) collective-permute-start(bf16[224,1024]{1,0:T(8,128)(2,1)S(1)} %copy-done.16), channel_id=1, source_target_pairs={{0,1},{1,2},{2,3},{3,0},{4,5},{5,6},{6,7},{7,4},{8,9},{9,10},{10,1... | collective-permute-start | bytes 1376264 | tf_op jit(solution)/shard_map/ppermute | solution.py:905
  218.2 27.1 %collective-permute-start.11 = (bf16[224,512]{1,0:T(8,128)(2,1)}, bf16[224,512]{1,0:T(8,128)(2,1)S(1)}, u32[]{:S(2)}, u32[]{:S(2)}) collective-permute-start(bf16[224,512]{1,0:T(8,128)(2,1)} %get-tuple-element.190), channel_id=1, source_target_pairs={{0,4},{4,0},{1,5},{5,1},{2,6},{6,2},{3,7},{7,3},{8,12},{12,8},{9,1... | collective-permute-start | bytes 688136 | tf_op jit(solution)/shard_map/ppermute | solution.py:990
  219.7 29.1 %collective-permute-start.8 = (bf16[224,1024]{1,0:T(8,128)(2,1)S(1)}, bf16[224,1024]{1,0:T(8,128)(2,1)S(1)}, u32[]{:S(2)}, u32[]{:S(2)}) collective-permute-start(bf16[224,1024]{1,0:T(8,128)(2,1)S(1)} %copy-done.16), channel_id=1, source_target_pairs={{0,2},{1,3},{2,0},{3,1},{4,6},{5,7},{6,4},{7,5},{8,10},{9,11},{10,... | collective-permute-start | bytes 1376264 | tf_op jit(solution)/shard_map/ppermute | solution.py:905
  223.4 27.6 %collective-permute-start.9 = (bf16[224,1024]{1,0:T(8,128)(2,1)S(1)}, bf16[224,1024]{1,0:T(8,128)(2,1)S(1)}, u32[]{:S(2)}, u32[]{:S(2)}) collective-permute-start(bf16[224,1024]{1,0:T(8,128)(2,1)S(1)} %copy-done.16), channel_id=1, source_target_pairs={{0,3},{1,0},{2,1},{3,2},{4,7},{5,4},{6,5},{7,6},{8,11},{9,8},{10,9... | collective-permute-start | bytes 1376264 | tf_op jit(solution)/shard_map/ppermute | solution.py:905
  245.2 21.5 %copy-start.37 = (bf16[224,512]{1,0:T(8,128)(2,1)}, bf16[224,512]{1,0:T(8,128)(2,1)S(1)}, u32[]{:S(2)}) copy-start(bf16[224,512]{1,0:T(8,128)(2,1)S(1)} %collective-permute-done.11.refs_12_) | copy-start | bytes 688132
  245.2 22.9 %collective-permute-start.15 = (bf16[224,1024]{1,0:T(8,128)(2,1)}, bf16[224,1024]{1,0:T(8,128)(2,1)S(1)}, u32[]{:S(2)}, u32[]{:S(2)}) collective-permute-start(bf16[224,1024]{1,0:T(8,128)(2,1)} %get-tuple-element.205), channel_id=1, source_target_pairs={{0,1},{1,2},{2,3},{3,0},{4,5},{5,6},{6,7},{7,4},{8,9},{9,10},{10,1... | collective-permute-start | bytes 1376264 | tf_op jit(solution)/shard_map/ppermute | solution.py:905
  246.5 24.4 %collective-permute-start.13 = (bf16[224,2048]{1,0:T(8,128)(2,1)}, bf16[224,2048]{1,0:T(8,128)(2,1)S(1)}, u32[]{:S(2)}, u32[]{:S(2)}) collective-permute-start(bf16[224,2048]{1,0:T(8,128)(2,1)} %get-tuple-element.203), channel_id=1, source_target_pairs={{0,4},{4,0},{1,5},{5,1},{2,6},{6,2},{3,7},{7,3},{8,12},{12,8},{9,1... | collective-permute-start | bytes 2752520 | tf_op jit(solution)/shard_map/ppermute | solution.py:990
  247.3 19.4 %copy-start.17 = (bf16[224,1024]{1,0:T(8,128)(2,1)}, bf16[224,1024]{1,0:T(8,128)(2,1)S(1)}, u32[]{:S(2)}) copy-start(bf16[224,1024]{1,0:T(8,128)(2,1)S(1)} %collective-permute-done.7.refs_1_) | copy-start | bytes 1376260
  247.3 22.2 %collective-permute-start.16 = (bf16[224,1024]{1,0:T(8,128)(2,1)}, bf16[224,1024]{1,0:T(8,128)(2,1)S(1)}, u32[]{:S(2)}, u32[]{:S(2)}) collective-permute-start(bf16[224,1024]{1,0:T(8,128)(2,1)} %get-tuple-element.206), channel_id=1, source_target_pairs={{0,2},{1,3},{2,0},{3,1},{4,6},{5,7},{6,4},{7,5},{8,10},{9,11},{10,... | collective-permute-start | bytes 1376264 | tf_op jit(solution)/shard_map/ppermute | solution.py:905
  248.8 20.9 %collective-permute-start.17 = (bf16[224,1024]{1,0:T(8,128)(2,1)}, bf16[224,1024]{1,0:T(8,128)(2,1)S(1)}, u32[]{:S(2)}, u32[]{:S(2)}) collective-permute-start(bf16[224,1024]{1,0:T(8,128)(2,1)} %get-tuple-element.207), channel_id=1, source_target_pairs={{0,3},{1,0},{2,1},{3,2},{4,7},{5,4},{6,5},{7,6},{8,11},{9,8},{10,9... | collective-permute-start | bytes 1376264 | tf_op jit(solution)/shard_map/ppermute | solution.py:905
  266.8 4.8 collective-permute-start.18
  268.2 2.8 collective-permute-start.14
  269.5 2.1 collective-permute-start.12
  271.0 12.8 %collective-permute-start.19 = (bf16[112,1024]{1,0:T(8,128)(2,1)}, bf16[112,1024]{1,0:T(8,128)(2,1)S(1)}, u32[]{:S(2)}, u32[]{:S(2)}) collective-permute-start(bf16[112,1024]{1,0:T(8,128)(2,1)} %get-tuple-element.215), channel_id=1, source_target_pairs={{0,1},{1,2},{2,3},{3,0},{4,5},{5,6},{6,7},{7,4},{8,9},{9,10},{10,1... | collective-permute-start | bytes 688136 | tf_op jit(solution)/shard_map/ppermute | solution.py:1138
  284.4 200.0 %reduce-scatter.7.cloned.1.call-start = ((), (), s32[]{:S(2)}) async-start(), calls=%async_computation.7 | async-start | bytes 13369344
  285.0 16.5 %collective-permute-start.20 = (bf16[224,2048]{1,0:T(8,128)(2,1)S(1)}, bf16[224,2048]{1,0:T(8,128)(2,1)S(1)}, u32[]{:S(2)}, u32[]{:S(2)}) collective-permute-start(bf16[224,2048]{1,0:T(8,128)(2,1)S(1)} %copy-done.66), channel_id=1, source_target_pairs={{0,4},{4,0},{1,5},{5,1},{2,6},{6,2},{3,7},{7,3},{8,12},{12,8},{9,1... | collective-permute-start | bytes 2752520 | tf_op jit(solution)/shard_map/ppermute | solution.py:990
  301.5 19.7 %copy-start.8 = (bf16[224,2048]{1,0:T(8,128)(2,1)}, bf16[224,2048]{1,0:T(8,128)(2,1)S(1)}, u32[]{:S(2)}) copy-start(bf16[224,2048]{1,0:T(8,128)(2,1)S(1)} %collective-permute-done.20.refs_16_) | copy-start | bytes 2752516
  301.6 28.2 %collective-permute-start.21 = (bf16[224,1024]{1,0:T(8,128)(2,1)}, bf16[224,1024]{1,0:T(8,128)(2,1)S(1)}, u32[]{:S(2)}, u32[]{:S(2)}) collective-permute-start(bf16[224,1024]{1,0:T(8,128)(2,1)} %get-tuple-element.241), channel_id=1, source_target_pairs={{0,1},{1,2},{2,3},{3,0},{4,5},{5,6},{6,7},{7,4},{8,9},{9,10},{10,1... | collective-permute-start | bytes 1376264 | tf_op jit(solution)/shard_map/ppermute | solution.py:905
  302.5 27.2 %collective-permute-start.22 = (bf16[224,1024]{1,0:T(8,128)(2,1)}, bf16[224,1024]{1,0:T(8,128)(2,1)S(1)}, u32[]{:S(2)}, u32[]{:S(2)}) collective-permute-start(bf16[224,1024]{1,0:T(8,128)(2,1)} %get-tuple-element.242), channel_id=1, source_target_pairs={{0,2},{1,3},{2,0},{3,1},{4,6},{5,7},{6,4},{7,5},{8,10},{9,11},{10,... | collective-permute-start | bytes 1376264 | tf_op jit(solution)/shard_map/ppermute | solution.py:905
  304.2 25.6 %collective-permute-start.23 = (bf16[224,1024]{1,0:T(8,128)(2,1)}, bf16[224,1024]{1,0:T(8,128)(2,1)S(1)}, u32[]{:S(2)}, u32[]{:S(2)}) collective-permute-start(bf16[224,1024]{1,0:T(8,128)(2,1)} %get-tuple-element.243), channel_id=1, source_target_pairs={{0,3},{1,0},{2,1},{3,2},{4,7},{5,4},{6,5},{7,6},{8,11},{9,8},{10,9... | collective-permute-start | bytes 1376264 | tf_op jit(solution)/shard_map/ppermute | solution.py:905
  336.6 13.5 %collective-permute-start.26 = (bf16[1024,512]{1,0:T(8,128)(2,1)}, bf16[1024,512]{1,0:T(8,128)(2,1)S(1)}, u32[]{:S(2)}, u32[]{:S(2)}) collective-permute-start(bf16[1024,512]{1,0:T(8,128)(2,1)} %get-tuple-element.266), channel_id=1, source_target_pairs={{0,4},{4,0},{1,5},{5,1},{2,6},{6,2},{3,7},{7,3},{8,12},{12,8},{9,1... | collective-permute-start | bytes 3145736 | tf_op jit(solution)/shard_map/ppermute | solution.py:990
  344.5 5.6 %collective-permute-start.29 = (bf16[1024,512]{1,0:T(8,128)(2,1)}, bf16[1024,512]{1,0:T(8,128)(2,1)S(1)}, u32[]{:S(2)}, u32[]{:S(2)}) collective-permute-start(bf16[1024,512]{1,0:T(8,128)(2,1)} %get-tuple-element.280), channel_id=1, source_target_pairs={{0,4},{4,0},{1,5},{5,1},{2,6},{6,2},{3,7},{7,3},{8,12},{12,8},{9,1... | collective-permute-start | bytes 3145736 | tf_op jit(solution)/shard_map/ppermute | solution.py:990
  344.7 3.2 collective-permute-start.25
  345.0 4.4 collective-permute-start.27
  345.2 4.3 collective-permute-start.28
  347.8 2.3 collective-permute-start.24
  366.7 19.7 %all-to-all-start.2 = ((bf16[4,200,512]{2,1,0:T(8,128)(2,1)}), bf16[4,200,512]{2,1,0:T(8,128)(2,1)}, u32[]{:S(2)}, u32[]{:S(2)}) async-start(bf16[4,200,512]{2,1,0:T(8,128)(2,1)} %get-tuple-element.297), calls=%async_computation.2 | async-start | bytes 1638400 | tf_op jit(solution)/shard_map/all_to_all | solution.py:1188
  385.8 9.9 %collective-permute-start.33 = (bf16[64,1024]{1,0:T(8,128)(2,1)S(1)}, bf16[64,1024]{1,0:T(8,128)(2,1)S(1)}, u32[]{:S(2)}, u32[]{:S(2)}) collective-permute-start(bf16[64,1024]{1,0:T(8,128)(2,1)S(1)} %convert_element_type.193), channel_id=1, source_target_pairs={{0,4},{4,0},{1,5},{5,1},{2,6},{6,2},{3,7},{7,3},{8,12},{12,8},{9,1... | collective-permute-start | bytes 393224 | tf_op jit(solution)/shard_map/ppermute | solution.py:990
  388.3 38.8 %copy-start.35 = (bf16[200,1024]{1,0:T(8,128)(2,1)S(1)}, bf16[200,1024]{1,0:T(8,128)(2,1)}, u32[]{:S(2)}) copy-start(bf16[200,1024]{1,0:T(8,128)(2,1)} %get-tuple-element.296) | copy-start | bytes 1228804
  389.5 45.6 %all-to-all-start.3 = ((bf16[800,1,4,128]{3,2,1,0:T(4,128)(2,1)}), bf16[800,1,4,128]{3,2,1,0:T(4,128)(2,1)S(1)}, u32[]{:S(2)}, u32[]{:S(2)}) async-start(bf16[800,1,4,128]{3,2,1,0:T(4,128)(2,1)} %bitcast.75), calls=%async_computation.3 | async-start | bytes 1638400 | tf_op jit(solution)/shard_map/all_to_all | solution.py:1192
  395.7 25.9 %collective-permute-start.34 = (bf16[64,1024]{1,0:T(8,128)(2,1)S(1)}, bf16[64,1024]{1,0:T(8,128)(2,1)S(1)}, u32[]{:S(2)}, u32[]{:S(2)}) collective-permute-start(bf16[64,1024]{1,0:T(8,128)(2,1)S(1)} %add_convert_fusion.2), channel_id=1, source_target_pairs={{0,16},{8,24},{16,0},{24,8},{1,17},{9,25},{17,1},{25,9},{2,18},{10... | collective-permute-start | bytes 393224 | tf_op jit(solution)/shard_map/ppermute | solution.py:999
  398.7 24.6 %collective-permute-start.35 = (bf16[64,1024]{1,0:T(8,128)(2,1)S(1)}, bf16[64,1024]{1,0:T(8,128)(2,1)S(1)}, u32[]{:S(2)}, u32[]{:S(2)}) collective-permute-start(bf16[64,1024]{1,0:T(8,128)(2,1)S(1)} %add_convert_fusion.2), channel_id=1, source_target_pairs={{0,8},{8,16},{16,24},{24,0},{1,9},{9,17},{17,25},{25,1},{2,10},{10... | collective-permute-start | bytes 393224 | tf_op jit(solution)/shard_map/ppermute | solution.py:999
  398.9 24.3 %collective-permute-start.36 = (bf16[64,1024]{1,0:T(8,128)(2,1)S(1)}, bf16[64,1024]{1,0:T(8,128)(2,1)S(1)}, u32[]{:S(2)}, u32[]{:S(2)}) collective-permute-start(bf16[64,1024]{1,0:T(8,128)(2,1)S(1)} %add_convert_fusion.2), channel_id=1, source_target_pairs={{0,24},{8,0},{16,8},{24,16},{1,25},{9,1},{17,9},{25,17},{2,26},{10... | collective-permute-start | bytes 393224 | tf_op jit(solution)/shard_map/ppermute | solution.py:999
  423.3 10.4 %collective-permute-start.37 = (bf16[64,1024]{1,0:T(8,128)(2,1)S(1)}, bf16[64,1024]{1,0:T(8,128)(2,1)S(1)}, u32[]{:S(2)}, u32[]{:S(2)}) collective-permute-start(bf16[64,1024]{1,0:T(8,128)(2,1)S(1)} %add_convert_fusion.1), channel_id=1, source_target_pairs={{0,64},{32,96},{64,0},{96,32},{1,65},{33,97},{65,1},{97,33},{2,66}... | collective-permute-start | bytes 393224 | tf_op jit(solution)/shard_map/ppermute | solution.py:999
  427.2 18.1 %collective-permute-start.30 = (bf16[200,1024]{1,0:T(8,128)(2,1)S(1)}, bf16[200,1024]{1,0:T(8,128)(2,1)S(1)}, u32[]{:S(2)}, u32[]{:S(2)}) collective-permute-start(bf16[200,1024]{1,0:T(8,128)(2,1)S(1)} %copy-done.35), channel_id=1, source_target_pairs={{0,1},{1,2},{2,3},{3,0},{4,5},{5,6},{6,7},{7,4},{8,9},{9,10},{10,1... | collective-permute-start | bytes 1228808 | tf_op jit(solution)/shard_map/ppermute | solution.py:979
  428.4 20.2 %collective-permute-start.31 = (bf16[200,1024]{1,0:T(8,128)(2,1)S(1)}, bf16[200,1024]{1,0:T(8,128)(2,1)S(1)}, u32[]{:S(2)}, u32[]{:S(2)}) collective-permute-start(bf16[200,1024]{1,0:T(8,128)(2,1)S(1)} %copy-done.35), channel_id=1, source_target_pairs={{0,2},{1,3},{2,0},{3,1},{4,6},{5,7},{6,4},{7,5},{8,10},{9,11},{10,... | collective-permute-start | bytes 1228808 | tf_op jit(solution)/shard_map/ppermute | solution.py:979
  431.0 18.0 %collective-permute-start.32 = (bf16[200,1024]{1,0:T(8,128)(2,1)S(1)}, bf16[200,1024]{1,0:T(8,128)(2,1)S(1)}, u32[]{:S(2)}, u32[]{:S(2)}) collective-permute-start(bf16[200,1024]{1,0:T(8,128)(2,1)S(1)} %copy-done.35), channel_id=1, source_target_pairs={{0,3},{1,0},{2,1},{3,2},{4,7},{5,4},{6,5},{7,6},{8,11},{9,8},{10,9... | collective-permute-start | bytes 1228808 | tf_op jit(solution)/shard_map/ppermute | solution.py:979
  431.9 9.1 %collective-permute-start.38 = (bf16[64,1024]{1,0:T(8,128)(2,1)S(1)}, bf16[64,1024]{1,0:T(8,128)(2,1)S(1)}, u32[]{:S(2)}, u32[]{:S(2)}) collective-permute-start(bf16[64,1024]{1,0:T(8,128)(2,1)S(1)} %add_convert_fusion.1), channel_id=1, source_target_pairs={{0,32},{32,64},{64,96},{96,0},{1,33},{33,65},{65,97},{97,1},{2,34}... | collective-permute-start | bytes 393224 | tf_op jit(solution)/shard_map/ppermute | solution.py:999
  433.7 8.1 %collective-permute-start.39 = (bf16[64,1024]{1,0:T(8,128)(2,1)S(1)}, bf16[64,1024]{1,0:T(8,128)(2,1)S(1)}, u32[]{:S(2)}, u32[]{:S(2)}) collective-permute-start(bf16[64,1024]{1,0:T(8,128)(2,1)S(1)} %add_convert_fusion.1), channel_id=1, source_target_pairs={{0,96},{32,0},{64,32},{96,64},{1,97},{33,1},{65,33},{97,65},{2,98}... | collective-permute-start | bytes 393224 | tf_op jit(solution)/shard_map/ppermute | solution.py:999
  441.9 14.0 %collective-permute-start.40 = (bf16[64,1024]{1,0:T(8,128)(2,1)S(1)}, bf16[64,1024]{1,0:T(8,128)(2,1)S(1)}, u32[]{:S(2)}, u32[]{:S(2)}) collective-permute-start(bf16[64,1024]{1,0:T(8,128)(2,1)S(1)} %add_convert_fusion), channel_id=1, source_target_pairs={{0,2},{1,3},{2,0},{3,1},{4,6},{5,7},{6,4},{7,5},{8,10},{9,11},{10,... | collective-permute-start | bytes 393224 | tf_op jit(solution)/shard_map/ppermute | solution.py:999
  444.7 11.2 %collective-permute-start.41 = (bf16[64,1024]{1,0:T(8,128)(2,1)S(1)}, bf16[64,1024]{1,0:T(8,128)(2,1)S(1)}, u32[]{:S(2)}, u32[]{:S(2)}) collective-permute-start(bf16[64,1024]{1,0:T(8,128)(2,1)S(1)} %add_convert_fusion), channel_id=1, source_target_pairs={{0,1},{1,2},{2,3},{3,0},{4,5},{5,6},{6,7},{7,4},{8,9},{9,10},{10,1... | collective-permute-start | bytes 393224 | tf_op jit(solution)/shard_map/ppermute | solution.py:999
  445.3 10.6 %collective-permute-start.42 = (bf16[64,1024]{1,0:T(8,128)(2,1)S(1)}, bf16[64,1024]{1,0:T(8,128)(2,1)S(1)}, u32[]{:S(2)}, u32[]{:S(2)}) collective-permute-start(bf16[64,1024]{1,0:T(8,128)(2,1)S(1)} %add_convert_fusion), channel_id=1, source_target_pairs={{0,3},{1,0},{2,1},{3,2},{4,7},{5,4},{6,5},{7,6},{8,11},{9,8},{10,9... | collective-permute-start | bytes 393224 | tf_op jit(solution)/shard_map/ppermute | solution.py:999
  459.5 6.9 %collective-permute-start.47 = (bf16[64,1024]{1,0:T(8,128)(2,1)S(1)}, bf16[64,1024]{1,0:T(8,128)(2,1)S(1)}, u32[]{:S(2)}, u32[]{:S(2)}) collective-permute-start(bf16[64,1024]{1,0:T(8,128)(2,1)S(1)} %get-tuple-element.403), channel_id=1, source_target_pairs={{0,1},{1,2},{2,3},{3,0},{4,5},{5,6},{6,7},{7,4},{8,9},{9,10},{10,1... | collective-permute-start | bytes 393224 | tf_op jit(solution)/shard_map/ppermute | solution.py:905
  460.8 10.0 %collective-permute-start.48 = (bf16[64,1024]{1,0:T(8,128)(2,1)S(1)}, bf16[64,1024]{1,0:T(8,128)(2,1)S(1)}, u32[]{:S(2)}, u32[]{:S(2)}) collective-permute-start(bf16[64,1024]{1,0:T(8,128)(2,1)S(1)} %get-tuple-element.405), channel_id=1, source_target_pairs={{0,2},{1,3},{2,0},{3,1},{4,6},{5,7},{6,4},{7,5},{8,10},{9,11},{10,... | collective-permute-start | bytes 393224 | tf_op jit(solution)/shard_map/ppermute | solution.py:905
  464.9 5.9 %collective-permute-start.49 = (bf16[64,1024]{1,0:T(8,128)(2,1)S(1)}, bf16[64,1024]{1,0:T(8,128)(2,1)S(1)}, u32[]{:S(2)}, u32[]{:S(2)}) collective-permute-start(bf16[64,1024]{1,0:T(8,128)(2,1)S(1)} %get-tuple-element.404), channel_id=1, source_target_pairs={{0,3},{1,0},{2,1},{3,2},{4,7},{5,4},{6,5},{7,6},{8,11},{9,8},{10,9... | collective-permute-start | bytes 393224 | tf_op jit(solution)/shard_map/ppermute | solution.py:905
  471.8 2.3 collective-permute-start.50
  485.6 6.4 %collective-permute-start.43 = (bf16[64,1280]{1,0:T(8,128)(2,1)S(1)}, bf16[64,1280]{1,0:T(8,128)(2,1)S(1)}, u32[]{:S(2)}, u32[]{:S(2)}) collective-permute-start(bf16[64,1280]{1,0:T(8,128)(2,1)S(1)} %get-tuple-element.400), channel_id=1, source_target_pairs={{0,1},{1,2},{2,3},{3,0},{4,5},{5,6},{6,7},{7,4},{8,9},{9,10},{10,1... | collective-permute-start | bytes 491528 | tf_op jit(solution)/shard_map/ppermute | solution.py:905
  487.0 9.3 %collective-permute-start.44 = (bf16[64,1280]{1,0:T(8,128)(2,1)S(1)}, bf16[64,1280]{1,0:T(8,128)(2,1)S(1)}, u32[]{:S(2)}, u32[]{:S(2)}) collective-permute-start(bf16[64,1280]{1,0:T(8,128)(2,1)S(1)} %get-tuple-element.402), channel_id=1, source_target_pairs={{0,2},{1,3},{2,0},{3,1},{4,6},{5,7},{6,4},{7,5},{8,10},{9,11},{10,... | collective-permute-start | bytes 491528 | tf_op jit(solution)/shard_map/ppermute | solution.py:905
  489.5 6.8 %collective-permute-start.45 = (bf16[64,1280]{1,0:T(8,128)(2,1)S(1)}, bf16[64,1280]{1,0:T(8,128)(2,1)S(1)}, u32[]{:S(2)}, u32[]{:S(2)}) collective-permute-start(bf16[64,1280]{1,0:T(8,128)(2,1)S(1)} %get-tuple-element.401), channel_id=1, source_target_pairs={{0,3},{1,0},{2,1},{3,2},{4,7},{5,4},{6,5},{7,6},{8,11},{9,8},{10,9... | collective-permute-start | bytes 491528 | tf_op jit(solution)/shard_map/ppermute | solution.py:905
  496.5 3.0 collective-permute-start.46
  (63 other events, 357.4 us)
Sparse Core Ops, SparseCore 0:
  11.0 152.4 all-gather.1
  283.9 83.5 reduce-scatter.8
  370.9 113.4 reduce-scatter.6

commit v3 on v2

--- a/solution.py
+++ b/solution.py
@@ -1134,7 +1134,7 @@
     sums = [None, None]
     got = attn_backward(core, 1, dmid, dattn, start, ln1_gain[1:2], weights, q, k, v, probs)
     grad, mixed_mine, mixed_other, pairs, dqv, rows_one, sent = got
-    sent, (dpre_got, dattn_got, acts) = after(sent, (dpre_got, dattn_got, acts))
+    sent, (dpre_got, dattn_got, c2_got) = after(sent, (dpre_got, dattn_got, c2_got))
     halo = lax.ppermute(sent, "tp", [(i, (i + 1) % TP) for i in range(TP)])
     mixed_got = swap_core(mixed_other)
     sums[1] = (db1, rows_two, dqv, rows_one, pairs)
@@ -1153,7 +1153,7 @@
     act_got = swap_core(act_other)
     got = mlp_backward(core, grad, halo, mid, ln2_gain[0:1], weights, slope)
     dmid, dmlp, dattn, db1, rows_two = got[:5]
-    dattn, (dpre, act_got) = after(dattn, (list(got[5:]), act_got))
+    dattn, (dpre, act_got, acts, tiles) = after(dattn, (list(got[5:]), act_got, acts, tiles))
     dpre = send_ahead(dpre)
     got = attn_backward(core, 0, dmid, dattn, start, ln1_gain[0:1], weights, q, k, v, probs)
     grad, mixed_mine, mixed_other, pairs, dqv, rows_one = got
@@ -1161,10 +1161,10 @@
     grad, dattn_sent = lax.optimization_barrier((grad, dattn))
     mixed_got, dattn_got = [swap_core(value) for value in (mixed_other, dattn_sent)]
     first, dm, dgain, dbias = merge_backward(core, parts, merge_gain_all, weights, grad)
-    first, (dpre, tiles, acts) = after(first, (dpre, tiles, acts))
-    first_got, dmlp_got = swap_core(first), swap_core(dmlp)
     last_other, last_mine = column_grads(core, tiles, acts)
     last_got = swap_core(last_other)
+    first, dpre = after(first, dpre)
+    first_got, dmlp_got = swap_core(first), swap_core(dmlp)
     up_other, up_mine = column_grads(core, c2_all, dpre)
     up_mine, (first_got, dmlp_got, last_got, mixed_got, dattn_got) = after(
         up_mine, (first_got, dmlp_got, last_got, mixed_got, dattn_got)

time: 514 us -> 509 us (level)
    unnamed x5, waiting for transfers between devices: 10.3 us -> 4.15 us
    ppermute x15, waiting for transfers between devices: 8.8 us -> 14.1 us  [send_ahead(): lax.ppermute(pieces[step], 'tp', [(i, (i + step) % TP) for i in range(TP)])]
  transfers between devices with their start and end apart: 58 -> 58, of which waited for: 21 -> 23; matrix products, arithmetic and copies ran while one was open for 13% -> 14% of each run, Pallas kernels for 27% -> 30%
where the time goes in v3:
time: 509 us; the launch traced here: 506 us
  Pallas kernels  162 us (32%)
  waiting for transfers between devices  153 us (30%)
  starting transfers between devices  86.4 us (17%)
  local copies, waits for them, and re-layouts  52.5 us (10%)
  between operations  24.2 us (5%)
  other arithmetic  16.4 us (3%)
  matrix products  11.1 us (2%)
    pallas_call x13, Pallas kernels, run(): pl.pallas_call(kernel, grid_spec=pltpu.PrefetchScalarGridSpec(num_scalar_...  159 us
    all_gather x1, waiting for transfers between devices, body(): lax.all_gather(piece.reshape(-1, D), GATHER_AXES, axis=0, tiled=True)  78.8 us
    ppermute x9, waiting for transfers between devices, sum_all(): lax.ppermute(sent, axis, [(i, (i + gap) % 4) for i in range(4)]).astype(F32)  28.2 us
    ppermute x15, starting transfers between devices, send_ahead(): lax.ppermute(pieces[step], 'tp', [(i, (i + step) % TP) for i in range(TP)])  20.9 us
    ppermute x9, starting transfers between devices, sum_all(): lax.ppermute(sent, axis, [(i, (i + gap) % 4) for i in range(4)]).astype(F32)  16.1 us
    unnamed x170, local copies, waits for them, and re-layouts  14.2 us
    ppermute x15, waiting for transfers between devices, send_ahead(): lax.ppermute(pieces[step], 'tp', [(i, (i + step) % TP) for i in range(TP)])  14.1 us
    all_to_all x1, waiting for transfers between devices, body(): parts = lax.all_to_all(tiles, 'tp', split_axis=0, concat_axis=0, tiled=True)  12.2 us
  transfers between devices with their start and end apart: 58, of which 23 were waited for; matrix products, arithmetic and copies ran while one was open for 14% of the time, Pallas kernels for 30%

profile of v3, /device:TPU:1, one launch (start us, length us, event | category | flops | bytes accessed | tf_op | source)
XLA Modules:
  0.0 505.6 jit_solution(15408772774065901207)
XLA Ops:
  7.9 2.8 shard_map.511
  11.5 2.5 collective-permute-start
  14.0 3.3 collective-permute-start.1
  19.3 9.0 %all-to-all-start = ((bf16[25,32,4,128]{3,2,0,1:T(4,128)(2,1)}), bf16[25,32,4,128]{3,2,0,1:T(4,128)(2,1)}, u32[]{:S(2)}, u32[]{:S(2)}) async-start(bf16[25,32,4,128]{3,2,0,1:T(4,128)(2,1)} %copy.96), calls=%async_computation | async-start | bytes 1638400 | tf_op jit(solution)/shard_map/all_to_all | solution.py:1043
  31.2 2.5 reshape.576
  33.7 1.7 copy.94
  51.7 6.0 %fusion.16 = f32[2,32,10,190]{3,1,2,0:T(8,128)S(1)} fusion(f32[10,190,361,1]{2,1,0,3:T(8,128)} %constant.309, f32[2,8,361]{2,1,0:T(8,128)S(1)} %reshape.574, f32[2,8,361]{2,1,0:T(8,128)S(1)} %reshape.572, f32[2,8,361]{2,1,0:T(8,128)S(1)} %reshape.570, f32[2,8,361]{2,1,0:T(8,128)S(1)} %reshape.568), kind=kOutput, calls=%fused_computation.80 | convolution fusion | flops 526840512 | bytes 3322416 | tf_op jit(solution)/shard_map/dot_general | solution.py:936
  59.6 1.9 copy.93
  62.9 2.2 fusion.1
  65.0 1.6 reshape.579
  68.4 3.5 all-to-all-start.1
  72.6 12.2 %all-to-all-done.1.x_ref = bf16[4,200,512]{2,1,0:T(8,128)(2,1)S(1)} async-done(((bf16[4,200,512]{2,1,0:T(8,128)(2,1)}), bf16[4,200,512]{2,1,0:T(8,128)(2,1)S(1)}, u32[]{:S(2)}, u32[]{:S(2)}) %all-to-all-start.1) | async-done | bytes 819232 | tf_op jit(solution)/shard_map/all_to_all | solution.py:1045
  84.8 78.8 %all-gather.2.cloned.1.call-done = bf16[26624,1024]{1,0:T(8,128)(2,1)} async-done(((bf16[208,1024]{1,0:T(8,128)(2,1)}), bf16[26624,1024]{1,0:T(8,128)(2,1)}) %all-gather.2.cloned.1.call-update) | async-done | bytes 54525968 | tf_op jit(solution)/shard_map/all_gather | solution.py:1040
  163.6 7.4 %shard_map.512 = (f32[224,1024]{1,0:T(8,128)}, bf16[224,1024]{1,0:T(8,128)(2,1)}, bf16[224,1024]{1,0:T(8,128)(2,1)}) custom-call(s32[2]{0:T(128)} %get-tuple-element.479.core_ref.refs_0_, bf16[4,200,512]{2,1,0:T(8,128)(2,1)} %copy-done.1, bf16[200,224]{1,0:T(8,128)(2,1)} %constant.244.clone.pack_ref, f32[4,1,512]{2,1,0:T(1,128)} %reshape.584.gain_ref, ...), custom_call_target="tpu_custom_call" | custom-call | bytes 1024 | tf_op jit(solution)/shard_map/pallas_call | solution.py:117
  171.8 11.2 %shard_map.513 = (f32[224,1024]{1,0:T(8,128)}, bf16[224,1024]{1,0:T(8,128)(2,1)}, bf16[224,1024]{1,0:T(8,128)(2,1)}, bf16[224,1024]{1,0:T(8,128)(2,1)}, bf16[224...) custom-call(s32[2]{0:T(128)} %get-tuple-element.479.core_ref.refs_0_, ...), custom_call_target="tpu_custom_call" | custom-call | bytes 1024 | tf_op jit(solution)/shard_map/pallas_call | solution.py:117
  183.4 13.2 %shard_map.514 = (bf16[224,1024]{1,0:T(8,128)(2,1)}, bf16[224,4096]{1,0:T(8,128)(2,1)}, bf16[112,1024]{1,0:T(8,128)(2,1)}, bf16[224,2048]{1,0:T(8,128)(2,1)}, bf...) custom-call(s32[2]{0:T(128)} %get-tuple-element.479.core_ref.refs_0_, f32[224,1024]{1,0:T(8,128)} %get-tuple-element.170.mid_ref, ...), custom_call_target="tpu_custom_call" | custom-call | bytes 1024 | tf_op jit(solution)/shard_map/pallas_call | solution.py:117
  196.7 1.7 collective-permute-start.4
  198.9 5.0 collective-permute-done.4.refs_2_
  204.6 12.4 %shard_map.515 = (f32[224,1024]{1,0:T(8,128)}, bf16[224,1024]{1,0:T(8,128)(2,1)}, bf16[224,1024]{1,0:T(8,128)(2,1)}, bf16[224,1024]{1,0:T(8,128)(2,1)}, bf16[224...) custom-call(s32[2]{0:T(128)} %get-tuple-element.479.core_ref.refs_0_, ...), custom_call_target="tpu_custom_call" | custom-call | bytes 1024 | tf_op jit(solution)/shard_map/pallas_call | solution.py:117
  218.5 3.7 collective-permute-start.8
  223.0 20.7 %shard_map.516 = (bf16[224,1024]{1,0:T(8,128)(2,1)}, bf16[200,1024]{1,0:T(8,128)(2,1)}, bf16[224,1024]{1,0:T(8,128)(2,1)}, bf16[224,1024]{1,0:T(8,128)(2,1)}, bf...) custom-call(s32[2]{0:T(128)} %get-tuple-element.479.core_ref.refs_0_, ...), custom_call_target="tpu_custom_call" | custom-call | bytes 1024 | tf_op jit(solution)/shard_map/pallas_call | solution.py:117
  245.1 15.7 %shard_map.517 = (f32[224,1024]{1,0:T(8,128)}, bf16[224,1536]{1,0:T(8,128)(2,1)}, bf16[224,1536]{1,0:T(8,128)(2,1)}, f32[32,112,112]{2,1,0:T(8,128)}, f32[2,1024...) custom-call(s32[2]{0:T(128)} %get-tuple-element.479.core_ref.refs_0_, ...), custom_call_target="tpu_custom_call" | custom-call | bytes 1024 | tf_op jit(solution)/shard_map/pallas_call | solution.py:117
  261.6 2.2 collective-permute-done.14.refs_2_
  264.4 1.7 collective-permute-start.16
  266.9 11.1 %shard_map.518 = bf16[16,4,64,1024]{3,2,1,0:T(8,128)(2,1)} custom-call(s32[2]{0:T(128)} %get-tuple-element.479.core_ref.refs_0_, bf16[224,1024]{1,0:T(8,128)(2,1)} %get-tuple-element.197.refs_1_, bf16[224,1024]{1,0:T(8,128)(2,1)} %copy-done.31, bf16[224,2048]{1,0:T(8,128)(2,1)} %get-tuple-element.201.refs_3_, bf16[224,2048]{1,0:T(8,128)(2,1)} %copy-done.9, ...), custom_call_target="tpu_custom_call" | custom-call | bytes 1024 | tf_op jit(solution)/shard_map/pallas_call | solution.py:117
  279.8 2.1 collective-permute-start.19
  282.4 15.4 %shard_map.519 = (f32[224,1024]{1,0:T(8,128)}, bf16[224,1024]{1,0:T(8,128)(2,1)}, bf16[224,1024]{1,0:T(8,128)(2,1)}, f32[1,4096]{1,0:T(1,128)}, f32[4,1024]{1,0:...) custom-call(s32[2]{0:T(128)} %get-tuple-element.479.core_ref.refs_0_, ...), custom_call_target="tpu_custom_call" | custom-call | bytes 1024 | tf_op jit(solution)/shard_map/pallas_call | solution.py:117
  297.8 4.7 collective-permute-done.19.refs_6_
  303.9 3.1 collective-permute-start.22
  307.0 7.0 %shard_map.523 = (bf16[1024,512]{1,0:T(8,128)(2,1)}, bf16[1024,512]{1,0:T(8,128)(2,1)}) custom-call(s32[2]{0:T(128)} %get-tuple-element.479.core_ref.refs_0_, bf16[224,1024]{1,0:T(8,128)(2,1)} %get-tuple-element.252.dx_ref.refs_0_, bf16[224,1024]{1,0:T(8,128)(2,1)} %get-tuple-element.253.refs_1_, bf16[224,1024]{1,0:T(8,128)(2,1)} %get-tuple-element.254.refs_2_, ...), custom_call_target="tpu_custom_call" | custom-call | bytes 1024 | tf_op jit(solution)/shard_map/pallas_call | solution.py:117
  315.1 15.4 %shard_map.520 = (f32[224,1024]{1,0:T(8,128)}, bf16[224,1536]{1,0:T(8,128)(2,1)}, bf16[224,1536]{1,0:T(8,128)(2,1)}, f32[32,112,112]{2,1,0:T(8,128)}, f32[2,1024]{1,0:T(2,128)}, /*index=5*/f32[2,1024]{1,0:T(2,128)}) custom-call(s32[2]{0:T(128)} %get-tuple-element.479.core_ref.refs_0_, f32[224,1024]{1,0:T(8,128)} %get-tuple-element.214.refs_1_, ...), custom_call_target="tpu_custom_call" | custom-call | bytes 1024 | tf_op jit(solution)/shard_map/pallas_call | solution.py:117
  330.5 8.4 %shard_map.521 = (bf16[224,1024]{1,0:T(8,128)(2,1)}, bf16[4,200,512]{2,1,0:T(8,128)(2,1)}, f32[4,1,512]{2,1,0:T(1,128)}, f32[4,1,512]{2,1,0:T(1,128)}) custom-call(s32[2]{0:T(128)} %get-tuple-element.479.core_ref.refs_0_, bf16[4,200,512]{2,1,0:T(8,128)(2,1)} %copy-done.1, bf16[200,224]{1,0:T(8,128)(2,1)} %constant.244.clone.pack_ref, ...), custom_call_target="tpu_custom_call" | custom-call | bytes 1024 | tf_op jit(solution)/shard_map/pallas_call | solution.py:117
  340.0 6.8 %shard_map.522 = (bf16[1024,512]{1,0:T(8,128)(2,1)}, bf16[1024,512]{1,0:T(8,128)(2,1)}) custom-call(s32[2]{0:T(128)} %get-tuple-element.479.core_ref.refs_0_, bf16[224,1024]{1,0:T(8,128)(2,1)} %get-tuple-element.234.refs_0_, bf16[224,1024]{1,0:T(8,128)(2,1)} %copy-done.15, bf16[224,1024]{1,0:T(8,128)(2,1)} %copy-done.16, bf16[224,1024]{1,0:T(8,128)(2,1)} %copy-done.17, ...), custom_call_target="tpu_custom_call" | custom-call | bytes 1024 | tf_op jit(solution)/shard_map/pallas_call | solution.py:117
  348.0 2.1 collective-permute-done.25.refs_14_
  350.2 1.5 collective-permute-done.28.refs_6_
  353.8 14.8 %shard_map.524 = bf16[16,4,64,1536]{3,2,1,0:T(8,128)(2,1)} custom-call(s32[2]{0:T(128)} %get-tuple-element.479.core_ref.refs_0_, bf16[224,1024]{1,0:T(8,128)(2,1)} %get-tuple-element.167.refs_1_, bf16[224,1024]{1,0:T(8,128)(2,1)} %collective-permute-done.5.refs_2_, bf16[224,1536]{1,0:T(8,128)(2,1)} %get-tuple-element.233.refs_3_, ...), custom_call_target="tpu_custom_call" | custom-call | bytes 1024 | tf_op jit(solution)/shard_map/pallas_call | solution.py:117
  368.6 4.4 all-to-all-start.2
  375.5 2.6 convolution_convert_fusion
  378.2 2.3 fusion.31
  382.8 2.6 convolution_convert_fusion.1
  388.1 1.6 copy.102
  391.3 6.3 %all-to-all-start.3 = ((bf16[800,1,4,128]{3,2,1,0:T(4,128)(2,1)}), bf16[800,1,4,128]{3,2,1,0:T(4,128)(2,1)S(1)}, u32[]{:S(2)}, u32[]{:S(2)}) async-start(bf16[800,1,4,128]{3,2,1,0:T(4,128)(2,1)} %bitcast.75), calls=%async_computation.3 | async-start | bytes 1638400 | tf_op jit(solution)/shard_map/all_to_all | solution.py:1192
  397.6 3.0 collective-permute-start.34
  400.9 2.4 collective-permute-start.36
  403.3 19.7 %collective-permute-done.34 = bf16[64,1024]{1,0:T(8,128)(2,1)S(1)} collective-permute-done((bf16[64,1024]{1,0:T(8,128)(2,1)S(1)}, bf16[64,1024]{1,0:T(8,128)(2,1)S(1)}, u32[]{:S(2)}, u32[]{:S(2)}) %collective-permute-start.34) | collective-permute-done | bytes 131104 | tf_op jit(solution)/shard_map/ppermute | solution.py:999
  424.5 1.7 collective-permute-done.36
  426.2 2.7 collective-permute-start.37
  429.0 1.8 collective-permute-start.30
  430.8 1.7 collective-permute-start.31
  432.5 1.8 collective-permute-start.32
  435.5 1.8 collective-permute-start.39
  437.4 1.6 copy.107
  439.0 4.1 collective-permute-done.38
  443.2 3.3 collective-permute-start.40
  446.5 2.7 collective-permute-start.42
  449.5 1.5 collective-permute-done.32
  454.3 3.6 copy.106
  461.9 4.8 collective-permute-start.48
  468.3 4.3 collective-permute-done.48
  473.5 1.5 collective-permute-start.50
  476.1 4.1 reduce-scatter.7.cloned.1.call-done
  482.8 2.6 collective-permute-start.44
  487.7 4.5 collective-permute-done.44
  492.3 1.9 collective-permute-start.46
  (405 shorter events, 69.7 us)
Async XLA Ops:
  7.2 156.4 %all-gather.2.cloned.1.call-start = ((), (), s32[]{:S(2)}) async-start(), calls=%async_computation.6 | async-start | bytes 54951936 | tf_op jit(solution)/shard_map/all_gather | solution.py:1040
  10.6 18.3 %copy-start.5 = (bf16[1,20,40,1024]{3,2,1,0:T(8,128)(2,1)S(1)}, bf16[1,20,40,1024]{3,2,1,0:T(8,128)(2,1)}, u32[]{:S(2)}) copy-start(bf16[1,20,40,1024]{3,2,1,0:T(8,128)(2,1)} %param.58) | copy-start | bytes 4915204
  11.5 38.7 %collective-permute-start = (f32[80,128]{1,0:T(8,128)}, f32[80,128]{1,0:T(8,128)}, u32[]{:S(2)}, u32[]{:S(2)}) collective-permute-start(f32[80,128]{1,0:T(8,128)} %bitcast.10), channel_id=1, source_target_pairs={{0,1},{1,2},{2,3},{3,0},{4,5},{5,6},{6,7},{7,4},{8,9},{9,10},{10,1... | collective-permute-start | bytes 122888 | tf_op jit(solution)/shard_map/ppermute | solution.py:979
  14.0 36.2 %collective-permute-start.1 = (f32[80,128]{1,0:T(8,128)}, f32[80,128]{1,0:T(8,128)}, u32[]{:S(2)}, u32[]{:S(2)}) collective-permute-start(f32[80,128]{1,0:T(8,128)} %bitcast.10), channel_id=1, source_target_pairs={{0,2},{1,3},{2,0},{3,1},{4,6},{5,7},{6,4},{7,5},{8,10},{9,11},{10,... | collective-permute-start | bytes 122888 | tf_op jit(solution)/shard_map/ppermute | solution.py:979
  17.3 32.9 %collective-permute-start.2 = (f32[80,128]{1,0:T(8,128)}, f32[80,128]{1,0:T(8,128)}, u32[]{:S(2)}, u32[]{:S(2)}) collective-permute-start(f32[80,128]{1,0:T(8,128)} %bitcast.10), channel_id=1, source_target_pairs={{0,3},{1,0},{2,1},{3,2},{4,7},{5,4},{6,5},{7,6},{8,11},{9,8},{10,9... | collective-permute-start | bytes 122888 | tf_op jit(solution)/shard_map/ppermute | solution.py:979
  19.3 45.8 %all-to-all-start = ((bf16[25,32,4,128]{3,2,0,1:T(4,128)(2,1)}), bf16[25,32,4,128]{3,2,0,1:T(4,128)(2,1)}, u32[]{:S(2)}, u32[]{:S(2)}) async-start(bf16[25,32,4,128]{3,2,0,1:T(4,128)(2,1)} %copy.96), calls=%async_computation | async-start | bytes 1638400 | tf_op jit(solution)/shard_map/all_to_all | solution.py:1043
  68.4 16.4 %all-to-all-start.1 = ((bf16[4,200,512]{2,1,0:T(8,128)(2,1)}), bf16[4,200,512]{2,1,0:T(8,128)(2,1)S(1)}, u32[]{:S(2)}, u32[]{:S(2)}) async-start(bf16[4,200,512]{2,1,0:T(8,128)(2,1)} %copy.98), calls=%async_computation.1 | async-start | bytes 1638400 | tf_op jit(solution)/shard_map/all_to_all | solution.py:1045
  71.9 388.5 %reduce-scatter.9.cloned.1.call-start = ((), (), s32[]{:S(2)}) async-start(), calls=%async_computation.8 | async-start | bytes 8912896
  84.8 78.8 %copy-start.1 = (bf16[4,200,512]{2,1,0:T(8,128)(2,1)}, bf16[4,200,512]{2,1,0:T(8,128)(2,1)S(1)}, u32[]{:S(2)}) copy-start(bf16[4,200,512]{2,1,0:T(8,128)(2,1)S(1)} %all-to-all-done.1.x_ref) | copy-start | bytes 2457604
  170.9 12.5 %collective-permute-start.3 = (bf16[224,1024]{1,0:T(8,128)(2,1)}, bf16[224,1024]{1,0:T(8,128)(2,1)S(1)}, u32[]{:S(2)}, u32[]{:S(2)}) collective-permute-start(bf16[224,1024]{1,0:T(8,128)(2,1)} %get-tuple-element.169), channel_id=1, source_target_pairs={{0,4},{4,0},{1,5},{5,1},{2,6},{6,2},{3,7},{7,3},{8,12},{12,8},{9,1... | collective-permute-start | bytes 1376264 | tf_op jit(solution)/shard_map/ppermute | solution.py:990
  183.1 39.1 %collective-permute-start.5 = (bf16[224,1024]{1,0:T(8,128)(2,1)}, bf16[224,1024]{1,0:T(8,128)(2,1)}, u32[]{:S(2)}, u32[]{:S(2)}) collective-permute-start(bf16[224,1024]{1,0:T(8,128)(2,1)} %get-tuple-element.167.refs_1_), channel_id=1, source_target_pairs={{0,4},{4,0},{1,5},{5,1},{2,6},{6,2},{3,7},{7,3},{8,12},{12,8},{9,1... | collective-permute-start | bytes 1376264 | tf_op jit(solution)/shard_map/ppermute | solution.py:990
  196.7 7.2 %collective-permute-start.4 = (bf16[112,1024]{1,0:T(8,128)(2,1)}, bf16[112,1024]{1,0:T(8,128)(2,1)S(1)}, u32[]{:S(2)}, u32[]{:S(2)}) collective-permute-start(bf16[112,1024]{1,0:T(8,128)(2,1)} %get-tuple-element.172), channel_id=1, source_target_pairs={{1,0},{2,1},{3,2},{0,3},{5,4},{6,5},{7,6},{4,7},{9,8},{10,9},{11,1... | collective-permute-start | bytes 688136 | tf_op jit(solution)/shard_map/ppermute | solution.py:1128
  198.4 20.2 %collective-permute-start.6 = (bf16[224,512]{1,0:T(8,128)(2,1)S(1)}, bf16[224,512]{1,0:T(8,128)(2,1)}, u32[]{:S(2)}, u32[]{:S(2)}) collective-permute-start(bf16[224,512]{1,0:T(8,128)(2,1)S(1)} %copy-done.68), channel_id=1, source_target_pairs={{0,4},{4,0},{1,5},{5,1},{2,6},{6,2},{3,7},{7,3},{8,12},{12,8},{9,1... | collective-permute-start | bytes 688136 | tf_op jit(solution)/shard_map/ppermute | solution.py:990
  204.6 17.6 %copy-start.56 = (f32[224]{0:T(256)S(1)}, f32[224]{0:T(256)}, u32[]{:S(2)}) copy-start(f32[224]{0:T(256)} %and_convert_fusion) | copy-start | bytes 2692
  217.0 26.8 %collective-permute-start.11 = (bf16[224,512]{1,0:T(8,128)(2,1)}, bf16[224,512]{1,0:T(8,128)(2,1)S(1)}, u32[]{:S(2)}, u32[]{:S(2)}) collective-permute-start(bf16[224,512]{1,0:T(8,128)(2,1)} %get-tuple-element.187), channel_id=1, source_target_pairs={{0,4},{4,0},{1,5},{5,1},{2,6},{6,2},{3,7},{7,3},{8,12},{12,8},{9,1... | collective-permute-start | bytes 688136 | tf_op jit(solution)/shard_map/ppermute | solution.py:990
  218.1 26.9 %collective-permute-start.10 = (bf16[224,1024]{1,0:T(8,128)(2,1)}, bf16[224,1024]{1,0:T(8,128)(2,1)S(1)}, u32[]{:S(2)}, u32[]{:S(2)}) collective-permute-start(bf16[224,1024]{1,0:T(8,128)(2,1)} %get-tuple-element.186.refs_5_), channel_id=1, source_target_pairs={{0,4},{4,0},{1,5},{5,1},{2,6},{6,2},{3,7},{7,3},{8,12},{12,8},{9,1... | collective-permute-start | bytes 1376264 | tf_op jit(solution)/shard_map/ppermute | solution.py:990
  218.2 26.8 %collective-permute-start.7 = (bf16[224,1024]{1,0:T(8,128)(2,1)S(1)}, bf16[224,1024]{1,0:T(8,128)(2,1)S(1)}, u32[]{:S(2)}, u32[]{:S(2)}) collective-permute-start(bf16[224,1024]{1,0:T(8,128)(2,1)S(1)} %copy-done.14), channel_id=1, source_target_pairs={{0,1},{1,2},{2,3},{3,0},{4,5},{5,6},{6,7},{7,4},{8,9},{9,10},{10,1... | collective-permute-start | bytes 1376264 | tf_op jit(solution)/shard_map/ppermute | solution.py:905
  218.5 26.5 %collective-permute-start.8 = (bf16[224,1024]{1,0:T(8,128)(2,1)S(1)}, bf16[224,1024]{1,0:T(8,128)(2,1)S(1)}, u32[]{:S(2)}, u32[]{:S(2)}) collective-permute-start(bf16[224,1024]{1,0:T(8,128)(2,1)S(1)} %copy-done.14), channel_id=1, source_target_pairs={{0,2},{1,3},{2,0},{3,1},{4,6},{5,7},{6,4},{7,5},{8,10},{9,11},{10,... | collective-permute-start | bytes 1376264 | tf_op jit(solution)/shard_map/ppermute | solution.py:905
  222.2 22.8 %collective-permute-start.9 = (bf16[224,1024]{1,0:T(8,128)(2,1)S(1)}, bf16[224,1024]{1,0:T(8,128)(2,1)S(1)}, u32[]{:S(2)}, u32[]{:S(2)}) collective-permute-start(bf16[224,1024]{1,0:T(8,128)(2,1)S(1)} %copy-done.14), channel_id=1, source_target_pairs={{0,3},{1,0},{2,1},{3,2},{4,7},{5,4},{6,5},{7,6},{8,11},{9,8},{10,9... | collective-permute-start | bytes 1376264 | tf_op jit(solution)/shard_map/ppermute | solution.py:905
  243.8 17.0 %copy-start.35 = (bf16[224,512]{1,0:T(8,128)(2,1)}, bf16[224,512]{1,0:T(8,128)(2,1)S(1)}, u32[]{:S(2)}) copy-start(bf16[224,512]{1,0:T(8,128)(2,1)S(1)} %collective-permute-done.11.refs_12_) | copy-start | bytes 688132
  243.8 20.6 %collective-permute-start.12 = (bf16[224,2048]{1,0:T(8,128)(2,1)}, bf16[224,2048]{1,0:T(8,128)(2,1)S(1)}, u32[]{:S(2)}, u32[]{:S(2)}) collective-permute-start(bf16[224,2048]{1,0:T(8,128)(2,1)} %get-tuple-element.199), channel_id=1, source_target_pairs={{0,4},{4,0},{1,5},{5,1},{2,6},{6,2},{3,7},{7,3},{8,12},{12,8},{9,1... | collective-permute-start | bytes 2752520 | tf_op jit(solution)/shard_map/ppermute | solution.py:990
  260.9 5.2 %collective-permute-start.15 = (bf16[224,1536]{1,0:T(8,128)(2,1)}, bf16[224,1536]{1,0:T(8,128)(2,1)S(1)}, u32[]{:S(2)}, u32[]{:S(2)}) collective-permute-start(bf16[224,1536]{1,0:T(8,128)(2,1)} %get-tuple-element.205), channel_id=1, source_target_pairs={{0,4},{4,0},{1,5},{5,1},{2,6},{6,2},{3,7},{7,3},{8,12},{12,8},{9,1... | collective-permute-start | bytes 2064392 | tf_op jit(solution)/shard_map/ppermute | solution.py:990
  261.0 2.8 collective-permute-start.14
  261.5 2.9 collective-permute-start.13
  264.4 13.6 %collective-permute-start.16 = (bf16[112,1024]{1,0:T(8,128)(2,1)}, bf16[112,1024]{1,0:T(8,128)(2,1)S(1)}, u32[]{:S(2)}, u32[]{:S(2)}) collective-permute-start(bf16[112,1024]{1,0:T(8,128)(2,1)} %get-tuple-element.209), channel_id=1, source_target_pairs={{0,1},{1,2},{2,3},{3,0},{4,5},{5,6},{6,7},{7,4},{8,9},{9,10},{10,1... | collective-permute-start | bytes 688136 | tf_op jit(solution)/shard_map/ppermute | solution.py:1138
  278.7 201.5 %reduce-scatter.7.cloned.1.call-start = ((), (), s32[]{:S(2)}) async-start(), calls=%async_computation.7 | async-start | bytes 13369344
  279.3 23.8 %collective-permute-start.17 = (bf16[224,2048]{1,0:T(8,128)(2,1)S(1)}, bf16[224,2048]{1,0:T(8,128)(2,1)S(1)}, u32[]{:S(2)}, u32[]{:S(2)}) collective-permute-start(bf16[224,2048]{1,0:T(8,128)(2,1)S(1)} %copy-done.64), channel_id=1, source_target_pairs={{0,4},{4,0},{1,5},{5,1},{2,6},{6,2},{3,7},{7,3},{8,12},{12,8},{9,1... | collective-permute-start | bytes 2752520 | tf_op jit(solution)/shard_map/ppermute | solution.py:990
  279.6 18.1 %collective-permute-start.18 = (bf16[224,1024]{1,0:T(8,128)(2,1)}, bf16[224,1024]{1,0:T(8,128)(2,1)S(1)}, u32[]{:S(2)}, u32[]{:S(2)}) collective-permute-start(bf16[224,1024]{1,0:T(8,128)(2,1)} %get-tuple-element.222), channel_id=1, source_target_pairs={{0,1},{1,2},{2,3},{3,0},{4,5},{5,6},{6,7},{7,4},{8,9},{9,10},{10,1... | collective-permute-start | bytes 1376264 | tf_op jit(solution)/shard_map/ppermute | solution.py:905
  279.8 22.7 %collective-permute-start.19 = (bf16[224,1024]{1,0:T(8,128)(2,1)S(1)}, bf16[224,1024]{1,0:T(8,128)(2,1)S(1)}, u32[]{:S(2)}, u32[]{:S(2)}) collective-permute-start(bf16[224,1024]{1,0:T(8,128)(2,1)S(1)} %copy-done.67), channel_id=1, source_target_pairs={{0,2},{1,3},{2,0},{3,1},{4,6},{5,7},{6,4},{7,5},{8,10},{9,11},{10,... | collective-permute-start | bytes 1376264 | tf_op jit(solution)/shard_map/ppermute | solution.py:905
  281.9 21.1 %collective-permute-start.20 = (bf16[224,1024]{1,0:T(8,128)(2,1)S(1)}, bf16[224,1024]{1,0:T(8,128)(2,1)S(1)}, u32[]{:S(2)}, u32[]{:S(2)}) collective-permute-start(bf16[224,1024]{1,0:T(8,128)(2,1)S(1)} %copy-done.66), channel_id=1, source_target_pairs={{0,3},{1,0},{2,1},{3,2},{4,7},{5,4},{6,5},{7,6},{8,11},{9,8},{10,9... | collective-permute-start | bytes 1376264 | tf_op jit(solution)/shard_map/ppermute | solution.py:905
  303.0 27.4 %copy-start.8 = (bf16[224,2048]{1,0:T(8,128)(2,1)}, bf16[224,2048]{1,0:T(8,128)(2,1)S(1)}, u32[]{:S(2)}) copy-start(bf16[224,2048]{1,0:T(8,128)(2,1)S(1)} %collective-permute-done.17.refs_16_) | copy-start | bytes 2752516
  303.0 35.8 %collective-permute-start.21 = (bf16[224,1024]{1,0:T(8,128)(2,1)}, bf16[224,1024]{1,0:T(8,128)(2,1)S(1)}, u32[]{:S(2)}, u32[]{:S(2)}) collective-permute-start(bf16[224,1024]{1,0:T(8,128)(2,1)} %get-tuple-element.242), channel_id=1, source_target_pairs={{0,1},{1,2},{2,3},{3,0},{4,5},{5,6},{6,7},{7,4},{8,9},{9,10},{10,1... | collective-permute-start | bytes 1376264 | tf_op jit(solution)/shard_map/ppermute | solution.py:905
  303.9 35.0 %collective-permute-start.22 = (bf16[224,1024]{1,0:T(8,128)(2,1)}, bf16[224,1024]{1,0:T(8,128)(2,1)S(1)}, u32[]{:S(2)}, u32[]{:S(2)}) collective-permute-start(bf16[224,1024]{1,0:T(8,128)(2,1)} %get-tuple-element.243), channel_id=1, source_target_pairs={{0,2},{1,3},{2,0},{3,1},{4,6},{5,7},{6,4},{7,5},{8,10},{9,11},{10,... | collective-permute-start | bytes 1376264 | tf_op jit(solution)/shard_map/ppermute | solution.py:905
  307.0 31.9 %collective-permute-start.23 = (bf16[224,1024]{1,0:T(8,128)(2,1)}, bf16[224,1024]{1,0:T(8,128)(2,1)S(1)}, u32[]{:S(2)}, u32[]{:S(2)}) collective-permute-start(bf16[224,1024]{1,0:T(8,128)(2,1)} %get-tuple-element.244), channel_id=1, source_target_pairs={{0,3},{1,0},{2,1},{3,2},{4,7},{5,4},{6,5},{7,6},{8,11},{9,8},{10,9... | collective-permute-start | bytes 1376264 | tf_op jit(solution)/shard_map/ppermute | solution.py:905
  314.0 38.4 %collective-permute-start.26 = (bf16[1024,512]{1,0:T(8,128)(2,1)}, bf16[1024,512]{1,0:T(8,128)(2,1)S(1)}, u32[]{:S(2)}, u32[]{:S(2)}) collective-permute-start(bf16[1024,512]{1,0:T(8,128)(2,1)} %get-tuple-element.260), channel_id=1, source_target_pairs={{0,4},{4,0},{1,5},{5,1},{2,6},{6,2},{3,7},{7,3},{8,12},{12,8},{9,1... | collective-permute-start | bytes 3145736 | tf_op jit(solution)/shard_map/ppermute | solution.py:990
  346.7 5.6 %collective-permute-start.29 = (bf16[1024,512]{1,0:T(8,128)(2,1)}, bf16[1024,512]{1,0:T(8,128)(2,1)S(1)}, u32[]{:S(2)}, u32[]{:S(2)}) collective-permute-start(bf16[1024,512]{1,0:T(8,128)(2,1)} %get-tuple-element.274), channel_id=1, source_target_pairs={{0,4},{4,0},{1,5},{5,1},{2,6},{6,2},{3,7},{7,3},{8,12},{12,8},{9,1... | collective-permute-start | bytes 3145736 | tf_op jit(solution)/shard_map/ppermute | solution.py:990
  346.8 3.3 collective-permute-start.25
  347.3 4.4 collective-permute-start.27
  347.4 4.3 collective-permute-start.28
  350.1 2.3 collective-permute-start.24
  368.6 19.5 %all-to-all-start.2 = ((bf16[4,200,512]{2,1,0:T(8,128)(2,1)}), bf16[4,200,512]{2,1,0:T(8,128)(2,1)}, u32[]{:S(2)}, u32[]{:S(2)}) async-start(bf16[4,200,512]{2,1,0:T(8,128)(2,1)} %get-tuple-element.291), calls=%async_computation.2 | async-start | bytes 1638400 | tf_op jit(solution)/shard_map/all_to_all | solution.py:1188
  387.6 10.0 %collective-permute-start.33 = (bf16[64,1024]{1,0:T(8,128)(2,1)S(1)}, bf16[64,1024]{1,0:T(8,128)(2,1)S(1)}, u32[]{:S(2)}, u32[]{:S(2)}) collective-permute-start(bf16[64,1024]{1,0:T(8,128)(2,1)S(1)} %convert_element_type.193), channel_id=1, source_target_pairs={{0,4},{4,0},{1,5},{5,1},{2,6},{6,2},{3,7},{7,3},{8,12},{12,8},{9,1... | collective-permute-start | bytes 393224 | tf_op jit(solution)/shard_map/ppermute | solution.py:990
  390.0 39.0 %copy-start.33 = (bf16[200,1024]{1,0:T(8,128)(2,1)S(1)}, bf16[200,1024]{1,0:T(8,128)(2,1)}, u32[]{:S(2)}) copy-start(bf16[200,1024]{1,0:T(8,128)(2,1)} %get-tuple-element.290) | copy-start | bytes 1228804
  391.3 46.0 %all-to-all-start.3 = ((bf16[800,1,4,128]{3,2,1,0:T(4,128)(2,1)}), bf16[800,1,4,128]{3,2,1,0:T(4,128)(2,1)S(1)}, u32[]{:S(2)}, u32[]{:S(2)}) async-start(bf16[800,1,4,128]{3,2,1,0:T(4,128)(2,1)} %bitcast.75), calls=%async_computation.3 | async-start | bytes 1638400 | tf_op jit(solution)/shard_map/all_to_all | solution.py:1192
  397.6 25.3 %collective-permute-start.34 = (bf16[64,1024]{1,0:T(8,128)(2,1)S(1)}, bf16[64,1024]{1,0:T(8,128)(2,1)S(1)}, u32[]{:S(2)}, u32[]{:S(2)}) collective-permute-start(bf16[64,1024]{1,0:T(8,128)(2,1)S(1)} %add_convert_fusion.2), channel_id=1, source_target_pairs={{0,16},{8,24},{16,0},{24,8},{1,17},{9,25},{17,1},{25,9},{2,18},{10... | collective-permute-start | bytes 393224 | tf_op jit(solution)/shard_map/ppermute | solution.py:999
  400.6 23.9 %collective-permute-start.35 = (bf16[64,1024]{1,0:T(8,128)(2,1)S(1)}, bf16[64,1024]{1,0:T(8,128)(2,1)S(1)}, u32[]{:S(2)}, u32[]{:S(2)}) collective-permute-start(bf16[64,1024]{1,0:T(8,128)(2,1)S(1)} %add_convert_fusion.2), channel_id=1, source_target_pairs={{0,8},{8,16},{16,24},{24,0},{1,9},{9,17},{17,25},{25,1},{2,10},{10... | collective-permute-start | bytes 393224 | tf_op jit(solution)/shard_map/ppermute | solution.py:999
  400.9 25.3 %collective-permute-start.36 = (bf16[64,1024]{1,0:T(8,128)(2,1)S(1)}, bf16[64,1024]{1,0:T(8,128)(2,1)S(1)}, u32[]{:S(2)}, u32[]{:S(2)}) collective-permute-start(bf16[64,1024]{1,0:T(8,128)(2,1)S(1)} %add_convert_fusion.2), channel_id=1, source_target_pairs={{0,24},{8,0},{16,8},{24,16},{1,25},{9,1},{17,9},{25,17},{2,26},{10... | collective-permute-start | bytes 393224 | tf_op jit(solution)/shard_map/ppermute | solution.py:999
  426.2 9.3 %collective-permute-start.37 = (bf16[64,1024]{1,0:T(8,128)(2,1)S(1)}, bf16[64,1024]{1,0:T(8,128)(2,1)S(1)}, u32[]{:S(2)}, u32[]{:S(2)}) collective-permute-start(bf16[64,1024]{1,0:T(8,128)(2,1)S(1)} %add_convert_fusion.1), channel_id=1, source_target_pairs={{0,64},{32,96},{64,0},{96,32},{1,65},{33,97},{65,1},{97,33},{2,66}... | collective-permute-start | bytes 393224 | tf_op jit(solution)/shard_map/ppermute | solution.py:999
  429.0 17.5 %collective-permute-start.30 = (bf16[200,1024]{1,0:T(8,128)(2,1)S(1)}, bf16[200,1024]{1,0:T(8,128)(2,1)S(1)}, u32[]{:S(2)}, u32[]{:S(2)}) collective-permute-start(bf16[200,1024]{1,0:T(8,128)(2,1)S(1)} %copy-done.33), channel_id=1, source_target_pairs={{0,1},{1,2},{2,3},{3,0},{4,5},{5,6},{6,7},{7,4},{8,9},{9,10},{10,1... | collective-permute-start | bytes 1228808 | tf_op jit(solution)/shard_map/ppermute | solution.py:979
  430.8 18.7 %collective-permute-start.31 = (bf16[200,1024]{1,0:T(8,128)(2,1)S(1)}, bf16[200,1024]{1,0:T(8,128)(2,1)S(1)}, u32[]{:S(2)}, u32[]{:S(2)}) collective-permute-start(bf16[200,1024]{1,0:T(8,128)(2,1)S(1)} %copy-done.33), channel_id=1, source_target_pairs={{0,2},{1,3},{2,0},{3,1},{4,6},{5,7},{6,4},{7,5},{8,10},{9,11},{10,... | collective-permute-start | bytes 1228808 | tf_op jit(solution)/shard_map/ppermute | solution.py:979
  432.5 18.6 %collective-permute-start.32 = (bf16[200,1024]{1,0:T(8,128)(2,1)S(1)}, bf16[200,1024]{1,0:T(8,128)(2,1)S(1)}, u32[]{:S(2)}, u32[]{:S(2)}) collective-permute-start(bf16[200,1024]{1,0:T(8,128)(2,1)S(1)} %copy-done.33), channel_id=1, source_target_pairs={{0,3},{1,0},{2,1},{3,2},{4,7},{5,4},{6,5},{7,6},{8,11},{9,8},{10,9... | collective-permute-start | bytes 1228808 | tf_op jit(solution)/shard_map/ppermute | solution.py:979
  434.3 8.8 %collective-permute-start.38 = (bf16[64,1024]{1,0:T(8,128)(2,1)S(1)}, bf16[64,1024]{1,0:T(8,128)(2,1)S(1)}, u32[]{:S(2)}, u32[]{:S(2)}) collective-permute-start(bf16[64,1024]{1,0:T(8,128)(2,1)S(1)} %add_convert_fusion.1), channel_id=1, source_target_pairs={{0,32},{32,64},{64,96},{96,0},{1,33},{33,65},{65,97},{97,1},{2,34}... | collective-permute-start | bytes 393224 | tf_op jit(solution)/shard_map/ppermute | solution.py:999
  435.5 7.6 %collective-permute-start.39 = (bf16[64,1024]{1,0:T(8,128)(2,1)S(1)}, bf16[64,1024]{1,0:T(8,128)(2,1)S(1)}, u32[]{:S(2)}, u32[]{:S(2)}) collective-permute-start(bf16[64,1024]{1,0:T(8,128)(2,1)S(1)} %add_convert_fusion.1), channel_id=1, source_target_pairs={{0,96},{32,0},{64,32},{96,64},{1,97},{33,1},{65,33},{97,65},{2,98}... | collective-permute-start | bytes 393224 | tf_op jit(solution)/shard_map/ppermute | solution.py:999
  443.2 14.7 %collective-permute-start.40 = (bf16[64,1024]{1,0:T(8,128)(2,1)S(1)}, bf16[64,1024]{1,0:T(8,128)(2,1)S(1)}, u32[]{:S(2)}, u32[]{:S(2)}) collective-permute-start(bf16[64,1024]{1,0:T(8,128)(2,1)S(1)} %add_convert_fusion), channel_id=1, source_target_pairs={{0,2},{1,3},{2,0},{3,1},{4,6},{5,7},{6,4},{7,5},{8,10},{9,11},{10,... | collective-permute-start | bytes 393224 | tf_op jit(solution)/shard_map/ppermute | solution.py:999
  446.5 11.4 %collective-permute-start.41 = (bf16[64,1024]{1,0:T(8,128)(2,1)S(1)}, bf16[64,1024]{1,0:T(8,128)(2,1)S(1)}, u32[]{:S(2)}, u32[]{:S(2)}) collective-permute-start(bf16[64,1024]{1,0:T(8,128)(2,1)S(1)} %add_convert_fusion), channel_id=1, source_target_pairs={{0,1},{1,2},{2,3},{3,0},{4,5},{5,6},{6,7},{7,4},{8,9},{9,10},{10,1... | collective-permute-start | bytes 393224 | tf_op jit(solution)/shard_map/ppermute | solution.py:999
  446.5 11.4 %collective-permute-start.42 = (bf16[64,1024]{1,0:T(8,128)(2,1)S(1)}, bf16[64,1024]{1,0:T(8,128)(2,1)S(1)}, u32[]{:S(2)}, u32[]{:S(2)}) collective-permute-start(bf16[64,1024]{1,0:T(8,128)(2,1)S(1)} %add_convert_fusion), channel_id=1, source_target_pairs={{0,3},{1,0},{2,1},{3,2},{4,7},{5,4},{6,5},{7,6},{8,11},{9,8},{10,9... | collective-permute-start | bytes 393224 | tf_op jit(solution)/shard_map/ppermute | solution.py:999
  461.5 6.8 %collective-permute-start.47 = (bf16[64,1024]{1,0:T(8,128)(2,1)S(1)}, bf16[64,1024]{1,0:T(8,128)(2,1)S(1)}, u32[]{:S(2)}, u32[]{:S(2)}) collective-permute-start(bf16[64,1024]{1,0:T(8,128)(2,1)S(1)} %get-tuple-element.397), channel_id=1, source_target_pairs={{0,1},{1,2},{2,3},{3,0},{4,5},{5,6},{6,7},{7,4},{8,9},{9,10},{10,1... | collective-permute-start | bytes 393224 | tf_op jit(solution)/shard_map/ppermute | solution.py:905
  461.9 10.6 %collective-permute-start.48 = (bf16[64,1024]{1,0:T(8,128)(2,1)S(1)}, bf16[64,1024]{1,0:T(8,128)(2,1)S(1)}, u32[]{:S(2)}, u32[]{:S(2)}) collective-permute-start(bf16[64,1024]{1,0:T(8,128)(2,1)S(1)} %get-tuple-element.399), channel_id=1, source_target_pairs={{0,2},{1,3},{2,0},{3,1},{4,6},{5,7},{6,4},{7,5},{8,10},{9,11},{10,... | collective-permute-start | bytes 393224 | tf_op jit(solution)/shard_map/ppermute | solution.py:905
  466.7 5.9 %collective-permute-start.49 = (bf16[64,1024]{1,0:T(8,128)(2,1)S(1)}, bf16[64,1024]{1,0:T(8,128)(2,1)S(1)}, u32[]{:S(2)}, u32[]{:S(2)}) collective-permute-start(bf16[64,1024]{1,0:T(8,128)(2,1)S(1)} %get-tuple-element.398), channel_id=1, source_target_pairs={{0,3},{1,0},{2,1},{3,2},{4,7},{5,4},{6,5},{7,6},{8,11},{9,8},{10,9... | collective-permute-start | bytes 393224 | tf_op jit(solution)/shard_map/ppermute | solution.py:905
  473.5 2.5 collective-permute-start.50
  481.4 6.3 %collective-permute-start.43 = (bf16[64,1280]{1,0:T(8,128)(2,1)S(1)}, bf16[64,1280]{1,0:T(8,128)(2,1)S(1)}, u32[]{:S(2)}, u32[]{:S(2)}) collective-permute-start(bf16[64,1280]{1,0:T(8,128)(2,1)S(1)} %get-tuple-element.394), channel_id=1, source_target_pairs={{0,1},{1,2},{2,3},{3,0},{4,5},{5,6},{6,7},{7,4},{8,9},{9,10},{10,1... | collective-permute-start | bytes 491528 | tf_op jit(solution)/shard_map/ppermute | solution.py:905
  482.8 9.4 %collective-permute-start.44 = (bf16[64,1280]{1,0:T(8,128)(2,1)S(1)}, bf16[64,1280]{1,0:T(8,128)(2,1)S(1)}, u32[]{:S(2)}, u32[]{:S(2)}) collective-permute-start(bf16[64,1280]{1,0:T(8,128)(2,1)S(1)} %get-tuple-element.396), channel_id=1, source_target_pairs={{0,2},{1,3},{2,0},{3,1},{4,6},{5,7},{6,4},{7,5},{8,10},{9,11},{10,... | collective-permute-start | bytes 491528 | tf_op jit(solution)/shard_map/ppermute | solution.py:905
  485.3 6.9 %collective-permute-start.45 = (bf16[64,1280]{1,0:T(8,128)(2,1)S(1)}, bf16[64,1280]{1,0:T(8,128)(2,1)S(1)}, u32[]{:S(2)}, u32[]{:S(2)}) collective-permute-start(bf16[64,1280]{1,0:T(8,128)(2,1)S(1)} %get-tuple-element.395), channel_id=1, source_target_pairs={{0,3},{1,0},{2,1},{3,2},{4,7},{5,4},{6,5},{7,6},{8,11},{9,8},{10,9... | collective-permute-start | bytes 491528 | tf_op jit(solution)/shard_map/ppermute | solution.py:905
  492.3 2.9 collective-permute-start.46
  (63 other events, 310.7 us)
Sparse Core Ops, SparseCore 0:
  11.0 152.5 all-gather.1
  278.2 81.6 reduce-scatter.8
  368.8 111.3 reduce-scatter.6
